TPU v7x, 32 devices: a whole 2x2x4 slice. The times are simulated.
32 devices in a mesh: dp: 8 (over y, x, core), seq: 4 (over z).
Axes of the slice: x: 2, y: 2, z: 4, core: 2. Of those that a mesh axis runs over, the one named last changes fastest.
Arguments:
- hidden_in: bfloat16 [8, 1024, 1536], P('dp', 'seq'), may hold values from -6 to 6
- out_grad: bfloat16 [8, 1024, 1536], P('dp', 'seq'), may hold values from -6 to 6
- prenorm: float32 [1536], P('dp'), may hold values from 0.5 to 1.5
- inproject: float32 [1536, 6448], P('dp'), may hold values from -0.15625 to 0.15625
- convtaps: float32 [5, 3328], P(None, 'dp'), may hold values from -0.5 to 0.5
- headcoefs: float32 [3, 48], replicated, may hold values from -12 to 3, as said below
- postnorm: float32 [3072], P('dp'), may hold values from 0.5 to 1.5
- outproject: float32 [3072, 1536], P('dp'), may hold values from -0.109375 to 0.109375
- prenorm_first: float32 [1536], P('dp'), may hold values from -56 to 56
- inproject_first: float32 [1536, 6448], P('dp'), may hold values from -56 to 56
- convtaps_first: float32 [5, 3328], P(None, 'dp'), may hold values from -56 to 56
- headcoefs_first: float32 [3, 48], replicated, may hold values from -56 to 56
- postnorm_first: float32 [3072], P('dp'), may hold values from -56 to 56
- outproject_first: float32 [3072, 1536], P('dp'), may hold values from -56 to 56
- prenorm_second: float32 [1536], P('dp'), may hold values from 16.384 to 163.84
- inproject_second: float32 [1536, 6448], P('dp'), may hold values from 16.384 to 163.84
- convtaps_second: float32 [5, 3328], P(None, 'dp'), may hold values from 16.384 to 163.84
- headcoefs_second: float32 [3, 48], replicated, may hold values from 16.384 to 163.84
- postnorm_second: float32 [3072], P('dp'), may hold values from 16.384 to 163.84
- outproject_second: float32 [3072, 1536], P('dp'), may hold values from 16.384 to 163.84
Outputs:
- output: float32 [8, 1024, 1536], P('dp', 'seq')
- input_gradient: float32 [8, 1024, 1536], P('dp', 'seq')
- prenorm_gradient: float32 [1536], P('dp')
- inproject_gradient: float32 [1536, 6448], P('dp')
- convtaps_gradient: float32 [5, 3328], P(None, 'dp')
- headcoefs_gradient: float32 [3, 48], replicated
- postnorm_gradient: float32 [3072], P('dp')
- outproject_gradient: float32 [3072, 1536], P('dp')
- prenorm_updated: float32 [1536], P('dp')
- inproject_updated: float32 [1536, 6448], P('dp')
- convtaps_updated: float32 [5, 3328], P(None, 'dp')
- headcoefs_updated: float32 [3, 48], replicated
- postnorm_updated: float32 [3072], P('dp')
- outproject_updated: float32 [3072, 1536], P('dp')
- prenorm_moment: float32 [1536], P('dp')
- inproject_moment: float32 [1536, 6448], P('dp')
- convtaps_moment: float32 [5, 3328], P(None, 'dp')
- headcoefs_moment: float32 [3, 48], replicated
- postnorm_moment: float32 [3072], P('dp')
- outproject_moment: float32 [3072, 1536], P('dp')
- prenorm_square: float32 [1536], P('dp')
- inproject_square: float32 [1536, 6448], P('dp')
- convtaps_square: float32 [5, 3328], P(None, 'dp')
- headcoefs_square: float32 [3, 48], replicated
- postnorm_square: float32 [3072], P('dp')
- outproject_square: float32 [3072, 1536], P('dp')
Inputs may be any that keep to these rules, and one draw needn't show every extreme that they name: `headcoefs`: row 0 holds step biases, row 1 logarithms of decay rates, row 2 skip weights.
All inputs are finite; a program needn't handle non-finite values.
Results may differ from a plain program's by a relative error of at most 0.00155.
The roundings to bfloat16 on the way count: a program that leaves them out, or rounds other values in their place, can miss the bound.
Values may be sent and summed in bfloat16 or wider, within the bound.
A program may use at most 320 MiB of HBM per device.

v0:
```python
import jax
import jax.numpy as jnp
from jax import lax
from jax.sharding import PartitionSpec as P

H = 48
N = 128
SPAN = 256
DI = 3072


norm_eps = 1e-05
highest = lax.Precision.HIGHEST
beta_moment = 0.9
beta_square = 0.95
adam_eps = 1e-08
adam_step = 3.0
rate_matrix = 0.005
rate_vector = 0.05
weight_decay = 0.1


def causal_conv(signal, conv_taps):
    tap_count = conv_taps.shape[0] - 1
    length = signal.shape[0]
    padded = jnp.pad(signal, ((tap_count - 1, 0), (0, 0)))
    summed = jnp.broadcast_to(conv_taps[tap_count][None, :], signal.shape)
    for offset in range(tap_count):
        summed = summed + conv_taps[offset][None, :] * padded[offset : offset + length]
    return jax.nn.silu(summed)


def mix_heads(inner_seq, shared_seq, rate_seq, inner_taps, shared_taps, head_rows):
    length = inner_seq.shape[0]
    head_count = rate_seq.shape[1]
    head_width = inner_seq.shape[1] // head_count
    state_count = shared_seq.shape[1] // 2
    blocks = length // SPAN
    conv_inner = causal_conv(inner_seq, inner_taps)
    conv_shared = causal_conv(shared_seq, shared_taps)
    step_size = jax.nn.softplus(rate_seq + head_rows[0][None, :])
    log_decay = -step_size * jnp.exp(head_rows[1])[None, :]
    values = conv_inner.reshape(blocks, SPAN, head_count, head_width)
    writes = conv_shared[:, :state_count].reshape(blocks, SPAN, state_count)
    readouts = conv_shared[:, state_count:].reshape(blocks, SPAN, state_count)
    cumulative = jnp.cumsum(log_decay.reshape(blocks, SPAN, head_count), axis=1)
    scaled = values * step_size.reshape(blocks, SPAN, head_count)[:, :, :, None]
    pair_scores = jnp.einsum("bln,bsn->bls", readouts, writes, precision=highest)
    position = jnp.arange(SPAN)
    causal = position[:, None] >= position[None, :]
    spread = cumulative[:, :, None, :] - cumulative[:, None, :, :]
    kernel = (
        jnp.exp(jnp.where(causal[None, :, :, None], spread, -1e30)) * pair_scores[:, :, :, None]
    )
    within = jnp.einsum("blsh,bshp->blhp", kernel, scaled, precision=highest)
    to_end = jnp.exp(cumulative[:, -1:, :] - cumulative)
    block_states = jnp.einsum("bsn,bsh,bshp->bhnp", writes, to_end, scaled, precision=highest)
    block_decay = jnp.exp(cumulative[:, -1, :])

    def advance(carried, pieces):
        decay_now, fresh_state = pieces
        return (carried * decay_now[:, None, None] + fresh_state, carried)

    initial = jnp.zeros((head_count, state_count, head_width), jnp.float32)
    final_state, entering = lax.scan(advance, initial, (block_decay, block_states))
    across = jnp.einsum(
        "bln,blh,bhnp->blhp", readouts, jnp.exp(cumulative), entering, precision=highest
    )
    result = within + across + head_rows[2][None, None, :, None] * values
    return result.reshape(length, head_count * head_width)


def rms_scale(values, scales):
    return values * lax.rsqrt(jnp.mean(values * values, axis=-1, keepdims=True) + norm_eps) * scales


def gated_norm(mixer_out, gate_values, scales):
    return rms_scale(mixer_out * jax.nn.silu(gate_values), scales)


def adam_update(weight, moment, square, gradient, step_rate, decay_rate):
    moment_new = beta_moment * moment + (1.0 - beta_moment) * gradient
    square_new = beta_square * square + (1.0 - beta_square) * gradient * gradient
    moment_hat = moment_new / (1.0 - beta_moment**adam_step)
    square_hat = square_new / (1.0 - beta_square**adam_step)
    updated = weight - step_rate * (
        moment_hat / (jnp.sqrt(square_hat) + adam_eps) + decay_rate * weight
    )
    return (updated, moment_new, square_new)


def on_device(
    hidden_in,
    out_grad,
    prenorm,
    inproject,
    convtaps,
    headcoefs,
    postnorm,
    outproject,
    prenorm_first,
    inproject_first,
    convtaps_first,
    headcoefs_first,
    postnorm_first,
    outproject_first,
    prenorm_second,
    inproject_second,
    convtaps_second,
    headcoefs_second,
    postnorm_second,
    outproject_second,
):
    group_size = lax.axis_size("seq")
    group_rank = lax.axis_index("seq")
    pre_scale, in_matrix, conv_taps, post_scale, out_matrix = (
        lax.all_gather(prenorm.astype(jnp.bfloat16), "dp", axis=0, tiled=True),
        lax.all_gather(inproject.astype(jnp.bfloat16), "dp", axis=0, tiled=True),
        lax.all_gather(convtaps.astype(jnp.bfloat16), "dp", axis=1, tiled=True),
        lax.all_gather(postnorm.astype(jnp.bfloat16), "dp", axis=0, tiled=True),
        lax.all_gather(outproject.astype(jnp.bfloat16), "dp", axis=0, tiled=True),
    )
    seq_here, tok_here, model_width = hidden_in.shape
    row_count = seq_here * tok_here
    hidden = hidden_in.reshape(row_count, model_width).astype(jnp.float32)
    cot_low = out_grad.reshape(row_count, model_width)
    pre_wide = pre_scale.astype(jnp.float32)
    normed_value, norm_pull = jax.vjp(rms_scale, hidden, pre_wide)
    normed_low = normed_value.astype(jnp.bfloat16)
    project = jnp.dot(normed_low, in_matrix, preferred_element_type=jnp.float32)
    gate_values = project[:, :DI]
    inner_low = project[:, DI : 2 * DI].astype(jnp.bfloat16).reshape(seq_here, tok_here, DI)
    shared_low = (
        project[:, 2 * DI : 2 * DI + 2 * N].astype(jnp.bfloat16).reshape(seq_here, tok_here, 2 * N)
    )
    rate_low = project[:, 2 * DI + 2 * N :].astype(jnp.bfloat16).reshape(seq_here, tok_here, H)
    inner_heads, rate_heads = (
        lax.all_to_all(inner_low, "seq", split_axis=2, concat_axis=1, tiled=True),
        lax.all_to_all(rate_low, "seq", split_axis=2, concat_axis=1, tiled=True),
    )
    shared_whole = lax.all_gather(shared_low, "seq", axis=1, tiled=True)
    local_inner = DI // group_size
    local_heads = H // group_size
    conv_wide = conv_taps.astype(jnp.float32)
    inner_taps = lax.dynamic_slice_in_dim(conv_wide, group_rank * local_inner, local_inner, 1)
    shared_taps = conv_wide[:, DI:]
    head_rows = lax.dynamic_slice_in_dim(headcoefs, group_rank * local_heads, local_heads, 1)

    def forward_one(pieces):
        return mix_heads(
            pieces[0].astype(jnp.float32),
            pieces[1].astype(jnp.float32),
            pieces[2].astype(jnp.float32),
            inner_taps,
            shared_taps,
            head_rows,
        ).astype(jnp.bfloat16)

    mixer_heads = lax.map(forward_one, (inner_heads, shared_whole, rate_heads))
    mixer_tokens = lax.all_to_all(mixer_heads, "seq", split_axis=1, concat_axis=2, tiled=True)
    mixer_tokens = mixer_tokens.reshape(row_count, DI).astype(jnp.float32)
    post_wide = post_scale.astype(jnp.float32)
    gated_out, gated_pull = jax.vjp(gated_norm, mixer_tokens, gate_values, post_wide)
    gated_low = gated_out.astype(jnp.bfloat16)
    output = hidden + jnp.dot(gated_low, out_matrix, preferred_element_type=jnp.float32)
    outproj_grad = lax.dot_general(
        gated_low, cot_low, (((0,), (0,)), ((), ())), preferred_element_type=jnp.float32
    )
    gated_grad = lax.dot_general(
        cot_low, out_matrix, (((1,), (1,)), ((), ())), preferred_element_type=jnp.float32
    )
    mixer_grad, gate_grad, postnorm_grad = gated_pull(gated_grad)
    mixer_low = mixer_grad.astype(jnp.bfloat16).reshape(seq_here, tok_here, DI)
    grad_heads = lax.all_to_all(mixer_low, "seq", split_axis=2, concat_axis=1, tiled=True)

    def mixer_back(totals, pieces):
        inner_seq, shared_seq, rate_seq, grad_seq = pieces
        primal, pullback = jax.vjp(
            mix_heads,
            inner_seq.astype(jnp.float32),
            shared_seq.astype(jnp.float32),
            rate_seq.astype(jnp.float32),
            inner_taps,
            shared_taps,
            head_rows,
        )
        grad_inner, grad_shared, grad_rate, grad_itaps, grad_staps, grad_head = pullback(
            grad_seq.astype(jnp.float32)
        )
        totals = (totals[0] + grad_itaps, totals[1] + grad_staps, totals[2] + grad_head)
        return (
            totals,
            (grad_inner.astype(jnp.bfloat16), grad_shared, grad_rate.astype(jnp.bfloat16)),
        )

    zero_totals = (
        jnp.zeros_like(inner_taps),
        jnp.zeros_like(shared_taps),
        jnp.zeros_like(head_rows),
    )
    (itaps_total, staps_total, head_local), (inner_back, shared_back, rate_back) = lax.scan(
        mixer_back, zero_totals, (inner_heads, shared_whole, rate_heads, grad_heads)
    )
    shared_tok = lax.psum_scatter(
        shared_back.astype(jnp.bfloat16), "seq", scatter_dimension=1, tiled=True
    )
    inner_tok, rate_tok = (
        lax.all_to_all(inner_back, "seq", split_axis=1, concat_axis=2, tiled=True),
        lax.all_to_all(rate_back, "seq", split_axis=1, concat_axis=2, tiled=True),
    )
    project_grad = jnp.concatenate(
        [
            gate_grad.astype(jnp.bfloat16),
            inner_tok.reshape(row_count, DI),
            shared_tok.reshape(row_count, 2 * N),
            rate_tok.reshape(row_count, H),
        ],
        axis=1,
    )
    inproj_grad = lax.dot_general(
        normed_low, project_grad, (((0,), (0,)), ((), ())), preferred_element_type=jnp.float32
    )
    normed_grad = lax.dot_general(
        project_grad, in_matrix, (((1,), (1,)), ((), ())), preferred_element_type=jnp.float32
    )
    hidden_grad, prenorm_grad = norm_pull(normed_grad)
    input_gradient = hidden_grad + cot_low.astype(jnp.float32)
    inner_full = lax.dynamic_update_slice_in_dim(
        jnp.zeros((conv_wide.shape[0], DI), jnp.float32), itaps_total, group_rank * local_inner, 1
    )
    conv_grad = jnp.concatenate([inner_full, staps_total], axis=1)
    head_full = lax.dynamic_update_slice_in_dim(
        jnp.zeros((3, H), jnp.float32), head_local, group_rank * local_heads, 1
    )
    head_total = lax.psum(head_full, ("dp", "seq"))
    grad_tuple = (prenorm_grad, inproj_grad, conv_grad, postnorm_grad, outproj_grad)
    owned_grads = (
        lax.psum_scatter(grad_tuple[0], "dp", scatter_dimension=0, tiled=True),
        lax.psum_scatter(grad_tuple[1], "dp", scatter_dimension=0, tiled=True),
        lax.psum_scatter(grad_tuple[2], "dp", scatter_dimension=1, tiled=True),
        lax.psum_scatter(grad_tuple[3], "dp", scatter_dimension=0, tiled=True),
        lax.psum_scatter(grad_tuple[4], "dp", scatter_dimension=0, tiled=True),
    )
    owned_grads = lax.psum(
        (owned_grads[0], owned_grads[1], owned_grads[2], owned_grads[3], owned_grads[4]), "seq"
    )
    prenorm_owned, inproj_owned, conv_owned, postnorm_owned, outproj_owned = owned_grads
    prenorm_new, prenorm_mom, prenorm_sq = adam_update(
        prenorm, prenorm_first, prenorm_second, prenorm_owned, rate_vector, 0.0
    )
    inproj_new, inproj_mom, inproj_sq = adam_update(
        inproject, inproject_first, inproject_second, inproj_owned, rate_matrix, weight_decay
    )
    conv_new, conv_mom, conv_sq = adam_update(
        convtaps, convtaps_first, convtaps_second, conv_owned, rate_vector, 0.0
    )
    head_new, head_mom, head_sq = adam_update(
        headcoefs, headcoefs_first, headcoefs_second, head_total, rate_vector, 0.0
    )
    postnorm_new, postnorm_mom, postnorm_sq = adam_update(
        postnorm, postnorm_first, postnorm_second, postnorm_owned, rate_vector, 0.0
    )
    outproj_new, outproj_mom, outproj_sq = adam_update(
        outproject, outproject_first, outproject_second, outproj_owned, rate_matrix, weight_decay
    )
    output = output.reshape(seq_here, tok_here, model_width)
    input_gradient = input_gradient.reshape(seq_here, tok_here, model_width)
    return (
        output,
        input_gradient,
        prenorm_owned,
        inproj_owned,
        conv_owned,
        head_total,
        postnorm_owned,
        outproj_owned,
        prenorm_new,
        inproj_new,
        conv_new,
        head_new,
        postnorm_new,
        outproj_new,
        prenorm_mom,
        inproj_mom,
        conv_mom,
        head_mom,
        postnorm_mom,
        outproj_mom,
        prenorm_sq,
        inproj_sq,
        conv_sq,
        head_sq,
        postnorm_sq,
        outproj_sq,
    )


def solution(mesh):
    placed = (
        P("dp", "seq", None),
        P("dp", "seq", None),
        P("dp"),
        P("dp", None),
        P(None, "dp"),
        P(),
        P("dp"),
        P("dp", None),
        P("dp"),
        P("dp", None),
        P(None, "dp"),
        P(),
        P("dp"),
        P("dp", None),
        P("dp"),
        P("dp", None),
        P(None, "dp"),
        P(),
        P("dp"),
        P("dp", None),
    )
    return jax.shard_map(
        on_device,
        mesh=mesh,
        in_specs=placed,
        out_specs=(
            P("dp", "seq", None),
            P("dp", "seq", None),
            P("dp"),
            P("dp", None),
            P(None, "dp"),
            P(),
            P("dp"),
            P("dp", None),
            P("dp"),
            P("dp", None),
            P(None, "dp"),
            P(),
            P("dp"),
            P("dp", None),
            P("dp"),
            P("dp", None),
            P(None, "dp"),
            P(),
            P("dp"),
            P("dp", None),
            P("dp"),
            P("dp", None),
            P(None, "dp"),
            P(),
            P("dp"),
            P("dp", None),
        ),
        check_vma=False,
    )
```

profile of v0, /device:TPU:0, one launch (start us, length us, event | category | flops | bytes accessed | tf_op | source)
XLA Modules:
  0.0 1324.9 jit_solution(8660592907399058365)
XLA Ops:
  7.3 4.3 convert_element_type.179
  14.4 15.3 %all-reduce.27 = bf16[1536]{0:T(1024)(128)(2,1)S(1)} all-reduce(bf16[1536]{0:T(1024)(128)(2,1)S(1)} %dynamic-update-slice), channel_id=1, replica_groups=mesh['dp'=8,'seq'=4] {'dp'}, use_global_device_ids=true, to_apply=%add.27 | all-reduce | flops 1536 | bytes 6144
  29.8 8.2 all-gather.1
  38.6 79.8 %all-gather.6.cloned.1.call-done = bf16[1536,6448]{1,0:T(8,128)(2,1)} async-done(((bf16[192,6448]{1,0:T(8,128)(2,1)}), bf16[1536,6448]{1,0:T(8,128)(2,1)}) %all-gather.6.cloned.1.call-update) | async-done | bytes 19808272 | tf_op jit(solution)/shard_map/all_gather | solution.py:118
  118.4 14.5 %fusion.144 = (bf16[256,6448]{0,1:T(8,128)(2,1)}, f32[256,6448]{0,1:T(8,128)}) fusion(bf16[1536,6448]{1,0:T(8,128)(2,1)} %all-gather.6.cloned.1.call-done, bf16[1,256,1536]{2,1,0:T(8,128)(2,1)S(1)} %copy-done.12, f32[1536]{0:T(1024)S(1)} %convert_element_type.177, f32[256]{0:T(256)S(1)} %fusion.125), kind=kOutput, calls=%fused_computation.255 | convolution fusion | flops 5074137088 | bytes 30505984 | tf_op jit(solution)/shard_map/dot_general | solution.py:130
  135.7 4.6 all-to-all-start.1
  141.8 17.5 %copy.552 = bf16[1,256,3072]{1,0,2:T(2,128)(2,1)S(1)} copy(bf16[1,256,3072]{1,2,0:T(8,128)(2,1)S(1)} %slice_bitcast_fusion) | data formatting | bytes 3145728 | tf_op jit(solution)/shard_map/reshape | solution.py:132
  159.4 16.7 %reduce.25 = bf16[3072,256]{1,0:T(8,128)(2,1)} reduce(bf16[3072,1,256]{2,1,0:T(2,128)(2,1)S(1)} %bitcast.309, bf16[]{:T(256)} %broadcast.416), dimensions={1}, to_apply=%bitcast.274.reduce_sub_computation | reduce | bytes 3145730
  176.1 3.7 reshape.637
  179.8 5.1 all-to-all-start
  185.9 46.2 %all-gather = bf16[1024,256]{0,1:T(8,128)(2,1)S(1)} all-gather(bf16[256,256]{0,1:T(8,128)(2,1)S(1)} %slice.240), channel_id=2, replica_groups=mesh['dp'=8,'seq'=4] {'seq'}, dimensions={0}, use_global_device_ids=true | all-gather | bytes 655360 | tf_op jit(solution)/shard_map/all_gather | solution.py:141
  252.9 3.6 fusion.46
  256.5 3.5 copy.330
  260.0 3.4 reshape.550
  263.5 5.8 fusion.75
  272.5 13.6 %while.71 = (s32[]{:T(128)}, f32[12,128,64]{2,1,0:T(8,128)}, f32[4,12,128,64]{2,3,1,0:T(8,128)}, f32[4,12]{1,0:T(4,128)S(1)}, f32[4,12,128,64]{3,2,1,0:T(8,128)}, /*index=5*/s32[]{:T(128)}, s32[]{:T(128)}) while((s32[]{:T(128)}, f32[12,128,64]{2,1,0:T(8,128)}, f32[4,12,128,64]{2,3,1,0:T(8,128)}, f32[4,12]{1,0:T(4,128)S(1)}, ...), condition=%wide.region_4.5_spmd.clone, body=%wide.region_3.4_spmd.clone.sunk | while | flops 294915 | bytes 3145979 | solution.py:65
  286.1 4.3 fusion.146
  290.5 25.7 %fusion.44 = bf16[4,256,12,64]{1,3,2,0:T(8,128)(2,1)S(1)} fusion(f32[4,256,12,64]{1,3,2,0:T(8,128)S(1)} %bitcast.326, f32[4,256,12,64]{1,0,3,2:T(4,128)S(1)} %copy-done.8, f32[4,256,256]{2,1,0:T(8,128)S(1)} %copy-done.36, f32[4,256,12]{1,2,0:T(8,128)S(1)} %bitcast.333, pred[256,256]{1,0:T(8,128)(4,1)S(1)} %iota_compare_fusion, ...), kind=kOutput, calls=%fused_computation.77 | convolution fusion | flops 2430074880 | bytes 9125936 | tf_op jit(solution)/shard_map/while/body/eval_jaxpr/blsh,bshp->blhp/dot_general | solution.py:55
  319.7 7.2 copy.348
  326.9 11.4 reduce.26
  338.3 3.7 reshape.639
  342.0 4.6 all-to-all-start.2
  346.7 8.9 all-gather.2
  357.6 22.3 %all-to-all-done.2 = bf16[4,2,98304]{2,1,0:T(2,128)(2,1)S(1)} async-done(((bf16[4,2,98304]{2,1,0:T(2,128)(2,1)}), bf16[4,2,98304]{2,1,0:T(2,128)(2,1)S(1)}, u32[]{:S(2)}, u32[]{:S(2)}) %all-to-all-start.2) | async-done | bytes 1572896 | tf_op jit(solution)/shard_map/all_to_all | solution.py:160
  387.1 3.6 copy.350
  390.7 5.6 multiply_reduce_fusion.8
  396.4 8.5 multiply_reduce_fusion.1
  404.9 4.7 fusion.27
  409.6 19.0 %copy.551 = bf16[1,256,3072]{1,0,2:T(2,128)(2,1)} copy(bf16[1,256,3072]{1,2,0:T(8,128)(2,1)S(1)} %get-tuple-element.576) | data formatting | bytes 3145728 | tf_op jit(solution)/shard_map/reshape | solution.py:173
  428.6 16.6 %reduce.27 = bf16[3072,256]{1,0:T(8,128)(2,1)S(1)} reduce(bf16[3072,1,256]{2,1,0:T(2,128)(2,1)} %bitcast.313, bf16[]{:T(256)} %broadcast.416), dimensions={1}, to_apply=%bitcast.273.reduce_sub_computation | reduce | bytes 3145730
  447.0 3.6 all-to-all-start.3
  452.7 11.0 while.72
  463.7 23.3 %all-to-all-done.3 = bf16[4,2,98304]{2,1,0:T(2,128)(2,1)S(1)} async-done(((bf16[4,2,98304]{2,1,0:T(2,128)(2,1)}), bf16[4,2,98304]{2,1,0:T(2,128)(2,1)S(1)}, u32[]{:S(2)}, u32[]{:S(2)}) %all-to-all-start.3) | async-done | bytes 1572896 | tf_op jit(solution)/shard_map/all_to_all | solution.py:174
  492.3 4.1 fusion.78
  496.4 11.2 fusion.86
  510.3 24.4 %while.73 = (s32[]{:T(128)}, f32[12,128,64]{2,1,0:T(8,128)S(1)}, f32[4,12]{1,0:T(4,128)}, f32[4,12,128,64]{3,2,1,0:T(8,128)}, f32[4,12,128,64]{2,3,1,0:T(8,128)}...) while((s32[]{:T(128)}, f32[12,128,64]{2,1,0:T(8,128)S(1)}, ...), condition=%wide.region_11.12_spmd.clone, body=%wide.region_9.11_spmd.clone.sunk | while | flops 589816 | bytes 4325816 | solution.py:65
  534.7 13.3 %fusion.13 = (f32[4,256,12]{1,2,0:T(8,128)}, f32[4,256,12]{1,2,0:T(8,128)}, f32[4,256,256]{2,1,0:T(8,128)S(1)}) fusion(f32[4,256,256]{2,1,0:T(8,128)} %fusion.145, f32[4,256,12]{1,2,0:T(8,128)} %bitcast.334, pred[256,256]{1,0:T(8,128)(4,1)} %copy-done.58, bf16[4,12,64,256]{3,2,1,0:T(8,128)(2,1)S(1)} %bitcast.301, f32[4,256,12,64]{1,0,3,2:T(4,128)} %copy-done.7, ...), kind=kOutput, calls=%fused_computation.27 | convolution fusion | flops 2444730368 | bytes 7077888 | tf_op jit(solution)/shard_map/while/body/eval_jaxpr/transpose(jvp(blsh,bshp->blhp))/dot_general | solution.py:55
  548.0 10.1 fusion.81
  562.9 3.4 convolution_add_fusion.1
  572.8 9.2 fusion.93
  583.0 7.5 fusion.41
  590.5 10.4 multiply_reduce_fusion
  608.7 8.7 fusion.34
  618.5 9.9 reduce-window.16
  638.3 4.1 copy.358
  644.8 3.7 copy.359
  651.6 9.7 multiply_reduce_fusion.5
  663.3 4.1 copy.550
  667.4 12.6 reduce.29
  679.9 3.7 reshape.645
  683.6 4.8 all-to-all-start.4
  691.1 33.8 %all-to-all-done.4 = bf16[4,2,98304]{2,1,0:T(2,128)(2,1)} async-done(((bf16[4,2,98304]{2,1,0:T(2,128)(2,1)}), bf16[4,2,98304]{2,1,0:T(2,128)(2,1)}, u32[]{:S(2)}, u32[]{:S(2)}) %all-to-all-start.4) | async-done | bytes 1572896 | tf_op jit(solution)/shard_map/all_to_all | solution.py:208
  724.9 4.4 reshape.646
  729.4 3.3 copy.440
  735.3 21.1 %fusion.97 = f32[1536,6448]{1,0:T(8,128)} fusion(bf16[256,48]{0,1:T(8,128)(2,1)S(1)} %reshape.570, bf16[256,256]{0,1:T(8,128)(2,1)} %bitcast.347, bf16[256,3072]{0,1:T(8,128)(2,1)} %bitcast.319, bf16[256,3072]{0,1:T(8,128)(2,1)} %get-tuple-element.575, bf16[1,256,1536]{2,1,0:T(8,128)(2,1)} %param.26, f32[1536]{0:T(1024)S(1)} %copy-done.43, ...), kind=kOutput, calls=%fused_computation.161 | convolution fusion | flops 5085691904 | bytes 43711488 | tf_op jit(solution)/shard_map/dot_general | solution.py:220
  759.1 231.4 %reduce-scatter.9.cloned.1.call-done = f32[192,6448]{1,0:T(8,128)} async-done(((f32[1536,6448]{1,0:T(8,128)}), f32[192,6448]{1,0:T(8,128)}) %reduce-scatter.9.cloned.1.call-update) | async-done | bytes 4952080 | tf_op jit(solution)/shard_map/reduce_scatter | solution.py:239
  991.7 7.7 fusion.50
  1001.0 39.4 %psum.45 = f32[3,48]{1,0:T(4,128)S(1)} all-reduce(f32[3,48]{1,0:T(4,128)S(1)} %dynamic_update_slice.48), channel_id=1, replica_groups=mesh['dp'=8,'seq'=4] {'dp','seq'}, use_global_device_ids=true, to_apply=%region_42.43 | all-reduce | flops 144 | bytes 1152 | tf_op jit(solution)/shard_map/psum | solution.py:235
  1042.4 11.3 fusion.60
  1053.7 25.5 %all-reduce.30 = (f32[1536]{0:T(1024)S(1)}, f32[3072]{0:T(1024)S(1)}) all-reduce(f32[1536]{0:T(1024)S(1)} %get-tuple-element.485, f32[3072]{0:T(1024)S(1)} %copy-done.74), channel_id=4, replica_groups=mesh['dp'=8,'seq'=4] {'dp'}, use_global_device_ids=true, to_apply=%region_22.23.clone | all-reduce | flops 4608 | bytes 36864
  1079.4 27.0 %all-reduce.31 = (f32[192]{0:T(256)S(1)}, f32[5,416]{1,0:T(8,128)S(1)}, f32[384]{0:T(512)S(1)}) all-reduce(f32[192]{0:T(256)S(1)} %dynamic-slice.3, f32[5,416]{1,0:T(8,128)S(1)} %copy.435, f32[384]{0:T(512)S(1)} %dynamic-slice.5), channel_id=1, replica_groups=mesh['dp'=8,'seq'=4] {'seq'}, use_global_device_ids=true, to_apply=%region_23.24 | all-reduce | flops 2656 | bytes 21248 | tf_op jit(solution)/shard_map/psum | solution.py:244
  1109.9 185.4 %all-reduce.35.cloned.1.call-done = (f32[192,6448]{1,0:T(8,128)}, f32[384,1536]{1,0:T(8,128)}) async-done(((f32[192,6448]{1,0:T(8,128)}, f32[384,1536]{1,0:T(8,128)}), (f32[192,6448]{1,0:T(8,128)}, f32[384,1536]{1,0:T(8,128)})) %all-reduce.35.cloned.1.call-update) | async-done | bytes 7311376 | tf_op jit(solution)/shard_map/psum | solution.py:244
  1295.3 13.9 %multiply_subtract_fusion = (f32[192,6448]{1,0:T(8,128)}, f32[192,6448]{1,0:T(8,128)}, f32[192,6448]{1,0:T(8,128)}) fusion(f32[192,6448]{1,0:T(8,128)} %param.29, f32[192,6448]{1,0:T(8,128)} %get-tuple-element.808, f32[192,6448]{1,0:T(8,128)} %param.35, f32[192,6448]{1,0:T(8,128)} %param.41), kind=kLoop, calls=%fused_computation.40 | loop fusion | flops 18570240 | bytes 34664448 | tf_op jit(solution)/shard_map/sub | solution.py:86
  1309.7 4.3 multiply_subtract_fusion.1
  (458 shorter events, 162.3 us)
Async XLA Ops:
  7.2 111.2 %all-gather.6.cloned.1.call-start = ((), (), s32[]{:S(2)}) async-start(), calls=%async_computation.10 | async-start | bytes 22560768 | tf_op jit(solution)/shard_map/all_gather | solution.py:118
  11.5 18.2 %copy-start.56 = (f32[5,416]{1,0:T(8,128)S(1)}, f32[5,416]{1,0:T(8,128)}, u32[]{:S(2)}) copy-start(f32[5,416]{1,0:T(8,128)} %param.30) | copy-start | bytes 24964
  11.6 26.5 %copy-start.89 = (f32[3,48]{1,0:T(4,128)S(1)}, f32[3,48]{1,0:T(4,128)}, u32[]{:S(2)}) copy-start(f32[3,48]{1,0:T(4,128)} %param.31) | copy-start | bytes 1732
  11.6 26.6 %copy-start.12 = (bf16[1,256,1536]{2,1,0:T(8,128)(2,1)S(1)}, bf16[1,256,1536]{2,1,0:T(8,128)(2,1)}, u32[]{:S(2)}) copy-start(bf16[1,256,1536]{2,1,0:T(8,128)(2,1)} %param.26) | copy-start | bytes 2359300
  11.6 384.7 %all-gather.8.cloned.1.call-start = ((), (), s32[]{:S(2)}) async-start(), calls=%async_computation.11 | async-start | bytes 10616832 | tf_op jit(solution)/shard_map/all_gather | solution.py:121
  29.7 103.2 %copy-start.42 = (f32[1536]{0:T(1024)}, f32[1536]{0:T(1024)S(1)}, u32[]{:S(2)}) copy-start(f32[1536]{0:T(1024)S(1)} %convert_element_type.177) | copy-start | bytes 18436
  38.1 94.8 %copy-start.94 = (f32[3,12]{1,0:T(4,128)}, f32[3,12]{1,0:T(4,128)S(1)}, u32[]{:S(2)}) copy-start(f32[3,12]{1,0:T(4,128)S(1)} %constant_dynamic-slice_fusion.4) | copy-start | bytes 436
  38.2 214.6 %copy-start.62 = (f32[768]{0:T(1024)}, f32[768]{0:T(1024)S(1)}, u32[]{:S(2)}) copy-start(f32[768]{0:T(1024)S(1)} %get-tuple-element.498) | copy-start | bytes 9220
  38.2 214.6 %copy-start.64 = (f32[768]{0:T(1024)}, f32[768]{0:T(1024)S(1)}, u32[]{:S(2)}) copy-start(f32[768]{0:T(1024)S(1)} %get-tuple-element.499) | copy-start | bytes 9220
  38.2 214.6 %copy-start.66 = (f32[768]{0:T(1024)}, f32[768]{0:T(1024)S(1)}, u32[]{:S(2)}) copy-start(f32[768]{0:T(1024)S(1)} %get-tuple-element.500) | copy-start | bytes 9220
  38.2 214.6 %copy-start.68 = (f32[768]{0:T(1024)}, f32[768]{0:T(1024)S(1)}, u32[]{:S(2)}) copy-start(f32[768]{0:T(1024)S(1)} %get-tuple-element.501) | copy-start | bytes 9220
  38.5 94.5 %copy-start.83 = (f32[256]{0:T(256)}, f32[256]{0:T(256)S(1)}, u32[]{:S(2)}) copy-start(f32[256]{0:T(256)S(1)} %fusion.64) | copy-start | bytes 3076
  38.5 94.5 %copy-start.54 = (f32[256]{0:T(256)}, f32[256]{0:T(256)S(1)}, u32[]{:S(2)}) copy-start(f32[256]{0:T(256)S(1)} %fusion.125) | copy-start | bytes 3076
  38.5 202.5 %copy-start.85 = (f32[12]{0:T(128)}, f32[12]{0:T(128)S(1)}, u32[]{:S(2)}) copy-start(f32[12]{0:T(128)S(1)} %get-tuple-element.603) | copy-start | bytes 148
  38.5 202.5 %copy-start.87 = (f32[12]{0:T(128)}, f32[12]{0:T(128)S(1)}, u32[]{:S(2)}) copy-start(f32[12]{0:T(128)S(1)} %get-tuple-element.604) | copy-start | bytes 148
  38.5 251.9 %copy-start.111 = (f32[12]{0:T(128)}, f32[12]{0:T(128)S(1)}, u32[]{:S(2)}) copy-start(f32[12]{0:T(128)S(1)} %get-tuple-element.602) | copy-start | bytes 148
  38.6 194.5 %copy-start.75 = (f32[1,256]{1,0:T(1,128)}, f32[1,256]{1,0:T(1,128)S(1)}, u32[]{:S(2)}) copy-start(f32[1,256]{1,0:T(1,128)S(1)} %get-tuple-element.590) | copy-start | bytes 3076
  38.6 194.5 %copy-start.77 = (f32[1,256]{1,0:T(1,128)}, f32[1,256]{1,0:T(1,128)S(1)}, u32[]{:S(2)}) copy-start(f32[1,256]{1,0:T(1,128)S(1)} %get-tuple-element.591) | copy-start | bytes 3076
  38.6 194.5 %copy-start.79 = (f32[1,256]{1,0:T(1,128)}, f32[1,256]{1,0:T(1,128)S(1)}, u32[]{:S(2)}) copy-start(f32[1,256]{1,0:T(1,128)S(1)} %get-tuple-element.592) | copy-start | bytes 3076
  38.6 194.4 %copy-start.81 = (f32[1,256]{1,0:T(1,128)}, f32[1,256]{1,0:T(1,128)S(1)}, u32[]{:S(2)}) copy-start(f32[1,256]{1,0:T(1,128)S(1)} %get-tuple-element.593) | copy-start | bytes 3076
  135.7 44.1 %all-to-all-start.1 = ((bf16[4,2,1536]{2,1,0:T(2,128)(2,1)}), bf16[4,2,1536]{2,1,0:T(2,128)(2,1)S(1)}, u32[]{:S(2)}, u32[]{:S(2)}) async-start(bf16[4,2,1536]{2,1,0:T(2,128)(2,1)} %reshape.635), calls=%async_computation.1 | async-start | bytes 49152 | tf_op jit(solution)/shard_map/all_to_all | solution.py:139
  179.8 65.3 %all-to-all-start = ((bf16[4,2,98304]{2,1,0:T(2,128)(2,1)}), bf16[4,2,98304]{2,1,0:T(2,128)(2,1)}, u32[]{:S(2)}, u32[]{:S(2)}) async-start(bf16[4,2,98304]{2,1,0:T(2,128)(2,1)} %reshape.637), calls=%async_computation | async-start | bytes 3145728 | tf_op jit(solution)/shard_map/all_to_all | solution.py:138
  184.9 105.5 %copy-start.58 = (pred[256,256]{1,0:T(8,128)(4,1)}, pred[256,256]{1,0:T(8,128)(4,1)S(1)}, u32[]{:S(2)}) copy-start(pred[256,256]{1,0:T(8,128)(4,1)S(1)} %iota_compare_fusion) | copy-start | bytes 196612
  241.2 49.3 %copy-start.40 = (f32[4,256,12]{1,2,0:T(8,128)}, f32[4,256,12]{1,2,0:T(8,128)S(1)}, u32[]{:S(2)}) copy-start(f32[4,256,12]{1,2,0:T(8,128)S(1)} %get-tuple-element.596) | copy-start | bytes 147460
  244.4 46.1 %copy-start.38 = (f32[4,12,256]{2,1,0:T(8,128)}, f32[4,12,256]{2,1,0:T(8,128)S(1)}, u32[]{:S(2)}) copy-start(f32[4,12,256]{2,1,0:T(8,128)S(1)} %reshape.620) | copy-start | bytes 147460
  245.1 18.3 %copy-start.34 = (f32[4,256,12]{1,2,0:T(8,128)}, f32[4,256,12]{1,2,0:T(8,128)S(1)}, u32[]{:S(2)}) copy-start(f32[4,256,12]{1,2,0:T(8,128)S(1)} %get-tuple-element.595) | copy-start | bytes 147460
  272.5 13.6 %copy-start.20 = (f32[4,256,128]{2,1,0:T(8,128)S(1)}, f32[4,256,128]{2,1,0:T(8,128)}, u32[]{:S(2)}) copy-start(f32[4,256,128]{2,1,0:T(8,128)} %copy-done.19) | copy-start | bytes 1572868
  342.0 37.8 %all-to-all-start.2 = ((bf16[4,2,98304]{2,1,0:T(2,128)(2,1)}), bf16[4,2,98304]{2,1,0:T(2,128)(2,1)S(1)}, u32[]{:S(2)}, u32[]{:S(2)}) async-start(bf16[4,2,98304]{2,1,0:T(2,128)(2,1)} %reshape.639), calls=%async_computation.2 | async-start | bytes 3145728 | tf_op jit(solution)/shard_map/all_to_all | solution.py:160
  447.0 40.0 %all-to-all-start.3 = ((bf16[4,2,98304]{2,1,0:T(2,128)(2,1)}), bf16[4,2,98304]{2,1,0:T(2,128)(2,1)S(1)}, u32[]{:S(2)}, u32[]{:S(2)}) async-start(bf16[4,2,98304]{2,1,0:T(2,128)(2,1)} %reshape.641), calls=%async_computation.3 | async-start | bytes 3145728 | tf_op jit(solution)/shard_map/all_to_all | solution.py:174
  450.6 284.7 %reduce-scatter.7.cloned.1.call-start = ((), (), s32[]{:S(2)}) async-start(), calls=%async_computation.12 | async-start | bytes 655360 | tf_op jit(solution)/shard_map/reduce_scatter | solution.py:204
  492.3 42.4 %copy-start.4 = (bf16[1,256,3072]{1,2,0:T(8,128)(2,1)}, bf16[1,256,3072]{1,2,0:T(8,128)(2,1)S(1)}, u32[]{:S(2)}) copy-start(bf16[1,256,3072]{1,2,0:T(8,128)(2,1)S(1)} %copy.439) | copy-start | bytes 4718596
  534.7 13.3 %copy-start.35 = (f32[4,256,12]{1,2,0:T(8,128)S(1)}, f32[4,256,12]{1,2,0:T(8,128)}, u32[]{:S(2)}) copy-start(f32[4,256,12]{1,2,0:T(8,128)} %copy-done.34) | copy-start | bytes 147460
  534.7 13.3 %copy-start.41 = (f32[4,256,12]{1,2,0:T(8,128)S(1)}, f32[4,256,12]{1,2,0:T(8,128)}, u32[]{:S(2)}) copy-start(f32[4,256,12]{1,2,0:T(8,128)} %copy-done.40) | copy-start | bytes 147460
  572.5 186.5 %reduce-scatter.11.cloned.1.call-start = ((), (), s32[]{:S(2)}) async-start(), calls=%async_computation.14 | async-start | bytes 21233664 | tf_op jit(solution)/shard_map/reduce_scatter | solution.py:242
  600.9 16.6 %copy-start.50 = (f32[4,256,12]{1,2,0:T(8,128)}, f32[4,256,12]{1,2,0:T(8,128)S(1)}, u32[]{:S(2)}) copy-start(f32[4,256,12]{1,2,0:T(8,128)S(1)} %get-tuple-element.483) | copy-start | bytes 147460
  600.9 17.5 %copy-start.48 = (f32[4,256,12]{1,2,0:T(8,128)}, f32[4,256,12]{1,2,0:T(8,128)S(1)}, u32[]{:S(2)}) copy-start(f32[4,256,12]{1,2,0:T(8,128)S(1)} %get-tuple-element.484) | copy-start | bytes 147460
  635.0 48.6 %all-to-all-start.5 = ((bf16[4,2,1536]{2,1,0:T(2,128)(2,1)}), bf16[4,2,1536]{2,1,0:T(2,128)(2,1)S(1)}, u32[]{:S(2)}, u32[]{:S(2)}) async-start(bf16[4,2,1536]{2,1,0:T(2,128)(2,1)} %reshape.643), calls=%async_computation.6 | async-start | bytes 49152 | tf_op jit(solution)/shard_map/all_to_all | solution.py:209
  683.6 41.3 %all-to-all-start.4 = ((bf16[4,2,98304]{2,1,0:T(2,128)(2,1)}), bf16[4,2,98304]{2,1,0:T(2,128)(2,1)}, u32[]{:S(2)}, u32[]{:S(2)}) async-start(bf16[4,2,98304]{2,1,0:T(2,128)(2,1)} %reshape.645), calls=%async_computation.4 | async-start | bytes 3145728 | tf_op jit(solution)/shard_map/all_to_all | solution.py:208
  688.5 302.0 %reduce-scatter.9.cloned.1.call-start = ((), (), s32[]{:S(2)}) async-start(), calls=%async_computation.13 | async-start | bytes 45121536 | tf_op jit(solution)/shard_map/reduce_scatter | solution.py:239
  756.5 284.6 %reduce-scatter.13.cloned.1.call-start = ((), (), s32[]{:S(2)}) async-start(), calls=%async_computation.15 | async-start | bytes 1916928
  759.0 536.3 %all-reduce.35.cloned.1.call-start = ((), (), s32[]{:S(2)}) async-start(), calls=%async_computation.16 | async-start | bytes 14745600 | tf_op jit(solution)/shard_map/psum | solution.py:244
  991.6 48.8 %copy-start.90 = (f32[3,48]{1,0:T(4,128)S(1)}, f32[3,48]{1,0:T(4,128)}, u32[]{:S(2)}) copy-start(f32[3,48]{1,0:T(4,128)} %param.31) | copy-start | bytes 1732
  991.6 48.8 %copy-start.100 = (f32[3,48]{1,0:T(4,128)S(1)}, f32[3,48]{1,0:T(4,128)}, u32[]{:S(2)}) copy-start(f32[3,48]{1,0:T(4,128)} %param.37) | copy-start | bytes 1732
  991.7 48.8 %copy-start.101 = (f32[3,48]{1,0:T(4,128)S(1)}, f32[3,48]{1,0:T(4,128)}, u32[]{:S(2)}) copy-start(f32[3,48]{1,0:T(4,128)} %param.43) | copy-start | bytes 1732
  991.7 50.5 %copy-start.51 = (bf16[1,256,256]{1,2,0:T(8,128)(2,1)S(1)}, bf16[1,256,256]{1,2,0:T(8,128)(2,1)}, u32[]{:S(2)}) copy-start(bf16[1,256,256]{1,2,0:T(8,128)(2,1)} %reduce-scatter.7.cloned.1.call-done) | copy-start | bytes 393220
  1042.2 64.1 %copy-start.84 = (f32[256]{0:T(256)S(1)}, f32[256]{0:T(256)}, u32[]{:S(2)}) copy-start(f32[256]{0:T(256)} %copy-done.83) | copy-start | bytes 3076
  1042.2 64.1 %copy-start.107 = (f32[192]{0:T(256)S(1)}, f32[192]{0:T(256)}, u32[]{:S(2)}) copy-start(f32[192]{0:T(256)} %param.28) | copy-start | bytes 2308
  1042.2 64.1 %copy-start.108 = (f32[192]{0:T(256)S(1)}, f32[192]{0:T(256)}, u32[]{:S(2)}) copy-start(f32[192]{0:T(256)} %param.34) | copy-start | bytes 2308
  1042.2 64.1 %copy-start.109 = (f32[192]{0:T(256)S(1)}, f32[192]{0:T(256)}, u32[]{:S(2)}) copy-start(f32[192]{0:T(256)} %param.40) | copy-start | bytes 2308
  1042.3 64.7 %copy-start.92 = (f32[384]{0:T(512)S(1)}, f32[384]{0:T(512)}, u32[]{:S(2)}) copy-start(f32[384]{0:T(512)} %param.32) | copy-start | bytes 4612
  1042.3 64.7 %copy-start.102 = (f32[384]{0:T(512)S(1)}, f32[384]{0:T(512)}, u32[]{:S(2)}) copy-start(f32[384]{0:T(512)} %param.38) | copy-start | bytes 4612
  1042.3 64.7 %copy-start.103 = (f32[384]{0:T(512)S(1)}, f32[384]{0:T(512)}, u32[]{:S(2)}) copy-start(f32[384]{0:T(512)} %param.44) | copy-start | bytes 4612
  1042.3 65.3 %copy-start.57 = (f32[5,416]{1,0:T(8,128)S(1)}, f32[5,416]{1,0:T(8,128)}, u32[]{:S(2)}) copy-start(f32[5,416]{1,0:T(8,128)} %param.30) | copy-start | bytes 24964
  1042.3 65.3 %copy-start.71 = (f32[5,416]{1,0:T(8,128)S(1)}, f32[5,416]{1,0:T(8,128)}, u32[]{:S(2)}) copy-start(f32[5,416]{1,0:T(8,128)} %param.36) | copy-start | bytes 24964
  1042.3 65.3 %copy-start.72 = (f32[5,416]{1,0:T(8,128)S(1)}, f32[5,416]{1,0:T(8,128)}, u32[]{:S(2)}) copy-start(f32[5,416]{1,0:T(8,128)} %param.42) | copy-start | bytes 24964
  1042.3 65.9 %copy-start.13 = (bf16[1,256,1536]{2,1,0:T(8,128)(2,1)S(1)}, bf16[1,256,1536]{2,1,0:T(8,128)(2,1)}, u32[]{:S(2)}) copy-start(bf16[1,256,1536]{2,1,0:T(8,128)(2,1)} %param.26) | copy-start | bytes 2359300
  1042.3 65.9 %copy-start.31 = (bf16[1,256,1536]{2,1,0:T(8,128)(2,1)S(1)}, bf16[1,256,1536]{2,1,0:T(8,128)(2,1)}, u32[]{:S(2)}) copy-start(bf16[1,256,1536]{2,1,0:T(8,128)(2,1)} %param.27) | copy-start | bytes 2359300
  1106.3 202.9 %copy-start.73 = (f32[5,416]{1,0:T(8,128)}, f32[5,416]{1,0:T(8,128)S(1)}, u32[]{:S(2)}) copy-start(f32[5,416]{1,0:T(8,128)S(1)} %get-tuple-element.809) | copy-start | bytes 24964
  1106.3 202.9 %copy-start.104 = (f32[384]{0:T(512)}, f32[384]{0:T(512)S(1)}, u32[]{:S(2)}) copy-start(f32[384]{0:T(512)S(1)} %get-tuple-element.811) | copy-start | bytes 4612
  1106.3 202.9 %copy-start.110 = (f32[192]{0:T(256)}, f32[192]{0:T(256)S(1)}, u32[]{:S(2)}) copy-start(f32[192]{0:T(256)S(1)} %get-tuple-element.807) | copy-start | bytes 2308
  1295.2 14.0 %copy-start.17 = (f32[384,1536]{1,0:T(8,128)S(1)}, f32[384,1536]{1,0:T(8,128)}, u32[]{:S(2)}) copy-start(f32[384,1536]{1,0:T(8,128)} %param.33) | copy-start | bytes 7077892
  1295.2 14.0 %copy-start.18 = (f32[384,1536]{1,0:T(8,128)S(1)}, f32[384,1536]{1,0:T(8,128)}, u32[]{:S(2)}) copy-start(f32[384,1536]{1,0:T(8,128)} %get-tuple-element.812) | copy-start | bytes 7077892
  1295.2 14.0 %copy-start.32 = (f32[384,1536]{1,0:T(8,128)S(1)}, f32[384,1536]{1,0:T(8,128)}, u32[]{:S(2)}) copy-start(f32[384,1536]{1,0:T(8,128)} %param.39) | copy-start | bytes 7077892
  1295.3 14.4 %copy-start.33 = (f32[384,1536]{1,0:T(8,128)S(1)}, f32[384,1536]{1,0:T(8,128)}, u32[]{:S(2)}) copy-start(f32[384,1536]{1,0:T(8,128)} %param.45) | copy-start | bytes 7077892
  (64 other events, 386.7 us)
Sparse Core Ops, SparseCore 0:
  11.7 106.6 all-gather.5
  120.9 58.8 all-gather.7
  572.7 19.7 reduce-scatter.6
  596.0 124.3 reduce-scatter.10
  756.6 233.8 reduce-scatter.8
  994.2 39.1 reduce-scatter.12
  1036.0 259.2 all-reduce.34
where the time goes:
time: 1340 us; the launch traced here: 1320 us
  waiting for transfers between devices  576 us (43%)
  matrix products  182 us (14%)
  local copies, waits for them, and re-layouts  181 us (14%)
  other arithmetic  171 us (13%)
  blocking collectives  171 us (13%)
  starting transfers between devices  26.2 us (2%)
  between operations  18.2 us (1%)
    reduce_scatter x1, waiting for transfers between devices, on_device(): lax.psum_scatter(grad_tuple[1], 'dp', scatter_dimension=0, tiled=True)  231 us
    psum x1, waiting for transfers between devices, on_device(): lax.psum((owned_grads[0], owned_grads[1], owned_grads[2], owned_grads[3],...  185 us
    all_gather x1, waiting for transfers between devices, on_device(): lax.all_gather(inproject.astype(jnp.bfloat16), 'dp', axis=0, tiled=True)  79.8 us
    unnamed x11, other arithmetic  61.3 us
    unnamed x258, local copies, waits for them, and re-layouts  56.1 us
    dot_general x3, matrix products, mix_heads(): within = jnp.einsum('blsh,bshp->blhp', kernel, scaled, precision=highest)  49.4 us
    all_gather x1, blocking collectives, on_device(): shared_whole = lax.all_gather(shared_low, 'seq', axis=1, tiled=True)  46.2 us
    unnamed x2, blocking collectives  40.9 us
  transfers between devices with their start and end apart: 13, of which 6 were waited for; matrix products, arithmetic and copies ran while one was open for 28% of the time, Pallas kernels for 0%

commit v1 on v0

v1 whole, which is shorter than its diff:
```python
import functools

import jax
import jax.numpy as jnp
from jax import lax
from jax.experimental import pallas as pl
from jax.experimental.pallas import tpu as pltpu
from jax.sharding import PartitionSpec as P

N = 128
LANES = 128
HALO = 16

norm_eps = 1e-05
beta_moment = 0.9
beta_square = 0.95
adam_eps = 1e-08
adam_step = 3.0
rate_matrix = 0.005
rate_vector = 0.05
weight_decay = 0.1

f32 = jnp.float32
bf16 = jnp.bfloat16
MESH = pl.DeviceIdType.MESH


def adam_update(weight, moment, square, gradient, step_rate, decay_rate):
    moment_new = beta_moment * moment + (1.0 - beta_moment) * gradient
    square_new = beta_square * square + (1.0 - beta_square) * gradient * gradient
    moment_hat = moment_new / (1.0 - beta_moment**adam_step)
    square_hat = square_new / (1.0 - beta_square**adam_step)
    updated = weight - step_rate * (
        moment_hat / (jnp.sqrt(square_hat) + adam_eps) + decay_rate * weight
    )
    return (updated, moment_new, square_new)


def mm(a, b, ca, cb):
    return lax.dot_general(a, b, (((ca,), (cb,)), ((), ())), preferred_element_type=f32)


def halves(a):
    hi = a.astype(bf16)
    return hi, (a - hi.astype(f32)).astype(bf16)


def thirds(a):
    hi = a.astype(bf16)
    rest = a - hi.astype(f32)
    mid = rest.astype(bf16)
    return hi, mid, (rest - mid.astype(f32)).astype(bf16)


def mm3(a, b, ca, cb):
    return mm(a[0], b[0], ca, cb) + mm(a[0], b[1], ca, cb) + mm(a[1], b[0], ca, cb)


def iota(shape, dim):
    return lax.broadcasted_iota(jnp.int32, shape, dim)


def head_lanes(tile, heads_a_tile, copies):
    rows = iota((copies * LANES, LANES), 0)
    lane_head = tile * heads_a_tile + iota((copies * LANES, LANES), 1) // (LANES // heads_a_tile)
    return (rows % LANES == lane_head).astype(f32).astype(bf16)


def conv_tile(conv_ref, halo_ref, u_ref, taps_ref, start, rows):
    cols = pl.ds(start, LANES)
    conv_ref[0:HALO, :] = halo_ref[:, cols].astype(f32)
    conv_ref[HALO : HALO + rows, :] = u_ref[:, cols].astype(f32)
    taps = taps_ref[:, cols]
    pre = taps[4:5, :] + taps[0:1, :] * conv_ref[HALO - 3 : HALO - 3 + rows, :]
    for k in range(1, 4):
        pre = pre + taps[k : k + 1, :] * conv_ref[HALO - 3 + k : HALO - 3 + k + rows, :]
    return pre, jax.nn.sigmoid(pre)


def seq_copy(src, dst, send, recv, to):
    return pltpu.make_async_remote_copy(
        src_ref=src,
        dst_ref=dst,
        send_sem=send,
        recv_sem=recv,
        device_id={"seq": to},
        device_id_type=MESH,
    )


def greet_seq(barrier, rank, last):
    @pl.when(rank > 0)
    def _():
        pl.semaphore_signal(barrier, inc=1, device_id={"seq": rank - 1}, device_id_type=MESH)

    @pl.when(rank < last)
    def _():
        pl.semaphore_signal(barrier, inc=1, device_id={"seq": rank + 1}, device_id_type=MESH)


def seq_neighbours(rank, last):
    return jnp.minimum(rank, 1) + jnp.minimum(last - rank, 1)


def forward_kernel(
    sizes,
    u_ref,
    rate_ref,
    heads_ref,
    skip_ref,
    taps_ref,
    mixer_ref,
    ypre_ref,
    enter_ref,
    halo_ref,
    step_ref,
    cum_ref,
    cumt_ref,
    conv_ref,
    score_ref,
    leave_ref,
    send_sem,
    recv_sem,
    halo_sem,
):
    rows, inner, tiles, per_tile = sizes
    conv_width = inner + 2 * N
    rank = lax.axis_index("seq")
    last = lax.axis_size("seq") - 1
    barrier = pltpu.get_barrier_semaphore()
    greet_seq(barrier, rank, last)
    pl.semaphore_wait(barrier, seq_neighbours(rank, last))
    right = jnp.minimum(rank + 1, last)
    halo_copy = seq_copy(
        u_ref.at[pl.ds(rows - HALO, HALO), pl.ds(0, conv_width)],
        halo_ref,
        halo_sem.at[0],
        halo_sem.at[1],
        right,
    )

    @pl.when(rank < last)
    def _():
        halo_copy.start()

    step = jax.nn.softplus(rate_ref[...] + heads_ref[0:1, :])
    decay = -step * jnp.exp(heads_ref[1:2, :])
    lower = (iota((rows, rows), 0) >= iota((rows, rows), 1)).astype(f32).astype(bf16)
    cum = sum(mm(lower, part, 1, 0) for part in thirds(decay))
    step_ref[...] = step
    cum_ref[...] = cum
    cumt_ref[...] = cum.T

    @pl.when(rank > 0)
    def _():
        halo_copy.wait_recv()

    @pl.when(rank == 0)
    def _():
        halo_ref[...] = jnp.zeros_like(halo_ref)

    pre_b, sig_b = conv_tile(conv_ref, halo_ref, u_ref, taps_ref, inner, rows)
    b_parts = halves(pre_b * sig_b)
    pre_c, sig_c = conv_tile(conv_ref, halo_ref, u_ref, taps_ref, inner + N, rows)
    c_parts = halves(pre_c * sig_c)
    scores = mm3(c_parts, b_parts, 1, 1)
    causal = iota((rows, rows), 0) >= iota((rows, rows), 1)
    score_ref[...] = jnp.where(causal, scores, 0.0)
    cum_parts = jnp.concatenate(thirds(cum), axis=1)
    step_parts = jnp.concatenate(thirds(step), axis=1)
    lane = iota((rows, LANES), 1)
    width = LANES // per_tile

    def chain(tile):
        return seq_copy(
            leave_ref.at[tile], enter_ref.at[tile], send_sem.at[tile], recv_sem.at[tile], right
        )

    def one(tile, carry):
        start = pl.multiple_of(tile * LANES, LANES)
        cols = pl.ds(start, LANES)
        pick = head_lanes(tile, per_tile, 3)
        cum_l = mm(cum_parts, pick, 1, 0)
        step_l = mm(step_parts, pick, 1, 0)
        pre, sig = conv_tile(conv_ref, halo_ref, u_ref, taps_ref, start, rows)
        values = pre * sig
        x = values * step_l
        total = cum_l[rows - 1 : rows, :]
        fresh = mm3(b_parts, halves(x * jnp.exp(total - cum_l)), 0, 0)

        @pl.when(rank > 0)
        def _():
            chain(tile).wait_recv()

        @pl.when(rank == 0)
        def _():
            enter_ref[tile] = jnp.zeros((N, LANES), f32)

        enter = enter_ref[tile]
        leave_ref[tile] = jnp.exp(total) * enter + fresh

        @pl.when(rank < last)
        def _():
            chain(tile).start()

        result = mm3(c_parts, halves(enter), 1, 0) * jnp.exp(cum_l)
        for h in range(per_tile):
            row = cumt_ref[pl.ds(tile * per_tile + h, 1), :]
            col = cum_l[:, h * width : h * width + 1]
            kernel = jnp.exp(jnp.minimum(col - row, 0.0)) * score_ref[...]
            own = (lane // width) == h
            result = result + mm3(halves(kernel), halves(jnp.where(own, x, 0.0)), 1, 0)
        ypre_ref[:, cols] = result
        mixer_ref[:, cols] = (result + skip_ref[0:1, cols] * values).astype(bf16)
        return carry

    lax.fori_loop(0, tiles, one, 0)

    @pl.when(rank < last)
    def _():
        halo_copy.wait_send()

        def drain(tile, carry):
            chain(tile).wait_send()
            return carry

        lax.fori_loop(0, tiles, drain, 0)


def backward_kernel(
    sizes,
    u_ref,
    halo_ref,
    rate_ref,
    step_ref,
    cum_ref,
    cumt_ref,
    heads_ref,
    skip_ref,
    taps_ref,
    dy_ref,
    ypre_ref,
    enter_ref,
    turn_ref,
    dproj_ref,
    conv_grad_ref,
    head_grad_ref,
    turned_ref,
    conv_ref,
    score_ref,
    dscore_ref,
    dread_ref,
    dwrite_ref,
    dcum_ref,
    dstep_ref,
    dpre_ref,
    leave_ref,
    arrive_ref,
    send_sem,
    recv_sem,
    halo_sem,
    turn_send,
    turn_recv,
    own_sem,
):
    rows, inner, tiles, per_tile = sizes
    conv_width = inner + 2 * N
    rank = lax.axis_index("seq")
    last = lax.axis_size("seq") - 1
    me = lax.axis_index("dp")
    group = lax.axis_size("dp")
    barrier = pltpu.get_barrier_semaphore()
    greet_seq(barrier, rank, last)
    for i in range(1, group):
        pl.semaphore_signal(
            barrier, inc=1, device_id={"dp": lax.rem(me + i, group)}, device_id_type=MESH
        )
    pl.semaphore_wait(barrier, seq_neighbours(rank, last) + group - 1)

    def turn(i):
        peer = lax.rem(me + i, group)
        return pltpu.make_async_remote_copy(
            src_ref=turn_ref.at[peer],
            dst_ref=turned_ref.at[:, pl.ds(pl.multiple_of(me * rows, rows), rows)],
            send_sem=turn_send.at[i],
            recv_sem=turn_recv.at[i],
            device_id={"dp": peer},
            device_id_type=MESH,
        )

    for i in range(1, group):
        turn(i).start()
    own_copy = pltpu.make_async_copy(
        turn_ref.at[me],
        turned_ref.at[:, pl.ds(pl.multiple_of(me * rows, rows), rows)],
        own_sem,
    )
    own_copy.start()

    left = jnp.maximum(rank - 1, 0)
    cum = cum_ref[...]
    step = step_ref[...]
    pre_b, sig_b = conv_tile(conv_ref, halo_ref, u_ref, taps_ref, inner, rows)
    b_parts = halves(pre_b * sig_b)
    pre_c, sig_c = conv_tile(conv_ref, halo_ref, u_ref, taps_ref, inner + N, rows)
    c_parts = halves(pre_c * sig_c)
    later = iota((rows, rows), 1) >= iota((rows, rows), 0)
    score_ref[...] = jnp.where(later, mm3(b_parts, c_parts, 1, 1), 0.0)
    dscore_ref[...] = jnp.zeros_like(dscore_ref)
    dread_ref[...] = jnp.zeros_like(dread_ref)
    dwrite_ref[...] = jnp.zeros_like(dwrite_ref)
    dcum_ref[...] = jnp.zeros_like(dcum_ref)
    dstep_ref[...] = jnp.zeros_like(dstep_ref)
    cum_parts = jnp.concatenate(thirds(cum), axis=1)
    step_parts = jnp.concatenate(thirds(step), axis=1)
    lane = iota((rows, LANES), 1)
    final_row = iota((rows, LANES), 0) == rows - 1
    width = LANES // per_tile

    def chain(tile):
        return seq_copy(
            leave_ref.at[tile], arrive_ref.at[tile], send_sem.at[tile], recv_sem.at[tile], left
        )

    def tap_grads(dpre, extra):
        sums = [
            jnp.sum(
                dpre * conv_ref[HALO - 3 + k : HALO - 3 + k + rows, :], axis=0, keepdims=True
            )
            for k in range(4)
        ]
        sums.append(jnp.sum(dpre, axis=0, keepdims=True))
        sums.append(extra)
        sums.append(jnp.zeros((2, LANES), f32))
        return jnp.concatenate(sums, axis=0)

    def one(tile, carry):
        start = pl.multiple_of(tile * LANES, LANES)
        cols = pl.ds(start, LANES)
        pick = head_lanes(tile, per_tile, 3)
        cum_l = mm(cum_parts, pick, 1, 0)
        step_l = mm(step_parts, pick, 1, 0)
        total = cum_l[rows - 1 : rows, :]
        dy = dy_ref[:, cols].astype(f32)
        reads = halves(dy * jnp.exp(cum_l))
        denter = mm3(c_parts, reads, 0, 0)

        @pl.when(rank < last)
        def _():
            chain(tile).wait_recv()

        @pl.when(rank == last)
        def _():
            arrive_ref[tile] = jnp.zeros((N, LANES), f32)

        arrive = arrive_ref[tile]
        leave_ref[tile] = jnp.exp(total) * arrive + denter

        @pl.when(rank > 0)
        def _():
            chain(tile).start()

        pre, sig = conv_tile(conv_ref, halo_ref, u_ref, taps_ref, start, rows)
        values = pre * sig
        x = values * step_l
        x_parts = halves(x)
        tail = jnp.exp(total - cum_l)
        enter = enter_ref[tile]
        arrive_parts = halves(arrive)
        dx_state = mm3(b_parts, arrive_parts, 1, 0) * tail
        dx = dx_state
        for h in range(per_tile):
            row = cumt_ref[pl.ds(tile * per_tile + h, 1), :]
            col = cum_l[:, h * width : h * width + 1]
            spread = jnp.exp(jnp.minimum(row - col, 0.0))
            kernel = halves(spread * score_ref[...])
            own = jnp.where((lane // width) == h, dy, 0.0).astype(bf16)
            dx = dx + (mm(kernel[0], own, 1, 0) + mm(kernel[1], own, 1, 0))
            pairs = mm(x_parts[0], own, 1, 1) + mm(x_parts[1], own, 1, 1)
            dscore_ref[...] += spread * pairs
        dread_ref[...] += mm3(reads, halves(enter), 1, 1)
        dwrite_ref[...] += mm3(halves(x * tail), arrive_parts, 1, 1)
        ends = jnp.sum(x * dx_state, axis=0, keepdims=True) + jnp.exp(total) * jnp.sum(
            enter * arrive, axis=0, keepdims=True
        )
        dcum = dy * ypre_ref[:, cols] - x * dx + jnp.where(final_row, ends, 0.0)
        own_head = pick[0:LANES, :]
        for part in halves(dcum):
            dcum_ref[...] += mm(part, own_head, 1, 1)
        for part in halves(dx * values):
            dstep_ref[...] += mm(part, own_head, 1, 1)
        dvalues = step_l * dx + skip_ref[0:1, cols] * dy
        dpre = dvalues * sig * (1.0 + pre * (1.0 - sig))
        dpre_ref[0:rows, cols] = dpre
        conv_grad_ref[:, cols] = tap_grads(dpre, jnp.sum(dy * values, axis=0, keepdims=True))
        return carry

    lax.fori_loop(0, tiles, one, 0)

    dscore = halves(jnp.where(later, dscore_ref[...], 0.0))
    dshared = (
        dwrite_ref[...] + mm3(dscore, c_parts, 1, 0),
        dread_ref[...] + mm3(dscore, b_parts, 0, 0),
    )
    for i in range(2):
        start = inner + i * N
        pre, sig = conv_tile(conv_ref, halo_ref, u_ref, taps_ref, start, rows)
        dpre = dshared[i] * sig * (1.0 + pre * (1.0 - sig))
        dpre_ref[0:rows, start : start + N] = dpre
        conv_grad_ref[:, start : start + N] = tap_grads(dpre, jnp.zeros((1, LANES), f32))

    edge = seq_copy(
        dpre_ref.at[pl.ds(0, 8), :],
        dpre_ref.at[pl.ds(rows, 8), :],
        halo_sem.at[0],
        halo_sem.at[1],
        left,
    )

    @pl.when(rank > 0)
    def _():
        edge.start()

    upper = (iota((rows, rows), 1) >= iota((rows, rows), 0)).astype(f32).astype(bf16)
    ddecay = sum(mm(upper, part, 1, 0) for part in thirds(dcum_ref[...]))
    exp_rate = jnp.exp(heads_ref[1:2, :])
    drate = (dstep_ref[...] - ddecay * exp_rate) * jax.nn.sigmoid(rate_ref[...] + heads_ref[0:1, :])
    head_grad_ref[...] = jnp.concatenate(
        [
            jnp.sum(drate, axis=0, keepdims=True),
            jnp.sum(ddecay * (-step * exp_rate), axis=0, keepdims=True),
            jnp.zeros((6, LANES), f32),
        ],
        axis=0,
    )
    heads = tiles * per_tile
    dproj_ref[:, conv_width : conv_width + heads] = drate[:, 0:heads].astype(bf16)

    @pl.when(rank == last)
    def _():
        dpre_ref[rows : rows + 8, :] = jnp.zeros((8, conv_width), f32)

    @pl.when(rank < last)
    def _():
        edge.wait_recv()

    def unconv(tile, carry):
        cols = pl.ds(pl.multiple_of(tile * LANES, LANES), LANES)
        taps = taps_ref[:, cols]
        du = taps[3:4, :] * dpre_ref[0:rows, cols]
        for k in range(3):
            du = du + taps[k : k + 1, :] * dpre_ref[3 - k : 3 - k + rows, cols]
        dproj_ref[:, cols] = du.astype(bf16)
        return carry

    lax.fori_loop(0, conv_width // LANES, unconv, 0)

    @pl.when(rank > 0)
    def _():
        edge.wait_send()

        def drain(tile, carry):
            chain(tile).wait_send()
            return carry

        lax.fori_loop(0, tiles, drain, 0)

    own_copy.wait()
    for i in range(1, group):
        turn(i).wait_send()
        origin = lax.rem(me + group - i, group)
        pltpu.make_async_remote_copy(
            src_ref=turn_ref.at[origin],
            dst_ref=turned_ref.at[:, pl.ds(pl.multiple_of(origin * rows, rows), rows)],
            send_sem=turn_send.at[i],
            recv_sem=turn_recv.at[i],
            device_id={"dp": origin},
            device_id_type=MESH,
        ).wait_recv()


def vmem(count):
    return [pl.BlockSpec(memory_space=pltpu.VMEM)] * count


def scan_forward(u, rate, heads, skip, taps, sizes):
    rows, inner, tiles, _ = sizes
    conv_width = inner + 2 * N
    shape = jax.ShapeDtypeStruct
    return pl.pallas_call(
        functools.partial(forward_kernel, sizes),
        out_shape=(
            shape((rows, inner), bf16),
            shape((rows, inner), f32),
            shape((tiles, N, LANES), f32),
            shape((HALO, conv_width), bf16),
            shape((rows, LANES), f32),
            shape((rows, LANES), f32),
            shape((LANES, rows), f32),
        ),
        in_specs=vmem(5),
        out_specs=tuple(vmem(7)),
        scratch_shapes=[
            pltpu.VMEM((HALO + rows, LANES), f32),
            pltpu.VMEM((rows, rows), f32),
            pltpu.VMEM((tiles, N, LANES), f32),
            pltpu.SemaphoreType.DMA((tiles,)),
            pltpu.SemaphoreType.DMA((tiles,)),
            pltpu.SemaphoreType.DMA((2,)),
        ],
        compiler_params=pltpu.CompilerParams(
            collective_id=1, has_side_effects=True, vmem_limit_bytes=40 * 2**20
        ),
        cost_estimate=pl.CostEstimate(flops=4 * 10**9, bytes_accessed=10**7, transcendentals=4 * 10**6),
    )(u, rate, heads, skip, taps)


def scan_backward(u, halo, rate, step, cum, cumt, heads, skip, taps, dy, ypre, enter, turn, sizes):
    rows, inner, tiles, _ = sizes
    conv_width = inner + 2 * N
    shape = jax.ShapeDtypeStruct
    group, turn_rows, _ = turn.shape
    return pl.pallas_call(
        functools.partial(backward_kernel, sizes),
        out_shape=(
            shape(u.shape, bf16),
            shape((8, conv_width), f32),
            shape((8, LANES), f32),
            shape((turn_rows, group * rows), bf16),
        ),
        in_specs=vmem(12) + [pl.BlockSpec(memory_space=pl.ANY)],
        out_specs=tuple(vmem(3) + [pl.BlockSpec(memory_space=pl.ANY)]),
        scratch_shapes=[
            pltpu.VMEM((HALO + rows, LANES), f32),
            pltpu.VMEM((rows, rows), f32),
            pltpu.VMEM((rows, rows), f32),
            pltpu.VMEM((rows, N), f32),
            pltpu.VMEM((rows, N), f32),
            pltpu.VMEM((rows, LANES), f32),
            pltpu.VMEM((rows, LANES), f32),
            pltpu.VMEM((rows + 8, conv_width), f32),
            pltpu.VMEM((tiles, N, LANES), f32),
            pltpu.VMEM((tiles, N, LANES), f32),
            pltpu.SemaphoreType.DMA((tiles,)),
            pltpu.SemaphoreType.DMA((tiles,)),
            pltpu.SemaphoreType.DMA((2,)),
            pltpu.SemaphoreType.DMA((group,)),
            pltpu.SemaphoreType.DMA((group,)),
            pltpu.SemaphoreType.DMA,
        ],
        compiler_params=pltpu.CompilerParams(
            collective_id=2, has_side_effects=True, vmem_limit_bytes=40 * 2**20
        ),
        cost_estimate=pl.CostEstimate(flops=6 * 10**9, bytes_accessed=2 * 10**7, transcendentals=4 * 10**6),
    )(u, halo, rate, step, cum, cumt, heads, skip, taps, dy, ypre, enter, turn)


def on_device(
    hidden_in,
    out_grad,
    prenorm,
    inproject,
    convtaps,
    headcoefs,
    postnorm,
    outproject,
    prenorm_first,
    inproject_first,
    convtaps_first,
    headcoefs_first,
    postnorm_first,
    outproject_first,
    prenorm_second,
    inproject_second,
    convtaps_second,
    headcoefs_second,
    postnorm_second,
    outproject_second,
):
    group = lax.axis_size("dp")
    me = lax.axis_index("dp")
    seq_here, rows, model_width = hidden_in.shape
    assert seq_here == 1
    heads = headcoefs.shape[1]
    own_in, proj_width = inproject.shape
    own_out = outproject.shape[0]
    inner = own_out * group
    width = inner // heads
    per_tile = LANES // width
    tiles = inner // LANES
    sizes = (rows, inner, tiles, per_tile)
    conv_own = convtaps.shape[1]
    conv_width = conv_own * group

    in_low = inproject.astype(bf16)
    scan_matrix = lax.all_gather(in_low[:, inner:], "dp", axis=0, tiled=True)
    small = jnp.concatenate([prenorm, postnorm, convtaps.reshape(-1)]).astype(bf16)
    small = lax.all_gather(small, "dp", axis=0).astype(f32)
    pre_scale = small[:, :own_in].reshape(-1)
    post_scale = small[:, own_in : own_in + own_out].reshape(-1)
    taps = small[:, own_in + own_out :].reshape(group, -1, conv_own)
    taps = jnp.swapaxes(taps, 0, 1).reshape(-1, conv_width)
    tap_rows = taps.shape[0]
    gate_matrix = lax.all_gather(in_low[:, :inner], "dp", axis=0, tiled=True)
    out_matrix = lax.all_gather(outproject.astype(bf16), "dp", axis=0, tiled=True)

    hidden = hidden_in.reshape(rows, model_width).astype(f32)
    cot_low = out_grad.reshape(rows, model_width)
    cot_all = lax.all_gather(cot_low, "dp", axis=0, tiled=True)
    root = lax.rsqrt(jnp.mean(hidden * hidden, axis=-1, keepdims=True) + norm_eps)
    normed_low = (hidden * root * pre_scale).astype(bf16)

    scan_in = jnp.dot(normed_low, scan_matrix, preferred_element_type=f32).astype(bf16)
    pad_heads = ((0, 0), (0, LANES - heads))
    rate = jnp.pad(scan_in[:, conv_width:].astype(f32), pad_heads)
    head_rows = jnp.pad(headcoefs, ((0, 8 - headcoefs.shape[0]), (0, LANES - heads)))
    skip = jnp.repeat(headcoefs[2:3], width, axis=1)
    taps_pad = jnp.pad(taps, ((0, 8 - tap_rows), (0, 0)))
    mixer_low, ypre, enter, halo, step, cum, cumt = scan_forward(
        scan_in, rate, head_rows, skip, taps_pad, sizes
    )

    gate = jnp.dot(normed_low, gate_matrix, preferred_element_type=f32)
    mixer = mixer_low.astype(f32)
    gate_sig = jax.nn.sigmoid(gate)
    gate_act = gate * gate_sig
    gated = mixer * gate_act
    post_root = lax.rsqrt(jnp.mean(gated * gated, axis=-1, keepdims=True) + norm_eps)
    whitened = gated * post_root
    post_low = (whitened * post_scale).astype(bf16)
    output = hidden + jnp.dot(post_low, out_matrix, preferred_element_type=f32)

    post_grad = mm(cot_low, out_matrix, 1, 1)
    postnorm_grad = jnp.sum(post_grad * whitened, axis=0)
    dwhite = post_grad * post_scale
    dgated = post_root * (dwhite - whitened * jnp.mean(dwhite * whitened, axis=-1, keepdims=True))
    dy = (dgated * gate_act).astype(bf16)
    gate_grad = (dgated * mixer * gate_sig * (1.0 + gate * (1.0 - gate_sig))).astype(bf16)

    turn = jnp.concatenate(
        [
            normed_low.T.reshape(group, own_in, rows),
            post_low.T.reshape(group, own_out, rows),
        ],
        axis=1,
    )
    scan_grad, conv_grad, head_grad, turned = scan_backward(
        scan_in, halo, rate, step, cum, cumt, head_rows, skip, taps_pad, dy, ypre, enter, turn, sizes
    )
    gate_all = lax.all_gather(gate_grad, "dp", axis=0, tiled=True)
    scan_all = lax.all_gather(scan_grad, "dp", axis=0, tiled=True)
    normed_turned = turned[:own_in]
    outproj_owned = lax.psum(
        jnp.dot(turned[own_in:], cot_all, preferred_element_type=f32), "seq"
    )
    gate_owned = lax.psum(jnp.dot(normed_turned, gate_all, preferred_element_type=f32), "seq")
    scan_owned = lax.psum(jnp.dot(normed_turned, scan_all, preferred_element_type=f32), "seq")
    inproj_owned = jnp.concatenate([gate_owned, scan_owned], axis=1)

    normed_grad = mm(gate_grad, gate_matrix, 1, 1) + mm(scan_grad, scan_matrix, 1, 1)
    plain = hidden * root
    prenorm_grad = jnp.sum(normed_grad * plain, axis=0)
    dplain = normed_grad * pre_scale
    input_gradient = root * (
        dplain - plain * jnp.mean(dplain * plain, axis=-1, keepdims=True)
    ) + cot_low.astype(f32)

    head_sums = jnp.concatenate(
        [
            head_grad[:2, :heads],
            jnp.sum(conv_grad[tap_rows : tap_rows + 1, :inner].reshape(1, heads, width), axis=-1),
        ],
        axis=0,
    )
    packed = jnp.concatenate(
        [
            prenorm_grad,
            postnorm_grad,
            conv_grad[:tap_rows].reshape(-1),
            head_sums.reshape(-1),
        ]
    )
    packed = lax.psum(packed, ("dp", "seq"))
    prenorm_owned = lax.dynamic_slice_in_dim(packed, me * own_in, own_in, 0)
    postnorm_owned = lax.dynamic_slice_in_dim(packed, model_width + me * own_out, own_out, 0)
    conv_at = model_width + inner
    conv_end = conv_at + tap_rows * conv_width
    conv_owned = lax.dynamic_slice_in_dim(
        packed[conv_at:conv_end].reshape(tap_rows, conv_width), me * conv_own, conv_own, 1
    )
    head_total = packed[conv_end:].reshape(3, heads)

    prenorm_new, prenorm_mom, prenorm_sq = adam_update(
        prenorm, prenorm_first, prenorm_second, prenorm_owned, rate_vector, 0.0
    )
    inproj_new, inproj_mom, inproj_sq = adam_update(
        inproject, inproject_first, inproject_second, inproj_owned, rate_matrix, weight_decay
    )
    conv_new, conv_mom, conv_sq = adam_update(
        convtaps, convtaps_first, convtaps_second, conv_owned, rate_vector, 0.0
    )
    head_new, head_mom, head_sq = adam_update(
        headcoefs, headcoefs_first, headcoefs_second, head_total, rate_vector, 0.0
    )
    postnorm_new, postnorm_mom, postnorm_sq = adam_update(
        postnorm, postnorm_first, postnorm_second, postnorm_owned, rate_vector, 0.0
    )
    outproj_new, outproj_mom, outproj_sq = adam_update(
        outproject, outproject_first, outproject_second, outproj_owned, rate_matrix, weight_decay
    )
    return (
        output.reshape(seq_here, rows, model_width),
        input_gradient.reshape(seq_here, rows, model_width),
        prenorm_owned,
        inproj_owned,
        conv_owned,
        head_total,
        postnorm_owned,
        outproj_owned,
        prenorm_new,
        inproj_new,
        conv_new,
        head_new,
        postnorm_new,
        outproj_new,
        prenorm_mom,
        inproj_mom,
        conv_mom,
        head_mom,
        postnorm_mom,
        outproj_mom,
        prenorm_sq,
        inproj_sq,
        conv_sq,
        head_sq,
        postnorm_sq,
        outproj_sq,
    )


def solution(mesh):
    weights = (P("dp"), P("dp", None), P(None, "dp"), P(), P("dp"), P("dp", None))
    tokens = (P("dp", "seq", None), P("dp", "seq", None))
    return jax.shard_map(
        on_device,
        mesh=mesh,
        in_specs=tokens + weights * 3,
        out_specs=tokens + weights * 4,
        check_vma=False,
    )
```

time: 1340 us -> 845 us (0.63); the launches traced: 1320 us -> 844 us
  blocking collectives: 171 us -> 10.7 us
  local copies, waits for them, and re-layouts: 181 us -> 23.3 us
  other arithmetic: 171 us -> 39.1 us
  matrix products: 182 us -> 72.8 us
  Pallas kernels: 0 us -> 93 us
  starting transfers between devices: 26.2 us -> 0.55 us
  waiting for transfers between devices: 576 us -> 590 us
    reduce_scatter x3 -> x0, waiting for transfers between devices: 231 us -> none  [the longest x1 231 us: on_device(): lax.psum_scatter(grad_tuple[1], 'dp', scatter_dimension=0, tiled=True)]
    psum x1 -> x2, waiting for transfers between devices: 185 us -> 363 us  [the longest x1 258 us: on_device(): lax.psum(jnp.dot(normed_turned, gate_all, preferred_element_type=f32), 's...]
    all_gather x2 -> x6, waiting for transfers between devices: 79.8 us -> 227 us  [the longest x1 72 us: on_device(): scan_all = lax.all_gather(scan_grad, 'dp', axis=0, tiled=True)]
    dot_general x18 -> x9, matrix products: 177 us -> 72.8 us  [the longest x3 24.3 us: mm(): lax.dot_general(a, b, (((ca,), (cb,)), ((), ())), preferred_element_type=...]
    pallas_call x0 -> x2, Pallas kernels: none -> 93 us  [the longest x1 54.7 us: scan_backward(): pl.pallas_call(functools.partial(backward_kernel, sizes), out_shape=(shap...]
    all_to_all x6 -> x0, waiting for transfers between devices: 79.3 us -> none  [the longest x1 33.8 us: on_device(): lax.all_to_all(inner_back, 'seq', split_axis=1, concat_axis=2, tiled=True)]
    psum x2 -> x0, blocking collectives: 66.4 us -> none  [the longest x1 39.4 us: on_device(): head_total = lax.psum(head_full, ('dp', 'seq'))]
    unnamed x11 -> x0, other arithmetic: 61.3 us -> none
  transfers between devices with their start and end apart: 13 -> 8, of which waited for: 6 -> 7; matrix products, arithmetic and copies ran while one was open for 28% -> 12% of each run, Pallas kernels for 0% -> 11%
where the time goes in v1:
time: 845 us; the launch traced here: 844 us
  waiting for transfers between devices  590 us (70%)
  Pallas kernels  93 us (11%)
  matrix products  72.8 us (9%)
  other arithmetic  39.1 us (5%)
  local copies, waits for them, and re-layouts  23.3 us (3%)
  between operations  14.8 us (2%)
  blocking collectives  10.7 us (1%)
    psum x1, waiting for transfers between devices, on_device(): lax.psum(jnp.dot(normed_turned, gate_all, preferred_element_type=f32), 's...  258 us
    psum x1, waiting for transfers between devices, on_device(): packed = lax.psum(packed, ('dp', 'seq'))  104 us
    all_gather x1, waiting for transfers between devices, on_device(): scan_all = lax.all_gather(scan_grad, 'dp', axis=0, tiled=True)  72 us
    pallas_call x1, Pallas kernels, scan_backward(): pl.pallas_call(functools.partial(backward_kernel, sizes), out_shape=(shap...  54.7 us
    all_gather x1, waiting for transfers between devices, on_device(): lax.all_gather(outproject.astype(bf16), 'dp', axis=0, tiled=True)  52.3 us
    all_gather x1, waiting for transfers between devices, on_device(): scan_matrix = lax.all_gather(in_low[:, inner:], 'dp', axis=0, tiled=True)  49.3 us
    all_gather x1, waiting for transfers between devices, on_device(): gate_all = lax.all_gather(gate_grad, 'dp', axis=0, tiled=True)  43.2 us
    pallas_call x1, Pallas kernels, scan_forward(): pl.pallas_call(functools.partial(forward_kernel, sizes), out_shape=(shape...  38.3 us
  transfers between devices with their start and end apart: 8, of which 7 were waited for; matrix products, arithmetic and copies ran while one was open for 12% of the time, Pallas kernels for 11%

profile of v1, /device:TPU:0, one launch (start us, length us, event | category | flops | bytes accessed | tf_op | source)
XLA Modules:
  0.0 844.3 jit_solution(924463643721113819)
XLA Ops:
  7.2 2.7 convert_element_type.55
  9.9 1.2 slice.60
  11.2 1.2 slice.63
  12.4 2.9 convert_element_type.59
  15.4 0.5 all-gather.19.cloned.1.call-update
  16.1 0.1 concatenate.31
  16.2 0.1 concatenate.32
  16.3 10.7 %all-gather.1 = bf16[8,1,2656]{2,1,0:T(2,128)(2,1)S(1)} all-gather(bf16[1,1,2656]{2,1,0:T(2,128)(2,1)S(1)} %bitcast.60), channel_id=1, replica_groups=mesh['dp'=8,'seq'=4] {'dp'}, dimensions={0}, use_global_device_ids=true | all-gather | bytes 47808 | tf_op jit(solution)/shard_map/all_gather | solution.py:598
  27.3 0.1 broadcast_in_dim.10.skip_ref
  27.4 0.1 reshape.170
  27.6 0.1 reshape.171
  27.7 0.6 mul.337
  28.3 0.2 fusion.20
  28.6 49.3 %all-gather.9.cloned.1.call-done = bf16[1536,3376]{1,0:T(8,128)(2,1)} async-done(((bf16[192,3376]{1,0:T(8,128)(2,1)}), bf16[1536,3376]{1,0:T(8,128)(2,1)}) %all-gather.9.cloned.1.call-update) | async-done | bytes 10371088 | tf_op jit(solution)/shard_map/all_gather | solution.py:596
  77.9 7.1 convolution_convert_fusion.u_ref
  85.0 38.3 %shard_map.395 = (bf16[256,3072]{1,0:T(8,128)(2,1)S(1)}, f32[256,3072]{1,0:T(8,128)S(1)}, f32[24,128,128]{2,1,0:T(8,128)S(1)}, bf16[16,3328]{1,0:T(8,128)(2,1)S(...) custom-call(bf16[256,3376]{1,0:T(8,128)(2,1)S(1)} %convolution_convert_fusion.u_ref, ...), custom_call_target="tpu_custom_call" | custom-call | flops 4000000000 | bytes 10000000 | tf_op jit(solution)/shard_map/pallas_call | solution.py:490
  123.4 1.2 copy-done
  124.6 1.7 copy-done.4
  126.2 1.1 copy-done.5
  127.4 0.7 copy-done.7
  128.0 0.7 copy-done.9
  128.7 0.6 copy-done.11
  129.3 9.9 %all-gather.11.cloned.1.call-done = bf16[1536,3072]{1,0:T(8,128)(2,1)} async-done(((bf16[192,3072]{1,0:T(8,128)(2,1)}), bf16[1536,3072]{1,0:T(8,128)(2,1)}) %all-gather.11.cloned.1.call-update) | async-done | bytes 9437200 | tf_op jit(solution)/shard_map/all_gather | solution.py:604
  139.2 9.0 %multiply_reduce_fusion.2 = (f32[256]{0:T(256)S(1)}, f32[256,3072]{1,0:T(8,128)}) fusion(bf16[256,3072]{1,0:T(8,128)(2,1)S(1)} %get-tuple-element.37, bf16[1536,3072]{1,0:T(8,128)(2,1)} %all-gather.11.cloned.1.call-done, bf16[1,256,1536]{2,1,0:T(8,128)(2,1)} %param.20, f32[1536]{0:T(1024)S(1)} %mul.329, f32[256]{0:T(256)} %copy-done.32), kind=kOutput, calls=%fused_computation.18 | convolution fusion | flops 2423783168 | bytes 14950400 | tf_op jit(solution)/shard_map/dot_general | solution.py:623
  148.2 52.3 %all-gather.13.cloned.1.call-done = bf16[3072,1536]{1,0:T(8,128)(2,1)} async-done(((bf16[384,1536]{1,0:T(8,128)(2,1)}), bf16[3072,1536]{1,0:T(8,128)(2,1)}) %all-gather.13.cloned.1.call-update) | async-done | bytes 9437200 | tf_op jit(solution)/shard_map/all_gather | solution.py:605
  200.5 8.5 %multiply_reduce_fusion = (f32[3072]{0:T(1024)}, f32[256]{0:T(256)S(1)}, f32[256,3072]{1,0:T(8,128)S(1)}) fusion(f32[256]{0:T(256)S(1)} %add_rsqrt_fusion, bf16[256,3072]{1,0:T(8,128)(2,1)S(1)} %get-tuple-element.37, f32[256,3072]{1,0:T(8,128)} %get-tuple-element.80, f32[3072]{0:T(1024)S(1)} %copy-done.27, ...), kind=kOutput, calls=%fused_computation.13 | convolution fusion | flops 2425352960 | bytes 18114560 | tf_op jit(solution)/shard_map/dot_general | solution.py:40
  209.0 4.5 fusion.5
  213.6 1.4 fusion.32
  215.0 1.2 copy.55
  216.2 1.7 copy.56
  218.0 1.4 pad_maximum_fusion.turn_ref
  219.4 0.2 copy-done.1
  219.6 0.5 copy-done.6
  220.1 54.7 %shard_map.396 = (bf16[256,3376]{1,0:T(8,128)(2,1)}, f32[8,3328]{1,0:T(8,128)S(1)}, f32[8,128]{1,0:T(8,128)S(1)}, bf16[576,2048]{1,0:T(8,128)(2,1)S(1)}) custom-call(bf16[256,3376]{1,0:T(8,128)(2,1)S(1)} %copy-done.1, bf16[16,3328]{1,0:T(8,128)(2,1)S(1)} %copy-done.12, f32[256,128]{1,0:T(8,128)S(1)} %pad_convert_fusion.rate_ref, ...), custom_call_target="tpu_custom_call" | custom-call | flops 6000000000 | bytes 20000000 | tf_op jit(solution)/shard_map/pallas_call | solution.py:523
  274.8 1.4 copy-done.2
  276.3 0.3 all-reduce.7.cloned.1.call-start
  276.6 0.1 reduce_sum.71
  276.9 7.9 fusion.42
  284.9 7.9 fusion.19
  292.8 0.6 pad_maximum_fusion.1
  293.6 6.8 fusion
  300.4 43.2 %all-gather.15.cloned.1.call-done = bf16[2048,3072]{1,0:T(8,128)(2,1)} async-done(((bf16[256,3072]{1,0:T(8,128)(2,1)}), bf16[2048,3072]{1,0:T(8,128)(2,1)}) %all-gather.15.cloned.1.call-update) | async-done | bytes 12582928 | tf_op jit(solution)/shard_map/all_gather | solution.py:650
  343.5 8.6 %fusion.26 = f32[192,3072]{1,0:T(8,128)} fusion(bf16[2048,3072]{1,0:T(8,128)(2,1)} %all-gather.15.cloned.1.call-done, bf16[576,2048]{1,0:T(8,128)(2,1)S(1)} %copy-done.3), kind=kOutput, calls=%fused_computation.47 | convolution fusion | flops 2415919104 | bytes 15728640 | tf_op jit(solution)/shard_map/dot_general | solution.py:656
  352.1 72.0 %all-gather.17.cloned.1.call-done = bf16[2048,3376]{1,0:T(8,128)(2,1)} async-done(((bf16[256,3376]{1,0:T(8,128)(2,1)}), bf16[2048,3376]{1,0:T(8,128)(2,1)}) %all-gather.17.cloned.1.call-update) | async-done | bytes 13828112 | tf_op jit(solution)/shard_map/all_gather | solution.py:651
  424.1 9.5 %fusion.24 = f32[192,3376]{1,0:T(8,128)} fusion(bf16[2048,3376]{1,0:T(8,128)(2,1)} %all-gather.17.cloned.1.call-done, bf16[576,2048]{1,0:T(8,128)(2,1)S(1)} %copy-done.3), kind=kOutput, calls=%fused_computation.45 | convolution fusion | flops 2654994432 | bytes 17207296 | tf_op jit(solution)/shard_map/dot_general | solution.py:657
  433.7 1.1 copy-done.22
  434.8 3.0 fusion.18
  437.9 7.5 fusion.7
  445.4 104.3 %all-reduce.7.cloned.1.call-done = f32[21392]{0:T(1024)} async-done(((f32[21392]{0:T(1024)}), f32[21392]{0:T(1024)}) %all-reduce.7.cloned.1.call-update) | async-done | bytes 85584 | tf_op jit(solution)/shard_map/psum | solution.py:683
  549.7 0.9 slice.65
  550.6 0.7 slice.66
  551.4 1.4 multiply_subtract_fusion.5
  552.8 0.6 multiply_subtract_fusion.4
  553.4 1.4 multiply_subtract_fusion.3
  554.8 0.7 multiply_subtract_fusion.2
  555.5 258.4 %all-reduce.9.cloned.1.call-done = (f32[192,3072]{1,0:T(8,128)}, f32[192,3376]{1,0:T(8,128)}, f32[384,1536]{1,0:T(8,128)}) async-done(((f32[192,3072]{1,0:T(8,128)}, f32[192,3376]{1,0:T(8,128)}, f32[384,1536]{1,0:T(8,128)}), (f32[192,3072]{1,0:T(8,128)}, f32[192,3376]{1,0:T(8,128)}, f32[384,1536]{1,0:T(8,128)})) %all-reduce.9.cloned.1.call-update) | async-done | bytes 7311376 | tf_op jit(solution)/shard_map/psum | solution.py:656
  813.9 2.0 constant_dynamic-update-slice_fusion.1
  815.9 0.5 copy-done.23
  816.4 0.2 constant_dynamic-update-slice_fusion
  816.6 13.7 %multiply_subtract_fusion = (f32[192,6448]{1,0:T(8,128)}, f32[192,6448]{1,0:T(8,128)}, f32[192,6448]{1,0:T(8,128)}) fusion(f32[192,6448]{1,0:T(8,128)} %param.23, f32[192,6448]{1,0:T(8,128)S(1)} %constant_dynamic-update-slice_fusion, f32[192,6448]{1,0:T(8,128)} %param.29, f32[192,6448]{1,0:T(8,128)} %param.35), kind=kLoop, calls=%fused_computation.5 | loop fusion | flops 18570240 | bytes 34664448 | tf_op jit(solution)/shard_map/sub | solution.py:33
  830.3 0.2 copy-done.24
  830.5 1.2 copy-done.25
  831.7 4.3 multiply_subtract_fusion.1
  836.0 1.4 copy.66
  (127 shorter events, 1.4 us)
Async XLA Ops:
  7.2 70.7 %all-gather.9.cloned.1.call-start = ((), (), s32[]{:S(2)}) async-start(), calls=%async_computation | async-start | bytes 11943936 | tf_op jit(solution)/shard_map/all_gather | solution.py:596
  11.1 128.1 %all-gather.11.cloned.1.call-start = ((), (), s32[]{:S(2)}) async-start(), calls=%async_computation.1 | async-start | bytes 10616832 | tf_op jit(solution)/shard_map/all_gather | solution.py:604
  12.3 3.6 copy-start.44
  12.4 3.7 copy-start.36
  12.4 3.7 copy-start.26
  12.4 14.9 %copy-start.34 = (f32[3,48]{1,0:T(4,128)S(1)}, f32[3,48]{1,0:T(4,128)}, u32[]{:S(2)}) copy-start(f32[3,48]{1,0:T(4,128)} %param.25) | copy-start | bytes 1732
  12.4 15.9 %copy-start.16 = (bf16[1,256,1536]{2,1,0:T(8,128)(2,1)S(1)}, bf16[1,256,1536]{2,1,0:T(8,128)(2,1)}, u32[]{:S(2)}) copy-start(bf16[1,256,1536]{2,1,0:T(8,128)(2,1)} %param.20) | copy-start | bytes 2359300
  12.4 188.1 %all-gather.13.cloned.1.call-start = ((), (), s32[]{:S(2)}) async-start(), calls=%async_computation.2 | async-start | bytes 10616832 | tf_op jit(solution)/shard_map/all_gather | solution.py:605
  15.3 278.2 %all-gather.19.cloned.1.call-start = ((), (), s32[]{:S(2)}) async-start(), calls=%async_computation.6 | async-start | bytes 7077888 | tf_op jit(solution)/shard_map/all_gather | solution.py:609
  15.9 327.6 %all-gather.15.cloned.1.call-start = ((), (), s32[]{:S(2)}) async-start(), calls=%async_computation.4 | async-start | bytes 14155776 | tf_op jit(solution)/shard_map/all_gather | solution.py:650
  28.6 56.4 %copy-start.32 = (f32[256]{0:T(256)}, f32[256]{0:T(256)S(1)}, u32[]{:S(2)}) copy-start(f32[256]{0:T(256)S(1)} %add_rsqrt_fusion.1) | copy-start | bytes 3076
  123.4 1.2 copy-start
  124.6 1.7 copy-start.4
  126.2 1.1 copy-start.5
  127.4 0.7 copy-start.7
  128.0 0.7 copy-start.9
  128.7 0.6 copy-start.11
  139.2 61.3 %copy-start.21 = (bf16[1,256,1536]{2,1,0:T(8,128)(2,1)S(1)}, bf16[1,256,1536]{2,1,0:T(8,128)(2,1)}, u32[]{:S(2)}) copy-start(bf16[1,256,1536]{2,1,0:T(8,128)(2,1)} %param.21) | copy-start | bytes 2359300
  139.2 61.3 %copy-start.27 = (f32[3072]{0:T(1024)S(1)}, f32[3072]{0:T(1024)}, u32[]{:S(2)}) copy-start(f32[3072]{0:T(1024)} %mul.337) | copy-start | bytes 36868
  148.2 60.8 %copy-start.39 = (f32[256]{0:T(256)}, f32[256]{0:T(256)S(1)}, u32[]{:S(2)}) copy-start(f32[256]{0:T(256)S(1)} %add_rsqrt_fusion) | copy-start | bytes 3076
  200.5 8.5 %copy-start.20 = (f32[256,3072]{1,0:T(8,128)S(1)}, f32[256,3072]{1,0:T(8,128)}, u32[]{:S(2)}) copy-start(f32[256,3072]{1,0:T(8,128)} %get-tuple-element.80) | copy-start | bytes 9437188
  200.5 8.5 %copy-start.28 = (f32[3072]{0:T(1024)S(1)}, f32[3072]{0:T(1024)}, u32[]{:S(2)}) copy-start(f32[3072]{0:T(1024)} %mul.337) | copy-start | bytes 36868
  213.6 210.5 %all-gather.17.cloned.1.call-start = ((), (), s32[]{:S(2)}) async-start(), calls=%async_computation.5 | async-start | bytes 15925248 | tf_op jit(solution)/shard_map/all_gather | solution.py:651
  217.9 1.7 copy-start.1
  217.9 2.2 copy-start.6
  217.9 2.2 copy-start.8
  217.9 2.2 copy-start.10
  217.9 2.2 copy-start.12
  274.8 1.4 copy-start.2
  276.3 273.4 %all-reduce.7.cloned.1.call-start = ((), (), s32[]{:S(2)}) async-start(), calls=%async_computation.3 | async-start | bytes 172032 | tf_op jit(solution)/shard_map/psum | solution.py:683
  276.9 8.0 copy-start.17
  276.9 8.0 copy-start.19
  276.9 8.0 copy-start.33
  284.9 7.9 copy-start.31
  284.9 8.7 %copy-start.3 = (bf16[576,2048]{1,0:T(8,128)(2,1)S(1)}, bf16[576,2048]{1,0:T(8,128)(2,1)}, u32[]{:S(2)}) copy-start(bf16[576,2048]{1,0:T(8,128)(2,1)} %copy-done.2) | copy-start | bytes 7077892
  293.5 520.4 %all-reduce.9.cloned.1.call-start = ((), (), s32[]{:S(2)}) async-start(), calls=%async_computation.7 | async-start | bytes 14745600 | tf_op jit(solution)/shard_map/psum | solution.py:656
  433.6 1.1 copy-start.22
  433.6 4.1 copy-start.18
  437.8 113.6 %copy-start.45 = (f32[192]{0:T(256)S(1)}, f32[192]{0:T(256)}, u32[]{:S(2)}) copy-start(f32[192]{0:T(256)} %param.22) | copy-start | bytes 2308
  437.8 113.6 %copy-start.46 = (f32[192]{0:T(256)S(1)}, f32[192]{0:T(256)}, u32[]{:S(2)}) copy-start(f32[192]{0:T(256)} %param.28) | copy-start | bytes 2308
  437.8 113.6 %copy-start.47 = (f32[192]{0:T(256)S(1)}, f32[192]{0:T(256)}, u32[]{:S(2)}) copy-start(f32[192]{0:T(256)} %param.34) | copy-start | bytes 2308
  437.8 115.0 %copy-start.35 = (f32[3,48]{1,0:T(4,128)S(1)}, f32[3,48]{1,0:T(4,128)}, u32[]{:S(2)}) copy-start(f32[3,48]{1,0:T(4,128)} %param.25) | copy-start | bytes 1732
  437.8 115.0 %copy-start.40 = (f32[3,48]{1,0:T(4,128)S(1)}, f32[3,48]{1,0:T(4,128)}, u32[]{:S(2)}) copy-start(f32[3,48]{1,0:T(4,128)} %param.31) | copy-start | bytes 1732
  437.8 114.9 %copy-start.41 = (f32[3,48]{1,0:T(4,128)S(1)}, f32[3,48]{1,0:T(4,128)}, u32[]{:S(2)}) copy-start(f32[3,48]{1,0:T(4,128)} %param.37) | copy-start | bytes 1732
  437.8 115.5 %copy-start.37 = (f32[384]{0:T(512)S(1)}, f32[384]{0:T(512)}, u32[]{:S(2)}) copy-start(f32[384]{0:T(512)} %param.26) | copy-start | bytes 4612
  437.9 115.5 %copy-start.42 = (f32[384]{0:T(512)S(1)}, f32[384]{0:T(512)}, u32[]{:S(2)}) copy-start(f32[384]{0:T(512)} %param.32) | copy-start | bytes 4612
  437.9 115.5 %copy-start.43 = (f32[384]{0:T(512)S(1)}, f32[384]{0:T(512)}, u32[]{:S(2)}) copy-start(f32[384]{0:T(512)} %param.38) | copy-start | bytes 4612
  437.9 116.9 %copy-start.29 = (f32[5,416]{1,0:T(8,128)S(1)}, f32[5,416]{1,0:T(8,128)}, u32[]{:S(2)}) copy-start(f32[5,416]{1,0:T(8,128)} %param.30) | copy-start | bytes 24964
  437.9 116.9 %copy-start.30 = (f32[5,416]{1,0:T(8,128)S(1)}, f32[5,416]{1,0:T(8,128)}, u32[]{:S(2)}) copy-start(f32[5,416]{1,0:T(8,128)} %param.36) | copy-start | bytes 24964
  551.4 265.2 %copy-start.38 = (f32[3,48]{1,0:T(4,128)}, f32[3,48]{1,0:T(4,128)S(1)}, u32[]{:S(2)}) copy-start(f32[3,48]{1,0:T(4,128)S(1)} %reshape.181) | copy-start | bytes 1732
  813.9 2.5 copy-start.23
  816.6 13.7 %copy-start.13 = (f32[192,6448]{1,0:T(8,128)}, f32[192,6448]{1,0:T(8,128)S(1)}, u32[]{:S(2)}) copy-start(f32[192,6448]{1,0:T(8,128)S(1)} %constant_dynamic-update-slice_fusion) | copy-start | bytes 14856196
  816.6 13.7 %copy-start.14 = (f32[384,1536]{1,0:T(8,128)S(1)}, f32[384,1536]{1,0:T(8,128)}, u32[]{:S(2)}) copy-start(f32[384,1536]{1,0:T(8,128)} %param.27) | copy-start | bytes 7077892
  816.6 13.7 %copy-start.15 = (f32[384,1536]{1,0:T(8,128)S(1)}, f32[384,1536]{1,0:T(8,128)}, u32[]{:S(2)}) copy-start(f32[384,1536]{1,0:T(8,128)} %get-tuple-element.90) | copy-start | bytes 7077892
  816.6 13.9 %copy-start.24 = (f32[384,1536]{1,0:T(8,128)S(1)}, f32[384,1536]{1,0:T(8,128)}, u32[]{:S(2)}) copy-start(f32[384,1536]{1,0:T(8,128)} %param.33) | copy-start | bytes 7077892
  816.6 15.1 %copy-start.25 = (f32[384,1536]{1,0:T(8,128)S(1)}, f32[384,1536]{1,0:T(8,128)}, u32[]{:S(2)}) copy-start(f32[384,1536]{1,0:T(8,128)} %param.39) | copy-start | bytes 7077892
Sparse Core Ops, SparseCore 0:
  11.2 66.5 all-gather.8
  80.3 58.8 all-gather.10
  141.7 58.7 all-gather.12
  202.3 67.6 all-gather.18
  272.3 71.2 all-gather.14
  345.3 78.7 all-gather.16
  430.2 119.4 all-reduce.6
  553.4 260.4 all-reduce.8

commit v2 on v1

--- a/solution.py
+++ b/solution.py
@@ -555,6 +555,207 @@
     )(u, halo, rate, step, cum, cumt, heads, skip, taps, dy, ypre, enter, turn)
 
 
+def line_kernel(shapes, root, lag, has_small, *refs):
+    count = len(shapes)
+    refs = list(refs)
+    parts = [refs.pop(0) for _ in range(count - has_small)]
+    small_ref = refs.pop(0) if has_small else None
+    outs = [refs.pop(0) for _ in range(count)]
+    from_left = [refs.pop(0) for _ in range(count)]
+    from_right = [refs.pop(0) for _ in range(count)]
+    if has_small:
+        small_sum, small_all, small_send, small_recv = (refs.pop(0) for _ in range(4))
+        parts.append(small_sum)
+    up_send, left_recv, right_recv, total_recv, down_left, down_right = refs
+
+    rank = lax.axis_index("seq")
+    last = lax.axis_size("seq") - 1
+    me = lax.axis_index("dp")
+    group = lax.axis_size("dp")
+    barrier = pltpu.get_barrier_semaphore()
+    greet_seq(barrier, rank, last)
+    if has_small:
+        for i in range(1, group):
+            pl.semaphore_signal(
+                barrier, inc=1, device_id={"dp": lax.rem(me + i, group)}, device_id_type=MESH
+            )
+        pl.semaphore_wait(barrier, seq_neighbours(rank, last) + group - 1)
+    else:
+        pl.semaphore_wait(barrier, seq_neighbours(rank, last))
+    left = jnp.maximum(rank - 1, 0)
+    right = jnp.minimum(rank + 1, last)
+
+    def small_copy(i, peer, slot):
+        return pltpu.make_async_remote_copy(
+            src_ref=small_ref.at[peer],
+            dst_ref=small_all.at[slot],
+            send_sem=small_send.at[i],
+            recv_sem=small_recv.at[i],
+            device_id={"dp": peer},
+            device_id_type=MESH,
+        )
+
+    if has_small:
+        for i in range(1, group):
+            small_copy(i, lax.rem(me + i, group), me).start()
+        small_all[me] = small_ref[me]
+
+    def rows_of(array, chunk):
+        size = shapes[array][1]
+        return pl.ds(pl.multiple_of(chunk * size, size), size)
+
+    def up_copy(array, chunk, step, source, target, recv, to):
+        rows = rows_of(array, chunk)
+        return seq_copy(
+            source[array].at[rows, :], target[array].at[rows, :], up_send.at[step], recv.at[step], to
+        )
+
+    def down_copy(array, chunk, step, send, to):
+        rows = rows_of(array, chunk)
+        return seq_copy(
+            outs[array].at[rows, :], outs[array].at[rows, :], send.at[step], total_recv.at[step], to
+        )
+
+    def up_side(array, chunk, step, inbox, recv, edge, to):
+        rows = rows_of(array, chunk)
+
+        @pl.when(rank == edge)
+        def _():
+            up_copy(array, chunk, step, parts, inbox, recv, to).start()
+
+        @pl.when(rank != edge)
+        def _():
+            up_copy(array, chunk, step, inbox, inbox, recv, to).wait_recv()
+            inbox[array][rows, :] += parts[array][rows, :]
+            up_copy(array, chunk, step, inbox, inbox, recv, to).start()
+
+    def up(array, chunk, step):
+        rows = rows_of(array, chunk)
+        if has_small and array == count - 1:
+            for i in range(1, group):
+                small_copy(i, lax.rem(me + i, group), me).wait_send()
+                origin = lax.rem(me + group - i, group)
+                small_copy(i, origin, origin).wait_recv()
+            small_sum[...] = jnp.sum(small_all[...], axis=0)
+
+        @pl.when(rank < root)
+        def _():
+            up_side(array, chunk, step, from_left, left_recv, 0, right)
+
+        @pl.when(rank > root)
+        def _():
+            up_side(array, chunk, step, from_right, right_recv, last, left)
+
+        @pl.when(rank == root)
+        def _():
+            total = parts[array][rows, :]
+            if root > 0:
+                up_copy(array, chunk, step, from_left, from_left, left_recv, left).wait_recv()
+                total = total + from_left[array][rows, :]
+            if root < last:
+                up_copy(array, chunk, step, from_right, from_right, right_recv, right).wait_recv()
+                total = total + from_right[array][rows, :]
+            outs[array][rows, :] = total
+            if root > 0:
+                down_copy(array, chunk, step, down_left, left).start()
+            if root < last:
+                down_copy(array, chunk, step, down_right, right).start()
+
+    def down(array, chunk, step):
+        @pl.when(rank < root)
+        def _():
+            down_copy(array, chunk, step, down_left, left).wait_recv()
+
+            @pl.when(rank > 0)
+            def _():
+                down_copy(array, chunk, step, down_left, left).start()
+
+        @pl.when(rank > root)
+        def _():
+            down_copy(array, chunk, step, down_right, right).wait_recv()
+
+            @pl.when(rank < last)
+            def _():
+                down_copy(array, chunk, step, down_right, right).start()
+
+    def drain(array, chunk, step):
+        @pl.when(rank < root)
+        def _():
+            up_copy(array, chunk, step, parts, from_left, left_recv, right).wait_send()
+
+        @pl.when(rank > root)
+        def _():
+            up_copy(array, chunk, step, parts, from_right, right_recv, left).wait_send()
+
+        @pl.when((rank <= root) & (rank > 0))
+        def _():
+            down_copy(array, chunk, step, down_left, left).wait_send()
+
+        @pl.when((rank >= root) & (rank < last))
+        def _():
+            down_copy(array, chunk, step, down_right, right).wait_send()
+
+    def each(step, action):
+        first = 0
+        for array in range(count):
+            chunks = shapes[array][0] // shapes[array][1]
+
+            @pl.when((step >= first) & (step < first + chunks))
+            def _(array=array, first=first):
+                action(array, step - first, step)
+
+            first += chunks
+        return first
+
+    steps = sum(shape[0] // shape[1] for shape in shapes)
+
+    def forward(step, carry):
+        each(step, up)
+        each(step - lag, down)
+        return carry
+
+    lax.fori_loop(0, steps + lag, forward, 0)
+
+    def finish(step, carry):
+        each(step, drain)
+        return carry
+
+    lax.fori_loop(0, steps, finish, 0)
+
+
+def line_reduce(parts, small, ident):
+    size = lax.axis_size("seq")
+    group = lax.axis_size("dp")
+    shapes = [(part.shape[0], part.shape[0] // 12) for part in parts]
+    full = [part.shape for part in parts]
+    args = list(parts)
+    extra = []
+    if small is not None:
+        shapes.append((8, 8))
+        full.append(small.shape[1:])
+        args.append(small)
+        extra = [
+            pltpu.VMEM(small.shape[1:], f32),
+            pltpu.VMEM(small.shape, f32),
+            pltpu.SemaphoreType.DMA((group,)),
+            pltpu.SemaphoreType.DMA((group,)),
+        ]
+    steps = sum(shape[0] // shape[1] for shape in shapes)
+    return pl.pallas_call(
+        functools.partial(line_kernel, shapes, size // 2, 4, small is not None),
+        out_shape=tuple(jax.ShapeDtypeStruct(shape, f32) for shape in full),
+        in_specs=vmem(len(args)),
+        out_specs=tuple(vmem(len(full))),
+        scratch_shapes=[pltpu.VMEM(shape, f32) for shape in full] * 2
+        + extra
+        + [pltpu.SemaphoreType.DMA((steps,))] * 6,
+        compiler_params=pltpu.CompilerParams(
+            collective_id=ident, has_side_effects=True, vmem_limit_bytes=40 * 2**20
+        ),
+        cost_estimate=pl.CostEstimate(flops=10**10, bytes_accessed=2 * 10**8, transcendentals=0),
+    )(*args)
+
+
 def on_device(
     hidden_in,
     out_grad,
@@ -650,12 +851,14 @@
     gate_all = lax.all_gather(gate_grad, "dp", axis=0, tiled=True)
     scan_all = lax.all_gather(scan_grad, "dp", axis=0, tiled=True)
     normed_turned = turned[:own_in]
-    outproj_owned = lax.psum(
-        jnp.dot(turned[own_in:], cot_all, preferred_element_type=f32), "seq"
-    )
-    gate_owned = lax.psum(jnp.dot(normed_turned, gate_all, preferred_element_type=f32), "seq")
-    scan_owned = lax.psum(jnp.dot(normed_turned, scan_all, preferred_element_type=f32), "seq")
-    inproj_owned = jnp.concatenate([gate_owned, scan_owned], axis=1)
+    outproj_owned, gate_owned = line_reduce(
+        [
+            jnp.dot(turned[own_in:], cot_all, preferred_element_type=f32),
+            jnp.dot(normed_turned, gate_all, preferred_element_type=f32),
+        ],
+        None,
+        3,
+    )
 
     normed_grad = mm(gate_grad, gate_matrix, 1, 1) + mm(scan_grad, scan_matrix, 1, 1)
     plain = hidden * root
@@ -672,23 +875,32 @@
         ],
         axis=0,
     )
+    conv_sums = conv_grad[:tap_rows].reshape(tap_rows, group, conv_own)
     packed = jnp.concatenate(
         [
-            prenorm_grad,
-            postnorm_grad,
-            conv_grad[:tap_rows].reshape(-1),
-            head_sums.reshape(-1),
-        ]
-    )
-    packed = lax.psum(packed, ("dp", "seq"))
-    prenorm_owned = lax.dynamic_slice_in_dim(packed, me * own_in, own_in, 0)
-    postnorm_owned = lax.dynamic_slice_in_dim(packed, model_width + me * own_out, own_out, 0)
-    conv_at = model_width + inner
-    conv_end = conv_at + tap_rows * conv_width
-    conv_owned = lax.dynamic_slice_in_dim(
-        packed[conv_at:conv_end].reshape(tap_rows, conv_width), me * conv_own, conv_own, 1
-    )
-    head_total = packed[conv_end:].reshape(3, heads)
+            prenorm_grad.reshape(group, own_in),
+            postnorm_grad.reshape(group, own_out),
+            jnp.swapaxes(conv_sums, 0, 1).reshape(group, -1),
+            jnp.broadcast_to(head_sums.reshape(1, -1), (group, 3 * heads)),
+        ],
+        axis=1,
+    )
+    packed_size = packed.shape[1]
+    packed_lanes = -(-packed_size // (8 * LANES)) * LANES
+    packed = jnp.pad(packed, ((0, 0), (0, 8 * packed_lanes - packed_size)))
+    scan_owned, packed = line_reduce(
+        [jnp.dot(normed_turned, scan_all, preferred_element_type=f32)],
+        packed.reshape(group, 8, packed_lanes),
+        4,
+    )
+    inproj_owned = jnp.concatenate([gate_owned, scan_owned], axis=1)
+    packed = packed.reshape(-1)
+    prenorm_owned = packed[:own_in]
+    postnorm_owned = packed[own_in : own_in + own_out]
+    conv_at = own_in + own_out
+    conv_end = conv_at + tap_rows * conv_own
+    conv_owned = packed[conv_at:conv_end].reshape(tap_rows, conv_own)
+    head_total = packed[conv_end:packed_size].reshape(3, heads)
 
     prenorm_new, prenorm_mom, prenorm_sq = adam_update(
         prenorm, prenorm_first, prenorm_second, prenorm_owned, rate_vector, 0.0

time: 845 us -> 761 us (0.901)
  waiting for transfers between devices: 590 us -> 148 us
  Pallas kernels: 93 us -> 460 us
  matrix products: 72.8 us -> 64.3 us
    pallas_call x0 -> x2, Pallas kernels: none -> 367 us  [line_reduce(): pl.pallas_call(functools.partial(line_kernel, shapes, size // 2, 4, small...]
    psum x2 -> x0, waiting for transfers between devices: 363 us -> none  [the longest x1 258 us: on_device(): lax.psum(jnp.dot(normed_turned, gate_all, preferred_element_type=f32), 's...]
    all_gather x1, waiting for transfers between devices: 72 us -> 0.01 us  [on_device(): scan_all = lax.all_gather(scan_grad, 'dp', axis=0, tiled=True)]
    all_gather x1, waiting for transfers between devices: 43.2 us -> 34.6 us  [on_device(): gate_all = lax.all_gather(gate_grad, 'dp', axis=0, tiled=True)]
  transfers between devices with their start and end apart: 8 -> 6, of which waited for: 7 -> 4; matrix products, arithmetic and copies ran while one was open for 12% -> 11% of each run, Pallas kernels for 11% -> 43%
where the time goes in v2:
time: 761 us
  Pallas kernels  460 us (60%)
  waiting for transfers between devices  148 us (19%)
  matrix products  64.3 us (8%)
  other arithmetic  37.1 us (5%)
  local copies, waits for them, and re-layouts  25.8 us (3%)
  between operations  14.8 us (2%)
  blocking collectives  10.7 us (1%)
    pallas_call x2, Pallas kernels, line_reduce(): pl.pallas_call(functools.partial(line_kernel, shapes, size // 2, 4, small...  367 us
    pallas_call x1, Pallas kernels, scan_backward(): pl.pallas_call(functools.partial(backward_kernel, sizes), out_shape=(shap...  54.9 us
    all_gather x1, waiting for transfers between devices, on_device(): lax.all_gather(outproject.astype(bf16), 'dp', axis=0, tiled=True)  52.3 us
    all_gather x1, waiting for transfers between devices, on_device(): scan_matrix = lax.all_gather(in_low[:, inner:], 'dp', axis=0, tiled=True)  49.3 us
    pallas_call x1, Pallas kernels, scan_forward(): pl.pallas_call(functools.partial(forward_kernel, sizes), out_shape=(shape...  38.3 us
    all_gather x1, waiting for transfers between devices, on_device(): gate_all = lax.all_gather(gate_grad, 'dp', axis=0, tiled=True)  34.6 us
    dot_general x3, matrix products, mm(): lax.dot_general(a, b, (((ca,), (cb,)), ((), ())), preferred_element_type=...  20.9 us
    sub x6, other arithmetic, adam_update(): weight - step_rate * (moment_hat / (jnp.sqrt(square_hat) + adam_eps) + de...  20.4 us
  transfers between devices with their start and end apart: 6, of which 4 were waited for; matrix products, arithmetic and copies ran while one was open for 11% of the time, Pallas kernels for 43%

profile of v2, /device:TPU:0, one launch (start us, length us, event | category | flops | bytes accessed | tf_op | source)
XLA Modules:
  0.0 760.6 jit_solution(9286824217935111786)
XLA Ops:
  7.2 2.7 convert_element_type.57
  9.9 1.2 slice.68
  11.2 1.2 slice.71
  12.4 2.9 convert_element_type.61
  15.4 0.5 all-gather.19.cloned.1.call-update
  16.1 0.1 concatenate.31
  16.2 0.1 concatenate.32
  16.3 10.7 %all-gather.1 = bf16[8,1,2656]{2,1,0:T(2,128)(2,1)S(1)} all-gather(bf16[1,1,2656]{2,1,0:T(2,128)(2,1)S(1)} %bitcast.70), channel_id=1, replica_groups=mesh['dp'=8,'seq'=4] {'dp'}, dimensions={0}, use_global_device_ids=true | all-gather | bytes 47808 | tf_op jit(solution)/shard_map/all_gather | solution.py:799
  27.3 0.1 broadcast_in_dim.17.skip_ref
  27.4 0.1 reshape.184
  27.6 0.1 reshape.185
  27.7 0.6 mul.328
  28.3 0.2 fusion.20
  28.6 49.3 %all-gather.9.cloned.1.call-done = bf16[1536,3376]{1,0:T(8,128)(2,1)} async-done(((bf16[192,3376]{1,0:T(8,128)(2,1)}), bf16[1536,3376]{1,0:T(8,128)(2,1)}) %all-gather.9.cloned.1.call-update) | async-done | bytes 10371088 | tf_op jit(solution)/shard_map/all_gather | solution.py:797
  77.9 7.1 convolution_convert_fusion.u_ref
  85.0 38.3 %shard_map.395 = (bf16[256,3072]{1,0:T(8,128)(2,1)S(1)}, f32[256,3072]{1,0:T(8,128)S(1)}, f32[24,128,128]{2,1,0:T(8,128)S(1)}, bf16[16,3328]{1,0:T(8,128)(2,1)S(...) custom-call(bf16[256,3376]{1,0:T(8,128)(2,1)S(1)} %convolution_convert_fusion.u_ref, ...), custom_call_target="tpu_custom_call" | custom-call | flops 4000000000 | bytes 10000000 | tf_op jit(solution)/shard_map/pallas_call | solution.py:490
  123.4 1.2 copy-done.1
  124.6 1.7 copy-done.5
  126.2 0.7 copy-done.9
  126.9 0.7 copy-done.11
  127.6 0.6 copy-done.13
  128.2 11.0 %all-gather.11.cloned.1.call-done = bf16[1536,3072]{1,0:T(8,128)(2,1)} async-done(((bf16[192,3072]{1,0:T(8,128)(2,1)}), bf16[1536,3072]{1,0:T(8,128)(2,1)}) %all-gather.11.cloned.1.call-update) | async-done | bytes 9437200 | tf_op jit(solution)/shard_map/all_gather | solution.py:805
  139.2 8.9 %multiply_reduce_fusion.2 = (f32[256]{0:T(256)S(1)}, f32[256,3072]{1,0:T(8,128)}) fusion(bf16[256,3072]{1,0:T(8,128)(2,1)S(1)} %get-tuple-element.41, bf16[1536,3072]{1,0:T(8,128)(2,1)} %all-gather.11.cloned.1.call-done, bf16[1,256,1536]{2,1,0:T(8,128)(2,1)} %param.20, f32[1536]{0:T(1024)S(1)} %mul.320, f32[256]{0:T(256)} %copy-done.29), kind=kOutput, calls=%fused_computation.18 | convolution fusion | flops 2423783168 | bytes 14950400 | tf_op jit(solution)/shard_map/dot_general | solution.py:824
  148.2 52.3 %all-gather.13.cloned.1.call-done = bf16[3072,1536]{1,0:T(8,128)(2,1)} async-done(((bf16[384,1536]{1,0:T(8,128)(2,1)}), bf16[3072,1536]{1,0:T(8,128)(2,1)}) %all-gather.13.cloned.1.call-update) | async-done | bytes 9437200 | tf_op jit(solution)/shard_map/all_gather | solution.py:806
  200.5 8.7 %multiply_reduce_fusion = (f32[3072]{0:T(1024)}, f32[256]{0:T(256)S(1)}, f32[256,3072]{1,0:T(8,128)S(1)}) fusion(f32[256]{0:T(256)S(1)} %add_rsqrt_fusion, bf16[256,3072]{1,0:T(8,128)(2,1)S(1)} %get-tuple-element.41, f32[256,3072]{1,0:T(8,128)} %get-tuple-element.84, f32[3072]{0:T(1024)} %mul.328, bf16[3072,1536]{1,0:T(8,128)(2,1)} %all-gather.13.cloned.1.call-done, ...), kind=kOutput, calls=%fused_computation.13 | convolution fusion | flops 2425352960 | bytes 18114560 | tf_op jit(solution)/shard_map/dot_general | solution.py:40
  209.2 4.6 fusion.5
  213.8 1.4 fusion.32
  215.2 1.2 copy.57
  216.4 1.7 copy.58
  218.2 1.4 pad_maximum_fusion.turn_ref
  219.6 0.2 copy-done.2
  219.8 0.5 copy-done.8
  220.3 54.9 %shard_map.396 = (bf16[256,3376]{1,0:T(8,128)(2,1)}, f32[8,3328]{1,0:T(8,128)S(1)}, f32[8,128]{1,0:T(8,128)S(1)}, bf16[576,2048]{1,0:T(8,128)(2,1)S(1)}) custom-call(bf16[256,3376]{1,0:T(8,128)(2,1)S(1)} %copy-done.2, bf16[16,3328]{1,0:T(8,128)(2,1)S(1)} %copy-done.14, f32[256,128]{1,0:T(8,128)S(1)} %pad_convert_fusion.rate_ref, ...), custom_call_target="tpu_custom_call" | custom-call | flops 6000000000 | bytes 20000000 | tf_op jit(solution)/shard_map/pallas_call | solution.py:523
  275.3 1.4 copy-done.3
  276.8 8.0 %fusion.42 = f32[256,1536]{1,0:T(8,128)S(1)} fusion(bf16[256,3376]{1,0:T(8,128)(2,1)} %get-tuple-element.48, bf16[1536,3376]{1,0:T(8,128)(2,1)} %all-gather.9.cloned.1.call-done), kind=kOutput, calls=%fused_computation.80 | convolution fusion | flops 2654994432 | bytes 13672448 | tf_op jit(solution)/shard_map/dot_general | solution.py:40
  284.8 0.3 slice-done.1
  285.1 1.2 slice-done.2
  286.3 4.3 fusion.19
  290.7 0.1 reshape.193
  290.8 0.1 reshape.194
  291.1 0.1 reduce_sum.71
  291.2 0.1 broadcast_in_dim.18
  291.3 0.1 concatenate.35
  291.4 3.4 fusion.18
  294.8 6.9 fusion.refs_0_
  301.7 7.4 fusion.7
  309.1 34.6 %all-gather.17.cloned.1.call-done = bf16[2048,3072]{1,0:T(8,128)(2,1)} async-done(((bf16[256,3072]{1,0:T(8,128)(2,1)}), bf16[2048,3072]{1,0:T(8,128)(2,1)}) %all-gather.17.cloned.1.call-update) | async-done | bytes 12582928 | tf_op jit(solution)/shard_map/all_gather | solution.py:851
  343.7 6.1 fusion.24.refs_1_
  349.9 236.6 %shard_map.398 = (f32[384,1536]{1,0:T(8,128)S(1)}, f32[192,3072]{1,0:T(8,128)S(1)}) custom-call(f32[384,1536]{1,0:T(8,128)S(1)} %copy-done.6, f32[192,3072]{1,0:T(8,128)S(1)} %fusion.24.refs_1_), custom_call_target="tpu_custom_call" | custom-call | flops 10000000000 | bytes 200000000 | tf_op jit(solution)/shard_map/pallas_call | solution.py:744
  586.5 1.6 constant_dynamic-update-slice_fusion.1
  588.1 0.9 copy-done.15
  589.0 0.7 copy-done.21
  589.7 4.2 multiply_subtract_fusion.1
  594.0 6.9 fusion.26.refs_0_
  600.9 129.9 %shard_map.397 = (f32[192,3376]{1,0:T(8,128)S(1)}, f32[8,384]{1,0:T(8,128)S(1)}) custom-call(f32[192,3376]{1,0:T(8,128)S(1)} %fusion.26.refs_0_, f32[8,8,384]{2,1,0:T(8,128)S(1)} %bitcast.60), custom_call_target="tpu_custom_call" | custom-call | flops 10000000000 | bytes 200000000 | tf_op jit(solution)/shard_map/pallas_call | solution.py:744
  730.8 1.5 copy-done
  732.6 0.1 reshape.199
  732.7 0.6 multiply_subtract_fusion.5
  733.3 3.5 constant_dynamic-update-slice_fusion
  736.7 0.7 multiply_subtract_fusion.3
  737.4 13.7 %multiply_subtract_fusion = (f32[192,6448]{1,0:T(8,128)}, f32[192,6448]{1,0:T(8,128)}, f32[192,6448]{1,0:T(8,128)}) fusion(f32[192,6448]{1,0:T(8,128)} %param.23, f32[192,6448]{1,0:T(8,128)} %constant_dynamic-update-slice_fusion, f32[192,6448]{1,0:T(8,128)} %param.29, f32[192,6448]{1,0:T(8,128)} %param.35), kind=kLoop, calls=%fused_computation.5 | loop fusion | flops 18570240 | bytes 34664448 | tf_op jit(solution)/shard_map/sub | solution.py:33
  751.1 0.6 multiply_subtract_fusion.2
  751.8 0.6 multiply_subtract_fusion.4
  752.4 1.4 copy.71
  (132 shorter events, 1.5 us)
Async XLA Ops:
  7.2 70.7 %all-gather.9.cloned.1.call-start = ((), (), s32[]{:S(2)}) async-start(), calls=%async_computation | async-start | bytes 11943936 | tf_op jit(solution)/shard_map/all_gather | solution.py:797
  11.1 128.1 %all-gather.11.cloned.1.call-start = ((), (), s32[]{:S(2)}) async-start(), calls=%async_computation.1 | async-start | bytes 10616832 | tf_op jit(solution)/shard_map/all_gather | solution.py:805
  12.3 3.6 copy-start.41
  12.3 3.7 copy-start.34
  12.4 3.7 copy-start.24
  12.4 14.9 %copy-start.31 = (f32[3,48]{1,0:T(4,128)S(1)}, f32[3,48]{1,0:T(4,128)}, u32[]{:S(2)}) copy-start(f32[3,48]{1,0:T(4,128)} %param.25) | copy-start | bytes 1732
  12.4 15.9 %copy-start.16 = (bf16[1,256,1536]{2,1,0:T(8,128)(2,1)S(1)}, bf16[1,256,1536]{2,1,0:T(8,128)(2,1)}, u32[]{:S(2)}) copy-start(bf16[1,256,1536]{2,1,0:T(8,128)(2,1)} %param.20) | copy-start | bytes 2359300
  12.4 188.1 %all-gather.13.cloned.1.call-start = ((), (), s32[]{:S(2)}) async-start(), calls=%async_computation.2 | async-start | bytes 10616832 | tf_op jit(solution)/shard_map/all_gather | solution.py:806
  15.3 279.5 %all-gather.19.cloned.1.call-start = ((), (), s32[]{:S(2)}) async-start(), calls=%async_computation.5 | async-start | bytes 7077888 | tf_op jit(solution)/shard_map/all_gather | solution.py:810
  15.9 327.8 %all-gather.17.cloned.1.call-start = ((), (), s32[]{:S(2)}) async-start(), calls=%async_computation.4 | async-start | bytes 14155776 | tf_op jit(solution)/shard_map/all_gather | solution.py:851
  28.6 56.4 %copy-start.29 = (f32[256]{0:T(256)}, f32[256]{0:T(256)S(1)}, u32[]{:S(2)}) copy-start(f32[256]{0:T(256)S(1)} %add_rsqrt_fusion.1) | copy-start | bytes 3076
  123.4 1.2 copy-start.1
  124.6 1.7 copy-start.5
  126.2 0.7 copy-start.9
  126.9 0.7 copy-start.11
  127.6 0.6 copy-start.13
  128.2 20.0 %copy-start.7 = (f32[24,128,128]{2,1,0:T(8,128)}, f32[24,128,128]{2,1,0:T(8,128)S(1)}, u32[]{:S(2)}) copy-start(f32[24,128,128]{2,1,0:T(8,128)S(1)} %get-tuple-element.47.enter_ref) | copy-start | bytes 4718596
  148.2 61.0 %copy-start.36 = (f32[256]{0:T(256)}, f32[256]{0:T(256)S(1)}, u32[]{:S(2)}) copy-start(f32[256]{0:T(256)S(1)} %add_rsqrt_fusion) | copy-start | bytes 3076
  200.5 8.7 %copy-start.20 = (f32[256,3072]{1,0:T(8,128)S(1)}, f32[256,3072]{1,0:T(8,128)}, u32[]{:S(2)}) copy-start(f32[256,3072]{1,0:T(8,128)} %get-tuple-element.84) | copy-start | bytes 9437188
  200.5 8.7 %copy-start.25 = (f32[3072]{0:T(1024)S(1)}, f32[3072]{0:T(1024)}, u32[]{:S(2)}) copy-start(f32[3072]{0:T(1024)} %mul.328) | copy-start | bytes 36868
  213.8 380.2 %all-gather.15.cloned.1.call-start = ((), (), s32[]{:S(2)}) async-start(), calls=%async_computation.3 | async-start | bytes 15925248 | tf_op jit(solution)/shard_map/all_gather | solution.py:852
  218.1 1.7 copy-start.2
  218.1 2.2 copy-start.8
  218.1 2.2 copy-start.10
  218.1 2.2 copy-start.12
  218.2 2.2 copy-start.14
  275.3 1.4 copy-start.3
  276.7 8.1 %slice-start = ((s8[9437184]{0:T(1024)(128)(4,1)}), s8[1048576]{0:T(1024)(128)(4,1)S(1)}, s32[]{:S(2)}) async-start(s8[9437184]{0:T(1024)(128)(4,1)} %bitcast.72), calls=%async_computation.6 | async-start | bytes 2097152
  276.7 8.1 %copy-start.17 = (bf16[1,256,1536]{2,1,0:T(8,128)(2,1)S(1)}, bf16[1,256,1536]{2,1,0:T(8,128)(2,1)}, u32[]{:S(2)}) copy-start(bf16[1,256,1536]{2,1,0:T(8,128)(2,1)} %param.20) | copy-start | bytes 2359300
  276.7 8.1 %copy-start.19 = (bf16[256,3072]{1,0:T(8,128)(2,1)S(1)}, bf16[256,3072]{1,0:T(8,128)(2,1)}, u32[]{:S(2)}) copy-start(bf16[256,3072]{1,0:T(8,128)(2,1)} %get-tuple-element.80) | copy-start | bytes 4718596
  276.7 8.1 %copy-start.30 = (f32[256]{0:T(256)S(1)}, f32[256]{0:T(256)}, u32[]{:S(2)}) copy-start(f32[256]{0:T(256)} %copy-done.29) | copy-start | bytes 3076
  276.7 8.4 %slice-start.1 = ((s8[9437184]{0:T(1024)(128)(4,1)}), s8[4194304]{0:T(1024)(128)(4,1)S(1)}, s32[]{:S(2)}) async-start(s8[9437184]{0:T(1024)(128)(4,1)} %bitcast.72), calls=%async_computation.7 | async-start | bytes 8388608
  276.8 9.6 %slice-start.2 = ((s8[9437184]{0:T(1024)(128)(4,1)}), s8[4194304]{0:T(1024)(128)(4,1)S(1)}, s32[]{:S(2)}) async-start(s8[9437184]{0:T(1024)(128)(4,1)} %bitcast.72), calls=%async_computation.8 | async-start | bytes 8388608
  286.3 4.3 copy-start.28
  291.3 3.5 copy-start.4
  294.8 6.9 copy-start.18
  343.7 6.2 copy-start.6
  349.9 238.2 %copy-start.22 = (f32[384,1536]{1,0:T(8,128)S(1)}, f32[384,1536]{1,0:T(8,128)}, u32[]{:S(2)}) copy-start(f32[384,1536]{1,0:T(8,128)} %param.39) | copy-start | bytes 7077892
  586.5 2.5 copy-start.15
  586.5 3.2 copy-start.21
  600.8 131.8 %copy-start.42 = (f32[192]{0:T(256)S(1)}, f32[192]{0:T(256)}, u32[]{:S(2)}) copy-start(f32[192]{0:T(256)} %param.22) | copy-start | bytes 2308
  600.8 131.8 %copy-start.43 = (f32[192]{0:T(256)S(1)}, f32[192]{0:T(256)}, u32[]{:S(2)}) copy-start(f32[192]{0:T(256)} %param.28) | copy-start | bytes 2308
  600.9 131.8 %copy-start.44 = (f32[192]{0:T(256)S(1)}, f32[192]{0:T(256)}, u32[]{:S(2)}) copy-start(f32[192]{0:T(256)} %param.34) | copy-start | bytes 2308
  730.8 1.5 copy-start
  732.5 18.5 %copy-start.23 = (f32[5,416]{1,0:T(8,128)}, f32[5,416]{1,0:T(8,128)S(1)}, u32[]{:S(2)}) copy-start(f32[5,416]{1,0:T(8,128)S(1)} %reshape.198) | copy-start | bytes 24964
  732.6 19.1 %copy-start.33 = (f32[3,48]{1,0:T(4,128)}, f32[3,48]{1,0:T(4,128)S(1)}, u32[]{:S(2)}) copy-start(f32[3,48]{1,0:T(4,128)S(1)} %reshape.199) | copy-start | bytes 1732
  733.2 3.5 copy-start.35
  733.2 3.5 copy-start.39
  733.3 3.5 copy-start.40
  737.4 13.7 %copy-start.26 = (f32[5,416]{1,0:T(8,128)S(1)}, f32[5,416]{1,0:T(8,128)}, u32[]{:S(2)}) copy-start(f32[5,416]{1,0:T(8,128)} %param.30) | copy-start | bytes 24964
  737.4 13.7 %copy-start.27 = (f32[5,416]{1,0:T(8,128)S(1)}, f32[5,416]{1,0:T(8,128)}, u32[]{:S(2)}) copy-start(f32[5,416]{1,0:T(8,128)} %param.36) | copy-start | bytes 24964
  737.4 14.3 %copy-start.32 = (f32[3,48]{1,0:T(4,128)S(1)}, f32[3,48]{1,0:T(4,128)}, u32[]{:S(2)}) copy-start(f32[3,48]{1,0:T(4,128)} %param.25) | copy-start | bytes 1732
  737.4 14.3 %copy-start.37 = (f32[3,48]{1,0:T(4,128)S(1)}, f32[3,48]{1,0:T(4,128)}, u32[]{:S(2)}) copy-start(f32[3,48]{1,0:T(4,128)} %param.31) | copy-start | bytes 1732
  737.4 14.3 %copy-start.38 = (f32[3,48]{1,0:T(4,128)S(1)}, f32[3,48]{1,0:T(4,128)}, u32[]{:S(2)}) copy-start(f32[3,48]{1,0:T(4,128)} %param.37) | copy-start | bytes 1732
Sparse Core Ops, SparseCore 0:
  11.2 66.5 all-gather.8
  80.3 58.8 all-gather.10
  141.7 58.7 all-gather.12
  202.3 67.8 all-gather.18
  272.5 71.2 all-gather.16
  345.5 78.7 all-gather.14

commit v3 on v1

--- a/solution.py
+++ b/solution.py
@@ -10,6 +10,7 @@
 N = 128
 LANES = 128
 HALO = 16
+WIDE = 256
 
 norm_eps = 1e-05
 beta_moment = 0.9
@@ -100,6 +101,23 @@
 
 def seq_neighbours(rank, last):
     return jnp.minimum(rank, 1) + jnp.minimum(last - rank, 1)
+
+
+def greet_plane(barrier, me, group):
+    for i in range(1, group):
+        pl.semaphore_signal(
+            barrier, inc=1, device_id={"dp": lax.rem(me + i, group)}, device_id_type=MESH
+        )
+
+
+def slot_of(device, group):
+    return lax.rem(device, 2) * (group // 2) + device // 2
+
+
+def ring_place(at, chips):
+    half = chips // 2
+    turned = at // half
+    return at * (1 - turned) + turned * (3 * half - 1 - at)
 
 
 def forward_kernel(
@@ -271,17 +289,17 @@
     group = lax.axis_size("dp")
     barrier = pltpu.get_barrier_semaphore()
     greet_seq(barrier, rank, last)
-    for i in range(1, group):
-        pl.semaphore_signal(
-            barrier, inc=1, device_id={"dp": lax.rem(me + i, group)}, device_id_type=MESH
-        )
+    greet_plane(barrier, me, group)
     pl.semaphore_wait(barrier, seq_neighbours(rank, last) + group - 1)
+
+    def landing(device):
+        return turned_ref.at[:, pl.ds(pl.multiple_of(slot_of(device, group) * rows, rows), rows)]
 
     def turn(i):
         peer = lax.rem(me + i, group)
         return pltpu.make_async_remote_copy(
             src_ref=turn_ref.at[peer],
-            dst_ref=turned_ref.at[:, pl.ds(pl.multiple_of(me * rows, rows), rows)],
+            dst_ref=landing(me),
             send_sem=turn_send.at[i],
             recv_sem=turn_recv.at[i],
             device_id={"dp": peer},
@@ -290,11 +308,7 @@
 
     for i in range(1, group):
         turn(i).start()
-    own_copy = pltpu.make_async_copy(
-        turn_ref.at[me],
-        turned_ref.at[:, pl.ds(pl.multiple_of(me * rows, rows), rows)],
-        own_sem,
-    )
+    own_copy = pltpu.make_async_copy(turn_ref.at[me], landing(me), own_sem)
     own_copy.start()
 
     left = jnp.maximum(rank - 1, 0)
@@ -433,8 +447,10 @@
         ],
         axis=0,
     )
-    heads = tiles * per_tile
-    dproj_ref[:, conv_width : conv_width + heads] = drate[:, 0:heads].astype(bf16)
+    dproj_ref[:, conv_width : conv_width + LANES] = drate.astype(bf16)
+    dproj_ref[:, conv_width + LANES :] = jnp.zeros(
+        (rows, dproj_ref.shape[1] - conv_width - LANES), bf16
+    )
 
     @pl.when(rank == last)
     def _():
@@ -471,7 +487,7 @@
         origin = lax.rem(me + group - i, group)
         pltpu.make_async_remote_copy(
             src_ref=turn_ref.at[origin],
-            dst_ref=turned_ref.at[:, pl.ds(pl.multiple_of(origin * rows, rows), rows)],
+            dst_ref=landing(origin),
             send_sem=turn_send.at[i],
             recv_sem=turn_recv.at[i],
             device_id={"dp": origin},
@@ -523,7 +539,7 @@
     return pl.pallas_call(
         functools.partial(backward_kernel, sizes),
         out_shape=(
-            shape(u.shape, bf16),
+            shape((rows, -(-u.shape[1] // WIDE) * WIDE), bf16),
             shape((8, conv_width), f32),
             shape((8, LANES), f32),
             shape((turn_rows, group * rows), bf16),
@@ -553,6 +569,409 @@
         ),
         cost_estimate=pl.CostEstimate(flops=6 * 10**9, bytes_accessed=2 * 10**7, transcendentals=4 * 10**6),
     )(u, halo, rate, step, cum, cumt, heads, skip, taps, dy, ypre, enter, turn)
+
+
+def tail_kernel(
+    sizes,
+    turned_ref,
+    cot_ref,
+    gate_ref,
+    scan_ref,
+    small_ref,
+    in_ref,
+    out_ref,
+    small_out_ref,
+    gathered_ref,
+    value_ref,
+    inbox_ref,
+    other_ref,
+    total_ref,
+    loaded_ref,
+    small_value_ref,
+    small_inbox_ref,
+    small_other_ref,
+    small_all_ref,
+    up_send,
+    inbox_recv,
+    other_recv,
+    total_recv,
+    left_send,
+    right_send,
+    store_sem,
+    ring_send,
+    ring_recv,
+    pair_send,
+    pair_recv,
+    own_sem,
+    load_sem,
+    small_send,
+    small_recv,
+):
+    rows, own_in, out_steps, gate_steps, steps, root, lag, spacing = sizes
+    chunks = steps - out_steps
+    rank = lax.axis_index("seq")
+    last = lax.axis_size("seq") - 1
+    me = lax.axis_index("dp")
+    group = lax.axis_size("dp")
+    chips = group // 2
+    reach = chips // 2
+    core = lax.rem(me, 2)
+    chip = me // 2
+    place = ring_place(chip, chips)
+    barrier = pltpu.get_barrier_semaphore()
+    greet_seq(barrier, rank, last)
+    greet_plane(barrier, me, group)
+    pl.semaphore_wait(barrier, seq_neighbours(rank, last) + group - 1)
+    left = jnp.maximum(rank - 1, 0)
+    right = jnp.minimum(rank + 1, last)
+
+    def plane_copy(src, dst, send, recv, to):
+        return pltpu.make_async_remote_copy(
+            src_ref=src,
+            dst_ref=dst,
+            send_sem=send,
+            recv_sem=recv,
+            device_id={"dp": to},
+            device_id_type=MESH,
+        )
+
+    def small_copy(i, peer, slot):
+        return plane_copy(
+            small_ref.at[peer], small_all_ref.at[slot], small_send.at[i], small_recv.at[i], peer
+        )
+
+    for i in range(1, group):
+        small_copy(i, lax.rem(me + i, group), me).start()
+    small_all_ref[me] = small_ref[me]
+
+    def ring_chip(ahead):
+        return ring_place(lax.rem(place + ahead + chips, chips), chips)
+
+    def block(chunk, origin, part):
+        ref = gathered_ref.at[chunk, core, origin]
+        return ref if part is None else ref.at[pl.ds(part * (rows // 2), rows // 2), :]
+
+    def hop(chunk, number, way, source=None):
+        origin = ring_chip(-way * (number - 1))
+        part = None if number < reach else (0 if way == 1 else 1)
+        at = 2 * (number - 1) + (0 if way == 1 else 1)
+        return plane_copy(
+            block(chunk, origin, part) if source is None else source,
+            block(chunk, origin, part),
+            ring_send.at[chunk, at],
+            ring_recv.at[chunk, at],
+            2 * ring_chip(way) + core,
+        )
+
+    def hop_in(chunk, number, way):
+        origin = ring_chip(-way * number)
+        part = None if number < reach else (0 if way == 1 else 1)
+        at = 2 * (number - 1) + (0 if way == 1 else 1)
+        return plane_copy(
+            block(chunk, origin, part),
+            block(chunk, origin, part),
+            ring_send.at[chunk, at],
+            ring_recv.at[chunk, at],
+            2 * ring_chip(way) + core,
+        )
+
+    def own_source(chunk, part, action):
+        part_rows = pl.ds(0, rows) if part is None else pl.ds(part * (rows // 2), rows // 2)
+
+        @pl.when(chunk < gate_steps)
+        def _():
+            start = pl.multiple_of(chunk * WIDE, WIDE)
+            action(gate_ref.at[part_rows, pl.ds(start, WIDE)])
+
+        @pl.when(chunk >= gate_steps)
+        def _():
+            start = pl.multiple_of((chunk - gate_steps) * WIDE, WIDE)
+            action(scan_ref.at[part_rows, pl.ds(start, WIDE)])
+
+    def own_copy(chunk, source):
+        return pltpu.make_async_copy(source, block(chunk, chip, None), own_sem.at[chunk])
+
+    def pair_copy(chunk, half):
+        return plane_copy(
+            gathered_ref.at[chunk, half],
+            gathered_ref.at[chunk, half],
+            pair_send.at[chunk],
+            pair_recv.at[chunk],
+            me + 1 - 2 * core,
+        )
+
+    def load_copy(chunk):
+        slot = lax.rem(chunk, 2)
+        return pltpu.make_async_copy(
+            gathered_ref.at[chunk], loaded_ref.at[slot], load_sem.at[slot]
+        )
+
+    def ring_stage(chunk, stage):
+        if stage == 0:
+            own_source(chunk, None, lambda source: own_copy(chunk, source).start())
+            for way in (1, -1):
+                part = None if reach > 1 else (0 if way == 1 else 1)
+                own_source(
+                    chunk, part, lambda source, way=way: hop(chunk, 1, way, source).start()
+                )
+        elif stage < reach:
+            for way in (1, -1):
+                hop_in(chunk, stage, way).wait_recv()
+                hop(chunk, stage + 1, way).start()
+        else:
+            for way in (1, -1):
+                hop_in(chunk, stage, way).wait_recv()
+            own_copy(chunk, block(chunk, chip, None)).wait()
+            pair_copy(chunk, core).start()
+
+    def compute(step):
+        @pl.when(step < out_steps)
+        def _():
+            cols = pl.ds(pl.multiple_of(step * LANES, LANES), LANES)
+            cot = jnp.concatenate(
+                [
+                    cot_ref[pl.ds((2 * (slot % chips) + slot // chips) * rows, rows), cols]
+                    for slot in range(group)
+                ],
+                axis=0,
+            )
+            for half in range(2):
+                rows_at = own_in * (1 + half)
+                value_ref[:, half * LANES : (half + 1) * LANES] = mm(
+                    turned_ref[rows_at : rows_at + own_in, :], cot, 1, 0
+                )
+
+        @pl.when(step >= out_steps)
+        def _():
+            chunk = step - out_steps
+            load_copy(chunk).wait()
+            arrived = loaded_ref[lax.rem(chunk, 2)].reshape(group * rows, WIDE)
+            value_ref[...] = mm(turned_ref[0:own_in, :], arrived, 1, 0)
+
+    def up_copy(source, target, step, recv, to):
+        return seq_copy(source, target, up_send.at[step], recv.at[step], to)
+
+    def up(value, inbox, other, total, step):
+        edge = ((rank == 0) | (rank == last)) & (rank != root)
+        inner = (rank != root) & (rank > 0) & (rank < last)
+
+        @pl.when(edge)
+        def _():
+            inbox[...] = value[...]
+
+        @pl.when(inner)
+        def _():
+            up_copy(inbox, inbox, step, inbox_recv, left).wait_recv()
+            inbox[...] += value[...]
+
+        @pl.when(rank < root)
+        def _():
+            up_copy(inbox, inbox, step, inbox_recv, right).start()
+
+        @pl.when(rank == root + 1)
+        def _():
+            up_copy(inbox, other, step, other_recv, left).start()
+
+        @pl.when(rank > root + 1)
+        def _():
+            up_copy(inbox, inbox, step, inbox_recv, left).start()
+
+        @pl.when(rank == root)
+        def _():
+            result = value[...]
+            if root > 0:
+                up_copy(inbox, inbox, step, inbox_recv, left).wait_recv()
+                result = result + inbox[...]
+            if root < last:
+                up_copy(other, other, step, other_recv, right).wait_recv()
+                result = result + other[...]
+            total[...] = result
+            if root > 0:
+                down_copy(total, step, left_send, left).start()
+            if root < last:
+                down_copy(total, step, right_send, right).start()
+
+    def down_copy(total, step, send, to):
+        return seq_copy(total, total, send.at[step], total_recv.at[step], to)
+
+    def down(total, step):
+        @pl.when(rank < root)
+        def _():
+            down_copy(total, step, left_send, left).wait_recv()
+
+            @pl.when(rank > 0)
+            def _():
+                down_copy(total, step, left_send, left).start()
+
+        @pl.when(rank > root)
+        def _():
+            down_copy(total, step, right_send, right).wait_recv()
+
+            @pl.when(rank < last)
+            def _():
+                down_copy(total, step, right_send, right).start()
+
+    def store_out(step, half):
+        cols = pl.ds(pl.multiple_of(step * LANES, LANES), LANES)
+        return pltpu.make_async_copy(
+            total_ref.at[step, :, pl.ds(half * LANES, LANES)],
+            out_ref.at[pl.ds(half * own_in, own_in), cols],
+            store_sem.at[step, half],
+        )
+
+    def store_in(step):
+        cols = pl.ds(pl.multiple_of((step - out_steps) * WIDE, WIDE), WIDE)
+        return pltpu.make_async_copy(
+            total_ref.at[step], in_ref.at[:, cols], store_sem.at[step, 0]
+        )
+
+    def stored(step, action):
+        @pl.when(step < out_steps)
+        def _():
+            for half in range(2):
+                action(store_out(step, half))
+
+        @pl.when(step >= out_steps)
+        def _():
+            action(store_in(step))
+
+    def drain(inbox, other, total, step):
+        @pl.when(rank < root)
+        def _():
+            up_copy(inbox, inbox, step, inbox_recv, right).wait_send()
+
+        @pl.when(rank > root)
+        def _():
+            up_copy(inbox, inbox, step, inbox_recv, left).wait_send()
+
+        @pl.when((rank <= root) & (rank > 0))
+        def _():
+            down_copy(total, step, left_send, left).wait_send()
+
+        @pl.when((rank >= root) & (rank < last))
+        def _():
+            down_copy(total, step, right_send, right).wait_send()
+
+    behind = lag * (jnp.maximum(rank - root, 0) + jnp.maximum(root - rank, 0))
+
+    def round_(step, carry):
+        for stage in range(reach, -1, -1):
+            chunk = step - stage * spacing
+
+            @pl.when((chunk >= 0) & (chunk < chunks))
+            def _(chunk=chunk, stage=stage):
+                ring_stage(chunk, stage)
+
+        ready = step - (out_steps - 1)
+
+        @pl.when((ready >= 0) & (ready < chunks))
+        def _():
+            pair_copy(ready, 1 - core).wait_recv()
+            load_copy(ready).start()
+
+        @pl.when(step < steps)
+        def _():
+            compute(step)
+            up(value_ref, inbox_ref.at[step], other_ref.at[step], total_ref.at[step], step)
+
+        @pl.when(step == steps)
+        def _():
+            for i in range(1, group):
+                small_copy(i, lax.rem(me + i, group), me).wait_send()
+                origin = lax.rem(me + group - i, group)
+                small_copy(i, origin, origin).wait_recv()
+            small_value_ref[...] = jnp.sum(small_all_ref[...], axis=0)
+            up(small_value_ref, small_inbox_ref, small_other_ref, small_out_ref, steps)
+
+        late = step - behind
+
+        @pl.when((late >= 0) & (late < steps))
+        def _():
+            down(total_ref.at[late], late)
+            stored(late, lambda copy: copy.start())
+
+        @pl.when(late == steps)
+        def _():
+            down(small_out_ref, steps)
+
+        return carry
+
+    lax.fori_loop(0, steps + 1 + behind, round_, 0)
+
+    def finish(step, carry):
+        drain(inbox_ref.at[step], other_ref.at[step], total_ref.at[step], step)
+        stored(step, lambda copy: copy.wait())
+        return carry
+
+    lax.fori_loop(0, steps, finish, 0)
+    drain(small_inbox_ref, small_other_ref, small_out_ref, steps)
+
+    def finish_ring(chunk, carry):
+        for number in range(1, reach + 1):
+            for way in (1, -1):
+                hop(chunk, number, way).wait_send()
+        pair_copy(chunk, core).wait_send()
+        return carry
+
+    lax.fori_loop(0, chunks, finish_ring, 0)
+
+
+def reduce_gradients(turned, cot_all, gate_grad, scan_grad, small, own_in):
+    size = lax.axis_size("seq")
+    group = lax.axis_size("dp")
+    rows = gate_grad.shape[0]
+    model_width = cot_all.shape[1]
+    out_steps = model_width // LANES
+    gate_steps = gate_grad.shape[1] // WIDE
+    chunks = gate_steps + scan_grad.shape[1] // WIDE
+    steps = out_steps + chunks
+    reach = group // 4
+    spacing = min(3, (out_steps - 2) // reach)
+    sizes = (rows, own_in, out_steps, gate_steps, steps, size // 2, 3, spacing)
+    shape = jax.ShapeDtypeStruct
+    dma = pltpu.SemaphoreType.DMA
+    small_shape = small.shape[1:]
+    anywhere = pl.BlockSpec(memory_space=pl.ANY)
+    return pl.pallas_call(
+        functools.partial(tail_kernel, sizes),
+        out_shape=(
+            shape((own_in, chunks * WIDE), f32),
+            shape((2 * own_in, model_width), f32),
+            shape(small_shape, f32),
+            shape((chunks, 2, group // 2, rows, WIDE), bf16),
+        ),
+        in_specs=vmem(2) + [anywhere] * 2 + vmem(1),
+        out_specs=(anywhere, anywhere, vmem(1)[0], anywhere),
+        scratch_shapes=[
+            pltpu.VMEM((own_in, WIDE), f32),
+            pltpu.VMEM((steps, own_in, WIDE), f32),
+            pltpu.VMEM((steps, own_in, WIDE), f32),
+            pltpu.VMEM((steps, own_in, WIDE), f32),
+            pltpu.VMEM((2, 2, group // 2, rows, WIDE), bf16),
+            pltpu.VMEM(small_shape, f32),
+            pltpu.VMEM(small_shape, f32),
+            pltpu.VMEM(small_shape, f32),
+            pltpu.VMEM(small.shape, f32),
+        ]
+        + [dma((steps + 1,))] * 6
+        + [
+            dma((steps, 2)),
+            dma((chunks, 2 * reach)),
+            dma((chunks, 2 * reach)),
+            dma((chunks,)),
+            dma((chunks,)),
+            dma((chunks,)),
+            dma((2,)),
+            dma((group,)),
+            dma((group,)),
+        ],
+        compiler_params=pltpu.CompilerParams(
+            collective_id=3, has_side_effects=True, vmem_limit_bytes=52 * 2**20
+        ),
+        cost_estimate=pl.CostEstimate(
+            flops=2 * 10**10, bytes_accessed=2 * 10**8, transcendentals=0
+        ),
+    )(turned, cot_all, gate_grad, scan_grad, small)
 
 
 def on_device(
@@ -647,17 +1066,9 @@
     scan_grad, conv_grad, head_grad, turned = scan_backward(
         scan_in, halo, rate, step, cum, cumt, head_rows, skip, taps_pad, dy, ypre, enter, turn, sizes
     )
-    gate_all = lax.all_gather(gate_grad, "dp", axis=0, tiled=True)
-    scan_all = lax.all_gather(scan_grad, "dp", axis=0, tiled=True)
-    normed_turned = turned[:own_in]
-    outproj_owned = lax.psum(
-        jnp.dot(turned[own_in:], cot_all, preferred_element_type=f32), "seq"
-    )
-    gate_owned = lax.psum(jnp.dot(normed_turned, gate_all, preferred_element_type=f32), "seq")
-    scan_owned = lax.psum(jnp.dot(normed_turned, scan_all, preferred_element_type=f32), "seq")
-    inproj_owned = jnp.concatenate([gate_owned, scan_owned], axis=1)
-
-    normed_grad = mm(gate_grad, gate_matrix, 1, 1) + mm(scan_grad, scan_matrix, 1, 1)
+    normed_grad = mm(gate_grad, gate_matrix, 1, 1) + mm(
+        scan_grad[:, : scan_matrix.shape[1]], scan_matrix, 1, 1
+    )
     plain = hidden * root
     prenorm_grad = jnp.sum(normed_grad * plain, axis=0)
     dplain = normed_grad * pre_scale
@@ -672,23 +1083,30 @@
         ],
         axis=0,
     )
+    conv_sums = conv_grad[:tap_rows].reshape(tap_rows, group, conv_own)
     packed = jnp.concatenate(
         [
-            prenorm_grad,
-            postnorm_grad,
-            conv_grad[:tap_rows].reshape(-1),
-            head_sums.reshape(-1),
-        ]
-    )
-    packed = lax.psum(packed, ("dp", "seq"))
-    prenorm_owned = lax.dynamic_slice_in_dim(packed, me * own_in, own_in, 0)
-    postnorm_owned = lax.dynamic_slice_in_dim(packed, model_width + me * own_out, own_out, 0)
-    conv_at = model_width + inner
-    conv_end = conv_at + tap_rows * conv_width
-    conv_owned = lax.dynamic_slice_in_dim(
-        packed[conv_at:conv_end].reshape(tap_rows, conv_width), me * conv_own, conv_own, 1
-    )
-    head_total = packed[conv_end:].reshape(3, heads)
+            prenorm_grad.reshape(group, own_in),
+            postnorm_grad.reshape(group, own_out),
+            jnp.swapaxes(conv_sums, 0, 1).reshape(group, -1),
+            jnp.broadcast_to(head_sums.reshape(1, -1), (group, 3 * heads)),
+        ],
+        axis=1,
+    )
+    packed_size = packed.shape[1]
+    packed_lanes = -(-packed_size // (8 * LANES)) * LANES
+    packed = jnp.pad(packed, ((0, 0), (0, 8 * packed_lanes - packed_size)))
+    inproj_padded, outproj_owned, packed, _ = reduce_gradients(
+        turned, cot_all, gate_grad, scan_grad, packed.reshape(group, 8, packed_lanes), own_in
+    )
+    inproj_owned = inproj_padded[:, :proj_width]
+    packed = packed.reshape(-1)
+    prenorm_owned = packed[:own_in]
+    postnorm_owned = packed[own_in : own_in + own_out]
+    conv_at = own_in + own_out
+    conv_end = conv_at + tap_rows * conv_own
+    conv_owned = packed[conv_at:conv_end].reshape(tap_rows, conv_own)
+    head_total = packed[conv_end:packed_size].reshape(3, heads)
 
     prenorm_new, prenorm_mom, prenorm_sq = adam_update(
         prenorm, prenorm_first, prenorm_second, prenorm_owned, rate_vector, 0.0

time: 845 us -> 521 us (0.62)
  waiting for transfers between devices: 590 us -> 111 us
  Pallas kernels: 93 us -> 285 us
  matrix products: 72.8 us -> 47.1 us
    psum x2 -> x0, waiting for transfers between devices: 363 us -> none  [the longest x1 258 us: on_device(): lax.psum(jnp.dot(normed_turned, gate_all, preferred_element_type=f32), 's...]
    pallas_call x0 -> x1, Pallas kernels: none -> 193 us  [reduce_gradients(): pl.pallas_call(functools.partial(tail_kernel, sizes), out_shape=(shape((o...]
    all_gather x2 -> x0, waiting for transfers between devices: 115 us -> none  [the longest x1 72 us: on_device(): scan_all = lax.all_gather(scan_grad, 'dp', axis=0, tiled=True)]
    dot_general x3 -> x0, matrix products: 24.9 us -> none  [the longest x1 9.55 us: on_device(): jnp.dot(normed_turned, scan_all, preferred_element_type=f32)]
  transfers between devices with their start and end apart: 8 -> 4, of which waited for: 7 -> 3; matrix products, arithmetic and copies ran while one was open for 12% -> 11% of each run, Pallas kernels for 11% -> 18%
where the time goes in v3:
time: 521 us
  Pallas kernels  285 us (55%)
  waiting for transfers between devices  111 us (21%)
  matrix products  47.1 us (9%)
  other arithmetic  35.3 us (7%)
  local copies, waits for them, and re-layouts  17.3 us (3%)
  between operations  14.4 us (3%)
  blocking collectives  10.7 us (2%)
    pallas_call x1, Pallas kernels, reduce_gradients(): pl.pallas_call(functools.partial(tail_kernel, sizes), out_shape=(shape((o...  193 us
    pallas_call x1, Pallas kernels, scan_backward(): pl.pallas_call(functools.partial(backward_kernel, sizes), out_shape=(shap...  53.9 us
    all_gather x1, waiting for transfers between devices, on_device(): lax.all_gather(outproject.astype(bf16), 'dp', axis=0, tiled=True)  52.5 us
    all_gather x1, waiting for transfers between devices, on_device(): scan_matrix = lax.all_gather(in_low[:, inner:], 'dp', axis=0, tiled=True)  47.9 us
    pallas_call x1, Pallas kernels, scan_forward(): pl.pallas_call(functools.partial(forward_kernel, sizes), out_shape=(shape...  38.3 us
    dot_general x3, matrix products, mm(): lax.dot_general(a, b, (((ca,), (cb,)), ((), ())), preferred_element_type=...  23.7 us
    sub x6, other arithmetic, adam_update(): weight - step_rate * (moment_hat / (jnp.sqrt(square_hat) + adam_eps) + de...  19.7 us
    all_gather x1, blocking collectives, on_device(): small = lax.all_gather(small, 'dp', axis=0).astype(f32)  10.7 us
  transfers between devices with their start and end apart: 4, of which 3 were waited for; matrix products, arithmetic and copies ran while one was open for 11% of the time, Pallas kernels for 18%

profile of v3, /device:TPU:0, one launch (start us, length us, event | category | flops | bytes accessed | tf_op | source)
XLA Modules:
  0.0 521.1 jit_solution(6357578749773837912)
XLA Ops:
  7.2 2.7 convert_element_type.57
  9.9 1.2 slice.68
  11.2 1.2 slice.71
  12.4 2.9 convert_element_type.61
  15.4 0.5 all-gather.13.cloned.1.call-update
  16.0 0.1 concatenate.28
  16.1 0.1 concatenate.29
  16.2 10.7 %all-gather.1 = bf16[8,1,2656]{2,1,0:T(2,128)(2,1)S(1)} all-gather(bf16[1,1,2656]{2,1,0:T(2,128)(2,1)S(1)} %bitcast.69), channel_id=1, replica_groups=mesh['dp'=8,'seq'=4] {'dp'}, dimensions={0}, use_global_device_ids=true | all-gather | bytes 47808 | tf_op jit(solution)/shard_map/all_gather | solution.py:1017
  26.9 0.1 slice.70
  27.0 0.1 slice.72
  27.1 0.1 mul.320
  27.2 0.1 broadcast_in_dim.16
  27.3 0.1 broadcast_in_dim.17.skip_ref
  27.4 0.1 reshape.184
  27.5 0.1 copy.56
  27.5 0.1 reshape.185
  27.6 0.6 mul.328
  28.3 0.2 fusion.20
  28.5 0.2 fusion.27
  28.8 1.2 copy.57
  29.9 47.9 %all-gather.7.cloned.1.call-done = bf16[1536,3376]{1,0:T(8,128)(2,1)} async-done(((bf16[192,3376]{1,0:T(8,128)(2,1)}), bf16[1536,3376]{1,0:T(8,128)(2,1)}) %all-gather.7.cloned.1.call-update) | async-done | bytes 10371088 | tf_op jit(solution)/shard_map/all_gather | solution.py:1015
  77.9 7.1 %convolution_convert_fusion.u_ref = bf16[256,3376]{1,0:T(8,128)(2,1)S(1)} fusion(bf16[1536,3376]{1,0:T(8,128)(2,1)} %all-gather.7.cloned.1.call-done, bf16[1,256,1536]{2,1,0:T(8,128)(2,1)S(1)} %copy-done.15, f32[1536]{0:T(1024)S(1)} %mul.320, f32[256]{0:T(256)S(1)} %add_rsqrt_fusion.1), kind=kOutput, calls=%fused_computation.1 | convolution fusion | flops 2657431552 | bytes 12893184 | tf_op jit(solution)/shard_map/dot_general | solution.py:1032
  85.1 38.3 %shard_map.395 = (bf16[256,3072]{1,0:T(8,128)(2,1)S(1)}, f32[256,3072]{1,0:T(8,128)S(1)}, f32[24,128,128]{2,1,0:T(8,128)S(1)}, bf16[16,3328]{1,0:T(8,128)(2,1)S(...) custom-call(bf16[256,3376]{1,0:T(8,128)(2,1)S(1)} %convolution_convert_fusion.u_ref, ...), custom_call_target="tpu_custom_call" | custom-call | flops 4000000000 | bytes 10000000 | tf_op jit(solution)/shard_map/pallas_call | solution.py:506
  123.4 1.2 copy-done.1
  124.6 1.7 copy-done.4
  126.3 1.1 copy-done.6
  127.4 0.7 copy-done.8
  128.1 0.7 copy-done.10
  128.7 0.6 copy-done.12
  129.4 9.9 %all-gather.9.cloned.1.call-done = bf16[1536,3072]{1,0:T(8,128)(2,1)} async-done(((bf16[192,3072]{1,0:T(8,128)(2,1)}), bf16[1536,3072]{1,0:T(8,128)(2,1)}) %all-gather.9.cloned.1.call-update) | async-done | bytes 9437200 | tf_op jit(solution)/shard_map/all_gather | solution.py:1023
  139.2 8.8 %multiply_reduce_fusion.2 = (f32[256]{0:T(256)S(1)}, f32[256,3072]{1,0:T(8,128)}) fusion(bf16[256,3072]{1,0:T(8,128)(2,1)S(1)} %get-tuple-element.40, bf16[1536,3072]{1,0:T(8,128)(2,1)} %all-gather.9.cloned.1.call-done, bf16[1,256,1536]{2,1,0:T(8,128)(2,1)S(1)} %copy-done.15, f32[1536]{0:T(1024)S(1)} %mul.320, f32[256]{0:T(256)} %copy-done.27), kind=kOutput, calls=%fused_computation.16 | convolution fusion | flops 2423783168 | bytes 14950400 | tf_op jit(solution)/shard_map/dot_general | solution.py:1042
  148.0 52.5 %all-gather.11.cloned.1.call-done = bf16[3072,1536]{1,0:T(8,128)(2,1)} async-done(((bf16[384,1536]{1,0:T(8,128)(2,1)}), bf16[3072,1536]{1,0:T(8,128)(2,1)}) %all-gather.11.cloned.1.call-update) | async-done | bytes 9437200 | tf_op jit(solution)/shard_map/all_gather | solution.py:1024
  200.6 8.5 %multiply_reduce_fusion = (f32[3072]{0:T(1024)}, f32[256]{0:T(256)S(1)}, f32[256,3072]{1,0:T(8,128)S(1)}) fusion(f32[256]{0:T(256)S(1)} %add_rsqrt_fusion, bf16[256,3072]{1,0:T(8,128)(2,1)S(1)} %get-tuple-element.40, f32[256,3072]{1,0:T(8,128)} %get-tuple-element.83, f32[3072]{0:T(1024)} %mul.328, bf16[3072,1536]{1,0:T(8,128)(2,1)} %all-gather.11.cloned.1.call-done, ...), kind=kOutput, calls=%fused_computation.11 | convolution fusion | flops 2425352960 | bytes 18114560 | tf_op jit(solution)/shard_map/dot_general | solution.py:41
  209.1 4.5 fusion.3
  213.6 1.7 copy.61
  215.4 1.4 pad_maximum_fusion.turn_ref
  216.8 0.1 copy-done
  217.0 0.5 copy-done.2
  217.6 1.4 copy-done.7
  219.0 53.9 %shard_map.396 = (bf16[256,3584]{1,0:T(8,128)(2,1)S(1)}, f32[8,3328]{1,0:T(8,128)S(1)}, f32[8,128]{1,0:T(8,128)S(1)}, bf16[576,2048]{1,0:T(8,128)(2,1)S(1)}) custom-call(bf16[256,3376]{1,0:T(8,128)(2,1)S(1)} %copy-done.2, bf16[16,3328]{1,0:T(8,128)(2,1)S(1)} %copy-done.13, f32[256,128]{1,0:T(8,128)S(1)} %pad_convert_fusion.rate_ref, ...), custom_call_target="tpu_custom_call" | custom-call | flops 6000000000 | bytes 20000000 | tf_op jit(solution)/shard_map/pallas_call | solution.py:539
  273.0 9.8 %fusion.11 = f32[256,1536]{1,0:T(8,128)} fusion(bf16[1536,3376]{1,0:T(8,128)(2,1)} %all-gather.7.cloned.1.call-done, bf16[256,3584]{1,0:T(8,128)(2,1)S(1)} %get-tuple-element.47.scan_ref), kind=kOutput, calls=%fused_computation.32 | convolution fusion | flops 2654994432 | bytes 13713408 | tf_op jit(solution)/shard_map/dot_general | solution.py:41
  282.8 5.5 %fusion.19 = (f32[1536]{0:T(1024)S(1)}, f32[256]{0:T(256)S(1)}, f32[256,1536]{1,0:T(8,128)}) fusion(bf16[1,256,1536]{2,1,0:T(8,128)(2,1)S(1)} %copy-done.16, f32[256]{0:T(256)S(1)} %copy-done.28, f32[1536]{0:T(1024)S(1)} %mul.320, f32[256,1536]{1,0:T(8,128)} %fusion.11, bf16[256,3072]{1,0:T(8,128)(2,1)S(1)} %get-tuple-element.79.gate_ref, ...), kind=kOutput, calls=%fused_computation.40 | convolution fusion | flops 2419063040 | bytes 14956544 | tf_op jit(solution)/shard_map/dot_general | solution.py:41
  288.3 0.1 reshape.191
  288.3 0.1 reshape.193
  288.4 0.1 copy.67
  288.5 0.1 reshape.194
  288.6 0.1 reshape.195
  288.7 0.1 reduce_sum.71
  288.9 0.1 broadcast_in_dim.18
  288.9 0.1 concatenate.32
  289.1 192.9 %shard_map.397 = (f32[192,6656]{1,0:T(8,128)}, f32[384,1536]{1,0:T(8,128)}, f32[8,384]{1,0:T(8,128)S(1)}, bf16[26,2,4,256,256]{4,3,2,1,0:T(8,128)(2,1)}) custom-call(bf16[576,2048]{1,0:T(8,128)(2,1)} %copy-done.5, bf16[2048,1536]{1,0:T(8,128)(2,1)} %bitcast.73, bf16[256,3072]{1,0:T(8,128)(2,1)S(1)} %get-tuple-element.79.gate_ref, ...), custom_call_target="tpu_custom_call" | custom-call | flops 20000000000 | bytes 200000000 | tf_op jit(solution)/shard_map/pallas_call | solution.py:935
  482.1 0.1 slice.74
  482.2 0.1 slice.75
  482.2 0.1 reshape.198
  482.3 0.1 reshape.199
  482.4 3.4 fusion.18
  485.9 0.6 multiply_subtract_fusion.5
  486.5 0.7 multiply_subtract_fusion.3
  487.2 6.8 %multiply_subtract_fusion.1 = (f32[384,1536]{1,0:T(8,128)}, f32[384,1536]{1,0:T(8,128)}, f32[384,1536]{1,0:T(8,128)}) fusion(f32[384,1536]{1,0:T(8,128)} %param.27, f32[384,1536]{1,0:T(8,128)S(1)} %copy-done.14, f32[384,1536]{1,0:T(8,128)S(1)} %copy-done.20, f32[384,1536]{1,0:T(8,128)} %param.39), kind=kLoop, calls=%fused_computation.30 | loop fusion | flops 8847360 | bytes 16515072 | tf_op jit(solution)/shard_map/sub | solution.py:34
  494.0 10.4 %multiply_subtract_fusion = (f32[192,6448]{1,0:T(8,128)}, f32[192,6448]{1,0:T(8,128)}, f32[192,6448]{1,0:T(8,128)}, f32[192,6448]{1,0:T(8,128)}) fusion(f32[192,6448]{1,0:T(8,128)S(1)} %bitcast.57, f32[192,6448]{1,0:T(8,128)S(1)} %bitcast.61, f32[192,6448]{1,0:T(8,128)} %param.35, f32[192,6656]{1,0:T(8,128)} %get-tuple-element.52), kind=kLoop, calls=%fused_computation.3 | loop fusion | flops 18570240 | bytes 39616512 | tf_op jit(solution)/shard_map/sub | solution.py:34
  504.4 0.6 multiply_subtract_fusion.2
  505.1 0.6 multiply_subtract_fusion.4
  505.7 7.4 %fusion.5 = f32[1,256,1536]{2,1,0:T(8,128)} fusion(bf16[256,3072]{1,0:T(8,128)(2,1)S(1)} %copy-done.17, bf16[3072,1536]{1,0:T(8,128)(2,1)} %all-gather.11.cloned.1.call-done, bf16[1,256,1536]{2,1,0:T(8,128)(2,1)S(1)} %copy-done.16), kind=kOutput, calls=%fused_computation.21 | convolution fusion | flops 2416705536 | bytes 13369344 | tf_op jit(solution)/shard_map/dot_general | solution.py:1050
  513.1 1.4 copy.71
  (126 shorter events, 0.7 us)
Async XLA Ops:
  7.2 70.7 %all-gather.7.cloned.1.call-start = ((), (), s32[]{:S(2)}) async-start(), calls=%async_computation | async-start | bytes 11943936 | tf_op jit(solution)/shard_map/all_gather | solution.py:1015
  11.1 128.1 %all-gather.9.cloned.1.call-start = ((), (), s32[]{:S(2)}) async-start(), calls=%async_computation.1 | async-start | bytes 10616832 | tf_op jit(solution)/shard_map/all_gather | solution.py:1023
  12.3 3.6 copy-start.39
  12.3 3.6 copy-start.32
  12.3 3.6 copy-start.22
  12.3 14.8 %copy-start.29 = (f32[3,48]{1,0:T(4,128)S(1)}, f32[3,48]{1,0:T(4,128)}, u32[]{:S(2)}) copy-start(f32[3,48]{1,0:T(4,128)} %param.25) | copy-start | bytes 1732
  12.4 15.9 %copy-start.15 = (bf16[1,256,1536]{2,1,0:T(8,128)(2,1)S(1)}, bf16[1,256,1536]{2,1,0:T(8,128)(2,1)}, u32[]{:S(2)}) copy-start(bf16[1,256,1536]{2,1,0:T(8,128)(2,1)} %param.20) | copy-start | bytes 2359300
  12.4 188.2 %all-gather.11.cloned.1.call-start = ((), (), s32[]{:S(2)}) async-start(), calls=%async_computation.2 | async-start | bytes 10616832 | tf_op jit(solution)/shard_map/all_gather | solution.py:1024
  15.3 273.8 %all-gather.13.cloned.1.call-start = ((), (), s32[]{:S(2)}) async-start(), calls=%async_computation.3 | async-start | bytes 7077888 | tf_op jit(solution)/shard_map/all_gather | solution.py:1028
  28.5 56.5 %copy-start.27 = (f32[256]{0:T(256)}, f32[256]{0:T(256)S(1)}, u32[]{:S(2)}) copy-start(f32[256]{0:T(256)S(1)} %add_rsqrt_fusion.1) | copy-start | bytes 3076
  123.4 1.2 copy-start.1
  124.6 1.7 copy-start.4
  126.3 1.1 copy-start.6
  127.4 0.7 copy-start.8
  128.1 0.7 copy-start.10
  128.7 0.6 copy-start.12
  139.2 61.3 %copy-start.19 = (bf16[1,256,1536]{2,1,0:T(8,128)(2,1)S(1)}, bf16[1,256,1536]{2,1,0:T(8,128)(2,1)}, u32[]{:S(2)}) copy-start(bf16[1,256,1536]{2,1,0:T(8,128)(2,1)} %param.21) | copy-start | bytes 2359300
  148.0 61.1 %copy-start.34 = (f32[256]{0:T(256)}, f32[256]{0:T(256)S(1)}, u32[]{:S(2)}) copy-start(f32[256]{0:T(256)S(1)} %add_rsqrt_fusion) | copy-start | bytes 3076
  200.5 8.5 %copy-start.18 = (f32[256,3072]{1,0:T(8,128)S(1)}, f32[256,3072]{1,0:T(8,128)}, u32[]{:S(2)}) copy-start(f32[256,3072]{1,0:T(8,128)} %get-tuple-element.83) | copy-start | bytes 9437188
  200.6 8.5 %copy-start.23 = (f32[3072]{0:T(1024)S(1)}, f32[3072]{0:T(1024)}, u32[]{:S(2)}) copy-start(f32[3072]{0:T(1024)} %mul.328) | copy-start | bytes 36868
  215.3 1.6 copy-start
  215.3 2.2 copy-start.2
  215.4 2.2 copy-start.9
  215.4 2.2 copy-start.11
  215.4 2.2 copy-start.13
  217.6 1.4 copy-start.7
  219.0 63.8 %slice-start.4 = ((s8[9437184]{0:T(1024)(128)(4,1)}), s8[1048576]{0:T(1024)(128)(4,1)S(1)}, s32[]{:S(2)}) async-start(s8[9437184]{0:T(1024)(128)(4,1)} %bitcast.71), calls=%async_computation.8 | async-start | bytes 2097152
  219.0 63.8 %slice-start.5 = ((s8[9437184]{0:T(1024)(128)(4,1)}), s8[4194304]{0:T(1024)(128)(4,1)S(1)}, s32[]{:S(2)}) async-start(s8[9437184]{0:T(1024)(128)(4,1)} %bitcast.71), calls=%async_computation.9 | async-start | bytes 8388608
  272.9 9.8 %copy-start.3 = (bf16[256,3584]{1,0:T(8,128)(2,1)}, bf16[256,3584]{1,0:T(8,128)(2,1)S(1)}, u32[]{:S(2)}) copy-start(bf16[256,3584]{1,0:T(8,128)(2,1)S(1)} %get-tuple-element.47.scan_ref) | copy-start | bytes 5505028
  272.9 9.8 %copy-start.5 = (bf16[576,2048]{1,0:T(8,128)(2,1)}, bf16[576,2048]{1,0:T(8,128)(2,1)S(1)}, u32[]{:S(2)}) copy-start(bf16[576,2048]{1,0:T(8,128)(2,1)S(1)} %get-tuple-element.48.turned_ref) | copy-start | bytes 7077892
  272.9 9.8 %copy-start.16 = (bf16[1,256,1536]{2,1,0:T(8,128)(2,1)S(1)}, bf16[1,256,1536]{2,1,0:T(8,128)(2,1)}, u32[]{:S(2)}) copy-start(bf16[1,256,1536]{2,1,0:T(8,128)(2,1)} %param.20) | copy-start | bytes 2359300
  272.9 9.8 %copy-start.28 = (f32[256]{0:T(256)S(1)}, f32[256]{0:T(256)}, u32[]{:S(2)}) copy-start(f32[256]{0:T(256)} %copy-done.27) | copy-start | bytes 3076
  272.9 9.8 %slice-start.6 = ((s8[9437184]{0:T(1024)(128)(4,1)}), s8[4194304]{0:T(1024)(128)(4,1)S(1)}, s32[]{:S(2)}) async-start(s8[9437184]{0:T(1024)(128)(4,1)} %bitcast.71), calls=%async_computation.10 | async-start | bytes 8388608
  282.8 5.6 %copy-start.26 = (f32[3072]{0:T(1024)S(1)}, f32[3072]{0:T(1024)}, u32[]{:S(2)}) copy-start(f32[3072]{0:T(1024)} %get-tuple-element.54) | copy-start | bytes 36868
  482.0 3.8 copy-start.40
  482.0 3.8 copy-start.41
  482.0 3.8 copy-start.42
  482.0 4.4 copy-start.33
  482.1 4.4 copy-start.37
  482.1 4.4 copy-start.38
  482.1 5.0 copy-start.14
  482.3 22.1 %copy-start.21 = (f32[5,416]{1,0:T(8,128)}, f32[5,416]{1,0:T(8,128)S(1)}, u32[]{:S(2)}) copy-start(f32[5,416]{1,0:T(8,128)S(1)} %reshape.198) | copy-start | bytes 24964
  482.4 22.7 %copy-start.31 = (f32[3,48]{1,0:T(4,128)}, f32[3,48]{1,0:T(4,128)S(1)}, u32[]{:S(2)}) copy-start(f32[3,48]{1,0:T(4,128)S(1)} %reshape.199) | copy-start | bytes 1732
  482.4 4.7 copy-start.20
  482.4 11.5 %slice-start = ((s8[5013504]{0:T(1024)(128)(4,1)}), s8[4194304]{0:T(1024)(128)(4,1)S(1)}, s32[]{:S(2)}) async-start(s8[5013504]{0:T(1024)(128)(4,1)} %bitcast.56), calls=%async_computation.4 | async-start | bytes 8388608
  482.4 11.5 %slice-start.2 = ((s8[5013504]{0:T(1024)(128)(4,1)}), s8[4194304]{0:T(1024)(128)(4,1)S(1)}, s32[]{:S(2)}) async-start(s8[5013504]{0:T(1024)(128)(4,1)} %bitcast.60), calls=%async_computation.6 | async-start | bytes 8388608
  487.1 6.8 %slice-start.1 = ((s8[5013504]{0:T(1024)(128)(4,1)}), s8[819200]{0:T(1024)(128)(4,1)S(1)}, s32[]{:S(2)}) async-start(s8[5013504]{0:T(1024)(128)(4,1)} %bitcast.56), calls=%async_computation.5 | async-start | bytes 1638400
  487.1 6.8 %slice-start.3 = ((s8[5013504]{0:T(1024)(128)(4,1)}), s8[819200]{0:T(1024)(128)(4,1)S(1)}, s32[]{:S(2)}) async-start(s8[5013504]{0:T(1024)(128)(4,1)} %bitcast.60), calls=%async_computation.7 | async-start | bytes 1638400
  494.0 10.5 %copy-start.24 = (f32[5,416]{1,0:T(8,128)S(1)}, f32[5,416]{1,0:T(8,128)}, u32[]{:S(2)}) copy-start(f32[5,416]{1,0:T(8,128)} %param.30) | copy-start | bytes 24964
  494.0 10.4 %copy-start.25 = (f32[5,416]{1,0:T(8,128)S(1)}, f32[5,416]{1,0:T(8,128)}, u32[]{:S(2)}) copy-start(f32[5,416]{1,0:T(8,128)} %param.36) | copy-start | bytes 24964
  494.0 11.1 %copy-start.30 = (f32[3,48]{1,0:T(4,128)S(1)}, f32[3,48]{1,0:T(4,128)}, u32[]{:S(2)}) copy-start(f32[3,48]{1,0:T(4,128)} %param.25) | copy-start | bytes 1732
  494.0 11.1 %copy-start.35 = (f32[3,48]{1,0:T(4,128)S(1)}, f32[3,48]{1,0:T(4,128)}, u32[]{:S(2)}) copy-start(f32[3,48]{1,0:T(4,128)} %param.31) | copy-start | bytes 1732
  494.0 11.1 %copy-start.36 = (f32[3,48]{1,0:T(4,128)S(1)}, f32[3,48]{1,0:T(4,128)}, u32[]{:S(2)}) copy-start(f32[3,48]{1,0:T(4,128)} %param.37) | copy-start | bytes 1732
  494.0 11.7 %copy-start.17 = (bf16[256,3072]{1,0:T(8,128)(2,1)S(1)}, bf16[256,3072]{1,0:T(8,128)(2,1)}, u32[]{:S(2)}) copy-start(bf16[256,3072]{1,0:T(8,128)(2,1)} %get-tuple-element.81) | copy-start | bytes 4718596
Sparse Core Ops, SparseCore 0:
  11.2 66.5 all-gather.6
  80.3 58.8 all-gather.8
  141.7 58.8 all-gather.10
  202.3 66.6 all-gather.12

commit v4 on v3

--- a/solution.py
+++ b/solution.py
@@ -11,6 +11,7 @@
 LANES = 128
 HALO = 16
 WIDE = 256
+HEIGHT = 32
 
 norm_eps = 1e-05
 beta_moment = 0.9
@@ -120,35 +121,237 @@
     return at * (1 - turned) + turned * (3 * half - 1 - at)
 
 
-def forward_kernel(
+def front_kernel(
     sizes,
-    u_ref,
-    rate_ref,
+    in_shard_ref,
+    out_shard_ref,
+    small_ref,
+    hidden_ref,
+    cot_ref,
     heads_ref,
     skip_ref,
-    taps_ref,
-    mixer_ref,
+    u_ref,
     ypre_ref,
     enter_ref,
     halo_ref,
     step_ref,
     cum_ref,
     cumt_ref,
+    taps_ref,
+    pre_scale_ref,
+    dy_ref,
+    gate_grad_ref,
+    post_grad_ref,
+    post_ref,
+    normed_t_ref,
+    post_t_ref,
+    token_ref,
+    scan_all_ref,
+    gate_all_ref,
+    out_all_ref,
+    in_wide_ref,
+    out_wide_ref,
+    scan_shard_ref,
+    gate_shard_ref,
+    out_low_ref,
+    small_all_ref,
+    post_scale_ref,
+    normed_ref,
+    weights_ref,
+    out_weights_ref,
     conv_ref,
     score_ref,
     leave_ref,
+    mixer_ref,
+    gate_ref,
+    gated_ref,
+    dpost_ref,
     send_sem,
     recv_sem,
     halo_sem,
+    small_send,
+    small_recv,
+    wide_sem,
+    weight_sem,
+    *ring_sems,
 ):
     rows, inner, tiles, per_tile = sizes
     conv_width = inner + 2 * N
+    own_in = in_shard_ref.shape[0]
+    own_out, model_width = out_shard_ref.shape
+    scan_width = in_shard_ref.shape[1] - inner
     rank = lax.axis_index("seq")
     last = lax.axis_size("seq") - 1
+    me = lax.axis_index("dp")
+    group = lax.axis_size("dp")
+    in_chunks = own_in // HEIGHT
+    out_height = 2 * HEIGHT
+    out_chunks = own_out // out_height
+
+    def wide_rows(chunk):
+        return pl.ds(pl.multiple_of(chunk * HEIGHT, HEIGHT), HEIGHT)
+
+    def in_wide(chunk):
+        some = wide_rows(chunk)
+        return pltpu.make_async_copy(
+            in_shard_ref.at[some, :], in_wide_ref.at[some, :], wide_sem.at[chunk]
+        )
+
+    out_wide = pltpu.make_async_copy(out_shard_ref, out_wide_ref, wide_sem.at[in_chunks])
+    for chunk in range(in_chunks):
+        in_wide(chunk).start()
+    out_wide.start()
     barrier = pltpu.get_barrier_semaphore()
     greet_seq(barrier, rank, last)
-    pl.semaphore_wait(barrier, seq_neighbours(rank, last))
+    greet_plane(barrier, me, group)
+    pl.semaphore_wait(barrier, seq_neighbours(rank, last) + group - 1)
     right = jnp.minimum(rank + 1, last)
+    left = jnp.maximum(rank - 1, 0)
+
+    def small_copy(i, peer, slot):
+        return plane_copy(
+            small_ref, small_all_ref.at[slot], small_send.at[i], small_recv.at[i], peer
+        )
+
+    for i in range(1, group):
+        small_copy(i, lax.rem(me + i, group), me).start()
+    small_all_ref[me] = small_ref[...]
+    scan_shard_ref[:, scan_width - scan_width % LANES :] = jnp.zeros(
+        (own_in, scan_shard_ref.shape[1] - scan_width + scan_width % LANES), bf16
+    )
+
+    def prepare_scan(chunk):
+        some = wide_rows(chunk)
+        in_wide(chunk).wait()
+        scan_shard_ref[some, 0:scan_width] = in_wide_ref[some, inner:].astype(bf16)
+
+    def prepare_gate(chunk):
+        some = wide_rows(chunk)
+        gate_shard_ref[some, :] = in_wide_ref[some, 0:inner].astype(bf16)
+
+    def prepare_out(chunk):
+        @pl.when(chunk == 0)
+        def _():
+            out_wide.wait()
+
+        some = pl.ds(pl.multiple_of(chunk * out_height, out_height), out_height)
+        out_low_ref[some, :] = out_wide_ref[some, :].astype(bf16)
+
+    scan_ring = weight_ring(scan_shard_ref, scan_all_ref, HEIGHT, ring_sems[0:5], prepare_scan)
+    gate_ring = weight_ring(gate_shard_ref, gate_all_ref, HEIGHT, ring_sems[5:10], prepare_gate)
+    out_ring = weight_ring(out_low_ref, out_all_ref, out_height, ring_sems[10:15], prepare_out)
+    spacing = 2
+    rings = (
+        (scan_ring, 0, in_chunks),
+        (gate_ring, in_chunks, in_chunks),
+        (out_ring, 2 * in_chunks, out_chunks),
+    )
+
+    def round_(step):
+        for ring, first, chunks in rings:
+            ring.round(step - first, chunks, spacing)
+
+    def rounds(first, end):
+        def one(step, carry):
+            round_(step)
+            return carry
+
+        lax.fori_loop(first, end, one, 0)
+
+    def complete(at):
+        ring, first, chunks = rings[at]
+        return first + chunks + spacing * ring.reach
+
+    def wait_pairs(at):
+        ring, _, chunks = rings[at]
+
+        def one(chunk, carry):
+            ring.wait_pair(chunk)
+            return carry
+
+        lax.fori_loop(0, chunks, one, 0)
+
+    rounds(0, 2)
+
+    for i in range(1, group):
+        small_copy(i, lax.rem(me + i, group), me).wait_send()
+        small_copy(i, me, lax.rem(me + group - i, group)).wait_recv()
+    conv_own = conv_width // group
+    taps_ref[...] = jnp.zeros_like(taps_ref)
+    for device in range(group):
+        small = small_all_ref[device].astype(f32)
+        pre_scale_ref[0:1, device * own_in : (device + 1) * own_in] = small[0:1, 0:own_in]
+        taps_ref[0:5, device * conv_own : (device + 1) * conv_own] = small[1:6, 0:conv_own]
+        post_scale_ref[0:1, device * own_out : (device + 1) * own_out] = small[6:7, 0:own_out]
+    pre_scale_ref[1:8, :] = jnp.zeros((7, model_width), f32)
+    token_ref[...] = jnp.zeros_like(token_ref)
+
+    def norm(at, carry):
+        some = pl.ds(pl.multiple_of(at * HEIGHT, HEIGHT), HEIGHT)
+        hidden = hidden_ref[some, :].astype(f32)
+        root = lax.rsqrt(jnp.mean(hidden * hidden, axis=-1, keepdims=True) + norm_eps)
+        normed_ref[some, :] = (hidden * root * pre_scale_ref[0:1, :]).astype(bf16)
+        return carry
+
+    lax.fori_loop(0, rows // HEIGHT, norm, 0)
+
+    def turn(source_ref, target_ref):
+        def one(at, carry):
+            cols = pl.ds(pl.multiple_of(at * LANES, LANES), LANES)
+            target_ref[cols, :] = source_ref[:, cols].astype(f32).T.astype(bf16)
+            return carry
+
+        lax.fori_loop(0, source_ref.shape[1] // LANES, one, 0)
+
+    turn(normed_ref, normed_t_ref)
+    rounds(2, complete(0))
+    wait_pairs(0)
+
+    def weight_copy(all_ref, at, width):
+        slot = lax.rem(at, 2)
+        cols = pl.ds(pl.multiple_of(at * WIDE, WIDE), width)
+        return pltpu.make_async_copy(
+            all_ref.at[:, :, :, cols],
+            weights_ref.at[slot, :, :, :, pl.ds(0, width)],
+            weight_sem.at[slot],
+        )
+
+    def columns(all_ref, action):
+        total = all_ref.shape[3]
+        full = total // WIDE
+        rest = total % WIDE
+
+        def fetch(at, act):
+            @pl.when(at < full)
+            def _():
+                act(weight_copy(all_ref, at, WIDE))
+
+            if rest:
+
+                @pl.when(at == full)
+                def _():
+                    act(weight_copy(all_ref, at, rest))
+
+        fetch(0, lambda copy: copy.start())
+
+        def one(at, carry):
+            fetch(at + 1, lambda copy: copy.start())
+            fetch(at, lambda copy: copy.wait())
+            weights = weights_ref[lax.rem(at, 2)].reshape(model_width, WIDE)
+            action(at, WIDE, mm(normed_ref[...], weights, 1, 0))
+            return carry
+
+        lax.fori_loop(0, full, one, 0)
+        if rest:
+            fetch(full, lambda copy: copy.wait())
+            weights = weights_ref[full % 2, :, :, :, 0:rest].reshape(model_width, rest)
+            action(full, rest, mm(normed_ref[...], weights, 1, 0))
+
+    def keep_scan(at, width, product):
+        cols = pl.ds(at * WIDE if isinstance(at, int) else pl.multiple_of(at * WIDE, WIDE), width)
+        u_ref[:, cols] = product.astype(bf16)
+
+    columns(scan_all_ref, keep_scan)
     halo_copy = seq_copy(
         u_ref.at[pl.ds(rows - HALO, HALO), pl.ds(0, conv_width)],
         halo_ref,
@@ -161,7 +364,8 @@
     def _():
         halo_copy.start()
 
-    step = jax.nn.softplus(rate_ref[...] + heads_ref[0:1, :])
+    round_(complete(0))
+    step = jax.nn.softplus(u_ref[:, conv_width:].astype(f32) + heads_ref[0:1, :])
     decay = -step * jnp.exp(heads_ref[1:2, :])
     lower = (iota((rows, rows), 0) >= iota((rows, rows), 1)).astype(f32).astype(bf16)
     cum = sum(mm(lower, part, 1, 0) for part in thirds(decay))
@@ -230,9 +434,92 @@
             result = result + mm3(halves(kernel), halves(jnp.where(own, x, 0.0)), 1, 0)
         ypre_ref[:, cols] = result
         mixer_ref[:, cols] = (result + skip_ref[0:1, cols] * values).astype(bf16)
+
+        @pl.when(lax.rem(tile, pace) == pace - 1)
+        def _():
+            round_(in_loop + tile // pace)
+
         return carry
 
+    in_loop = complete(0) + 1
+    pace = 4
     lax.fori_loop(0, tiles, one, 0)
+    at_round = in_loop + tiles // pace
+    rounds(at_round, max(at_round, complete(1)))
+    at_round = max(at_round, complete(1))
+    wait_pairs(1)
+
+    gated_ref_sum = score_ref
+
+    def keep_gate(at, width, product):
+        cols = pl.ds(at * WIDE if isinstance(at, int) else pl.multiple_of(at * WIDE, WIDE), width)
+        gated = mixer_ref[:, cols].astype(f32) * (product * jax.nn.sigmoid(product))
+        gate_ref[:, cols] = product
+        gated_ref[:, cols] = gated
+        square = gated * gated
+        total = square[:, 0:LANES]
+        for part in range(1, width // LANES):
+            total = total + square[:, part * LANES : (part + 1) * LANES]
+        gated_ref_sum[:, 0:LANES] += total
+
+    gated_ref_sum[:, 0:LANES] = jnp.zeros((rows, LANES), f32)
+    columns(gate_all_ref, keep_gate)
+    end_round = complete(2)
+    rounds(at_round, min(at_round + 1, end_round))
+    at_round = min(at_round + 1, end_round)
+    root = lax.rsqrt(
+        jnp.sum(gated_ref_sum[:, 0:LANES], axis=-1, keepdims=True) / inner + norm_eps
+    )
+
+    def keep_post(at, carry):
+        cols = pl.ds(pl.multiple_of(at * WIDE, WIDE), WIDE)
+        whitened = gated_ref[:, cols] * root
+        gated_ref[:, cols] = whitened
+        post_ref[:, cols] = (whitened * post_scale_ref[0:1, cols]).astype(bf16)
+        return carry
+
+    lax.fori_loop(0, inner // WIDE, keep_post, 0)
+    turn(post_ref, post_t_ref)
+    rounds(at_round, end_round)
+    wait_pairs(2)
+
+    span = 2 * own_out
+
+    def out_copy(chip):
+        slot = chip % 2
+        return pltpu.make_async_copy(
+            out_all_ref.at[chip], out_weights_ref.at[slot], weight_sem.at[slot]
+        )
+
+    out_copy(0).start()
+    overlap = jnp.zeros((rows, LANES), f32)
+    for chip in range(group // 2):
+        if chip + 1 < group // 2:
+            out_copy(chip + 1).start()
+        out_copy(chip).wait()
+        cols = slice(chip * span, (chip + 1) * span)
+        weights = out_weights_ref[chip % 2].reshape(span, model_width)
+        dpost = mm(cot_ref[...], weights, 1, 1)
+        dpost_ref[:, cols] = dpost
+        pulled = dpost * gated_ref[:, cols]
+        post_grad_ref[0:1, cols] = jnp.sum(pulled, axis=0, keepdims=True)
+        pulled = pulled * post_scale_ref[0:1, cols]
+        for part in range(span // LANES):
+            overlap = overlap + pulled[:, part * LANES : (part + 1) * LANES]
+    mean = jnp.sum(overlap, axis=-1, keepdims=True) / inner
+
+    def keep_back(at, carry):
+        cols = pl.ds(pl.multiple_of(at * WIDE, WIDE), WIDE)
+        gate = gate_ref[:, cols]
+        sig = jax.nn.sigmoid(gate)
+        dgated = root * (dpost_ref[:, cols] * post_scale_ref[0:1, cols] - gated_ref[:, cols] * mean)
+        dy_ref[:, cols] = (dgated * (gate * sig)).astype(bf16)
+        gate_grad_ref[:, cols] = (
+            dgated * mixer_ref[:, cols].astype(f32) * sig * (1.0 + gate * (1.0 - sig))
+        ).astype(bf16)
+        return carry
+
+    lax.fori_loop(0, inner // WIDE, keep_back, 0)
 
     @pl.when(rank < last)
     def _():
@@ -243,13 +530,20 @@
             return carry
 
         lax.fori_loop(0, tiles, drain, 0)
+
+    for ring, _, chunks in rings:
+
+        def finish(chunk, carry, ring=ring):
+            ring.finish(chunk)
+            return carry
+
+        lax.fori_loop(0, chunks, finish, 0)
 
 
 def backward_kernel(
     sizes,
     u_ref,
     halo_ref,
-    rate_ref,
     step_ref,
     cum_ref,
     cumt_ref,
@@ -259,7 +553,8 @@
     dy_ref,
     ypre_ref,
     enter_ref,
-    turn_ref,
+    normed_t_ref,
+    post_t_ref,
     dproj_ref,
     conv_grad_ref,
     head_grad_ref,
@@ -292,24 +587,36 @@
     greet_plane(barrier, me, group)
     pl.semaphore_wait(barrier, seq_neighbours(rank, last) + group - 1)
 
-    def landing(device):
-        return turned_ref.at[:, pl.ds(pl.multiple_of(slot_of(device, group) * rows, rows), rows)]
-
-    def turn(i):
-        peer = lax.rem(me + i, group)
-        return pltpu.make_async_remote_copy(
-            src_ref=turn_ref.at[peer],
-            dst_ref=landing(me),
-            send_sem=turn_send.at[i],
-            recv_sem=turn_recv.at[i],
-            device_id={"dp": peer},
-            device_id_type=MESH,
+    own_in = normed_t_ref.shape[0] // group
+    own_out = post_t_ref.shape[0] // group
+    turns = ((normed_t_ref, 0, own_in), (post_t_ref, own_in, own_out))
+
+    def landing(device, which):
+        _, first, height = turns[which]
+        cols = pl.ds(pl.multiple_of(slot_of(device, group) * rows, rows), rows)
+        return turned_ref.at[pl.ds(first, height), cols]
+
+    def leaving(device, which):
+        source, _, height = turns[which]
+        return source.at[pl.ds(pl.multiple_of(device * height, height), height), :]
+
+    def turn(i, which, peer, source):
+        return plane_copy(
+            leaving(peer, which),
+            landing(source, which),
+            turn_send.at[i, which],
+            turn_recv.at[i, which],
+            peer,
         )
 
-    for i in range(1, group):
-        turn(i).start()
-    own_copy = pltpu.make_async_copy(turn_ref.at[me], landing(me), own_sem)
-    own_copy.start()
+    own_copies = [
+        pltpu.make_async_copy(leaving(me, which), landing(me, which), own_sem.at[which])
+        for which in range(2)
+    ]
+    for which in range(2):
+        for i in range(1, group):
+            turn(i, which, lax.rem(me + i, group), me).start()
+        own_copies[which].start()
 
     left = jnp.maximum(rank - 1, 0)
     cum = cum_ref[...]
@@ -438,7 +745,9 @@
     upper = (iota((rows, rows), 1) >= iota((rows, rows), 0)).astype(f32).astype(bf16)
     ddecay = sum(mm(upper, part, 1, 0) for part in thirds(dcum_ref[...]))
     exp_rate = jnp.exp(heads_ref[1:2, :])
-    drate = (dstep_ref[...] - ddecay * exp_rate) * jax.nn.sigmoid(rate_ref[...] + heads_ref[0:1, :])
+    drate = (dstep_ref[...] - ddecay * exp_rate) * jax.nn.sigmoid(
+        u_ref[:, conv_width:].astype(f32) + heads_ref[0:1, :]
+    )
     head_grad_ref[...] = jnp.concatenate(
         [
             jnp.sum(drate, axis=0, keepdims=True),
@@ -481,61 +790,101 @@
 
         lax.fori_loop(0, tiles, drain, 0)
 
-    own_copy.wait()
-    for i in range(1, group):
-        turn(i).wait_send()
-        origin = lax.rem(me + group - i, group)
-        pltpu.make_async_remote_copy(
-            src_ref=turn_ref.at[origin],
-            dst_ref=landing(origin),
-            send_sem=turn_send.at[i],
-            recv_sem=turn_recv.at[i],
-            device_id={"dp": origin},
-            device_id_type=MESH,
-        ).wait_recv()
+    for which in range(2):
+        own_copies[which].wait()
+        for i in range(1, group):
+            turn(i, which, lax.rem(me + i, group), me).wait_send()
+            origin = lax.rem(me + group - i, group)
+            turn(i, which, origin, origin).wait_recv()
 
 
 def vmem(count):
     return [pl.BlockSpec(memory_space=pltpu.VMEM)] * count
 
 
-def scan_forward(u, rate, heads, skip, taps, sizes):
+def front(in_shard, out_shard, small, hidden, cot, heads, skip, sizes):
     rows, inner, tiles, _ = sizes
     conv_width = inner + 2 * N
     shape = jax.ShapeDtypeStruct
+    group = lax.axis_size("dp")
+    own_in, proj_width = in_shard.shape
+    own_out, model_width = out_shard.shape
+    scan_width = -(-(proj_width - inner) // LANES) * LANES
+    in_chunks = own_in // HEIGHT
+    out_chunks = own_out // (2 * HEIGHT)
+    anywhere = pl.BlockSpec(memory_space=pl.ANY)
+    dma = pltpu.SemaphoreType.DMA
     return pl.pallas_call(
-        functools.partial(forward_kernel, sizes),
+        functools.partial(front_kernel, sizes),
         out_shape=(
-            shape((rows, inner), bf16),
+            shape((rows, scan_width), bf16),
             shape((rows, inner), f32),
             shape((tiles, N, LANES), f32),
             shape((HALO, conv_width), bf16),
             shape((rows, LANES), f32),
             shape((rows, LANES), f32),
             shape((LANES, rows), f32),
+            shape((8, conv_width), f32),
+            shape((8, model_width), f32),
+            shape((rows, inner), bf16),
+            shape((rows, inner), bf16),
+            shape((1, inner), f32),
+            shape((rows, inner), bf16),
+            shape((model_width, rows), bf16),
+            shape((inner, rows), bf16),
+            shape((8, LANES), f32),
+            shape((group // 2, 2, own_in, scan_width), bf16),
+            shape((group // 2, 2, own_in, inner), bf16),
+            shape((group // 2, 2, own_out, model_width), bf16),
         ),
-        in_specs=vmem(5),
-        out_specs=tuple(vmem(7)),
+        in_specs=[anywhere] * 2 + vmem(5),
+        out_specs=tuple(vmem(16) + [anywhere] * 3),
         scratch_shapes=[
+            pltpu.VMEM(in_shard.shape, f32),
+            pltpu.VMEM(out_shard.shape, f32),
+            pltpu.VMEM((own_in, scan_width), bf16),
+            pltpu.VMEM((own_in, inner), bf16),
+            pltpu.VMEM((own_out, model_width), bf16),
+            pltpu.VMEM((group,) + small.shape, bf16),
+            pltpu.VMEM((1, inner), f32),
+            pltpu.VMEM((rows, model_width), bf16),
+            pltpu.VMEM((2, group // 2, 2, own_in, WIDE), bf16),
+            pltpu.VMEM((2, 2, own_out, model_width), bf16),
             pltpu.VMEM((HALO + rows, LANES), f32),
             pltpu.VMEM((rows, rows), f32),
             pltpu.VMEM((tiles, N, LANES), f32),
-            pltpu.SemaphoreType.DMA((tiles,)),
-            pltpu.SemaphoreType.DMA((tiles,)),
-            pltpu.SemaphoreType.DMA((2,)),
-        ],
+            pltpu.VMEM((rows, inner), bf16),
+            pltpu.VMEM((rows, inner), f32),
+            pltpu.VMEM((rows, inner), f32),
+            pltpu.VMEM((rows, inner), f32),
+            dma((tiles,)),
+            dma((tiles,)),
+            dma((2,)),
+            dma((group,)),
+            dma((group,)),
+            dma((in_chunks + 1,)),
+            dma((2,)),
+        ]
+        + PlaneRing.semaphores(in_chunks)
+        + PlaneRing.semaphores(in_chunks)
+        + PlaneRing.semaphores(out_chunks),
         compiler_params=pltpu.CompilerParams(
-            collective_id=1, has_side_effects=True, vmem_limit_bytes=40 * 2**20
+            collective_id=1, has_side_effects=True, vmem_limit_bytes=58 * 2**20
         ),
-        cost_estimate=pl.CostEstimate(flops=4 * 10**9, bytes_accessed=10**7, transcendentals=4 * 10**6),
-    )(u, rate, heads, skip, taps)
-
-
-def scan_backward(u, halo, rate, step, cum, cumt, heads, skip, taps, dy, ypre, enter, turn, sizes):
+        cost_estimate=pl.CostEstimate(
+            flops=10**10, bytes_accessed=10**8, transcendentals=4 * 10**6
+        ),
+    )(in_shard, out_shard, small, hidden, cot, heads, skip)
+
+
+def scan_backward(
+    u, halo, step, cum, cumt, heads, skip, taps, dy, ypre, enter, normed_t, post_t, sizes
+):
     rows, inner, tiles, _ = sizes
     conv_width = inner + 2 * N
     shape = jax.ShapeDtypeStruct
-    group, turn_rows, _ = turn.shape
+    group = lax.axis_size("dp")
+    turn_rows = (normed_t.shape[0] + post_t.shape[0]) // group
     return pl.pallas_call(
         functools.partial(backward_kernel, sizes),
         out_shape=(
@@ -544,7 +893,7 @@
             shape((8, LANES), f32),
             shape((turn_rows, group * rows), bf16),
         ),
-        in_specs=vmem(12) + [pl.BlockSpec(memory_space=pl.ANY)],
+        in_specs=vmem(11) + [pl.BlockSpec(memory_space=pl.ANY)] * 2,
         out_specs=tuple(vmem(3) + [pl.BlockSpec(memory_space=pl.ANY)]),
         scratch_shapes=[
             pltpu.VMEM((HALO + rows, LANES), f32),
@@ -560,15 +909,142 @@
             pltpu.SemaphoreType.DMA((tiles,)),
             pltpu.SemaphoreType.DMA((tiles,)),
             pltpu.SemaphoreType.DMA((2,)),
-            pltpu.SemaphoreType.DMA((group,)),
-            pltpu.SemaphoreType.DMA((group,)),
-            pltpu.SemaphoreType.DMA,
+            pltpu.SemaphoreType.DMA((group, 2)),
+            pltpu.SemaphoreType.DMA((group, 2)),
+            pltpu.SemaphoreType.DMA((2,)),
         ],
         compiler_params=pltpu.CompilerParams(
             collective_id=2, has_side_effects=True, vmem_limit_bytes=40 * 2**20
         ),
         cost_estimate=pl.CostEstimate(flops=6 * 10**9, bytes_accessed=2 * 10**7, transcendentals=4 * 10**6),
-    )(u, halo, rate, step, cum, cumt, heads, skip, taps, dy, ypre, enter, turn)
+    )(u, halo, step, cum, cumt, heads, skip, taps, dy, ypre, enter, normed_t, post_t)
+
+
+def plane_copy(src, dst, send, recv, to):
+    return pltpu.make_async_remote_copy(
+        src_ref=src,
+        dst_ref=dst,
+        send_sem=send,
+        recv_sem=recv,
+        device_id={"dp": to},
+        device_id_type=MESH,
+    )
+
+
+class PlaneRing:
+    def __init__(self, block, source, pair_block, sems, prepare=None):
+        group = lax.axis_size("dp")
+        me = lax.axis_index("dp")
+        self.block, self.source, self.pair_block = block, source, pair_block
+        self.prepare = prepare
+        self.ring_send, self.ring_recv, self.pair_send, self.pair_recv, self.own_sem = sems
+        self.chips = group // 2
+        self.reach = self.chips // 2
+        self.me = me
+        self.core = lax.rem(me, 2)
+        self.chip = me // 2
+        self.place = ring_place(self.chip, self.chips)
+
+    @staticmethod
+    def semaphores(chunks):
+        group = lax.axis_size("dp")
+        dma = pltpu.SemaphoreType.DMA
+        return [dma((chunks, group // 2)), dma((chunks, group // 2))] + [dma((chunks,))] * 3
+
+    def ring_chip(self, ahead):
+        return ring_place(lax.rem(self.place + ahead + self.chips, self.chips), self.chips)
+
+    def part(self, number, way):
+        return None if number < self.reach else (0 if way == 1 else 1)
+
+    def copy(self, chunk, number, way, origin, source=None):
+        block = self.block(chunk, origin, self.part(number, way))
+        at = 2 * (number - 1) + (0 if way == 1 else 1)
+        return plane_copy(
+            block if source is None else source,
+            block,
+            self.ring_send.at[chunk, at],
+            self.ring_recv.at[chunk, at],
+            2 * self.ring_chip(way) + self.core,
+        )
+
+    def hop(self, chunk, number, way, source=None):
+        return self.copy(chunk, number, way, self.ring_chip(-way * (number - 1)), source)
+
+    def hop_in(self, chunk, number, way):
+        return self.copy(chunk, number, way, self.ring_chip(-way * number))
+
+    def own_copy(self, chunk, source):
+        return pltpu.make_async_copy(
+            source, self.block(chunk, self.chip, None), self.own_sem.at[chunk]
+        )
+
+    def pair_copy(self, chunk, core):
+        block = self.pair_block(chunk, core)
+        return plane_copy(
+            block,
+            block,
+            self.pair_send.at[chunk],
+            self.pair_recv.at[chunk],
+            self.me + 1 - 2 * self.core,
+        )
+
+    def stage(self, chunk, number):
+        if number == 0:
+            if self.prepare is not None:
+                self.prepare(chunk)
+            self.source(chunk, None, lambda ref: self.own_copy(chunk, ref).start())
+            for way in (1, -1):
+                self.source(
+                    chunk,
+                    self.part(1, way),
+                    lambda ref, way=way: self.hop(chunk, 1, way, ref).start(),
+                )
+            return
+        for way in (1, -1):
+            self.hop_in(chunk, number, way).wait_recv()
+            if number < self.reach:
+                self.hop(chunk, number + 1, way).start()
+        if number == self.reach:
+            self.own_copy(chunk, self.block(chunk, self.chip, None)).wait()
+            self.pair_copy(chunk, self.core).start()
+
+    def wait_pair(self, chunk):
+        self.pair_copy(chunk, 1 - self.core).wait_recv()
+
+    def finish(self, chunk):
+        for number in range(1, self.reach + 1):
+            for way in (1, -1):
+                self.hop(chunk, number, way).wait_send()
+        self.pair_copy(chunk, self.core).wait_send()
+
+    def round(self, step, chunks, spacing):
+        for number in range(self.reach, -1, -1):
+            chunk = step - number * spacing
+
+            @pl.when((chunk >= 0) & (chunk < chunks))
+            def _(chunk=chunk, number=number):
+                self.stage(chunk, number)
+
+
+def weight_ring(shard_ref, all_ref, height, sems, prepare):
+    core = lax.rem(lax.axis_index("dp"), 2)
+
+    def rows_of(chunk, part):
+        size = height if part is None else height // 2
+        start = chunk * height + (0 if part is None else part * size)
+        return pl.ds(pl.multiple_of(start, size), size)
+
+    return PlaneRing(
+        lambda chunk, origin, part: all_ref.at[origin, core, rows_of(chunk, part), :],
+        lambda chunk, part, action: action(shard_ref.at[rows_of(chunk, part), :]),
+        lambda chunk, half: all_ref.at[:, half, rows_of(chunk, None), :],
+        sems,
+        prepare,
+    )
+
+
+HEIGHT = 32
 
 
 def tail_kernel(
@@ -578,19 +1054,29 @@
     gate_ref,
     scan_ref,
     small_ref,
+    hidden_ref,
+    own_cot_ref,
+    post_ref,
+    scale_ref,
+    gate_matrix_ref,
+    scan_matrix_ref,
+    out_matrix_ref,
     in_ref,
     out_ref,
     small_out_ref,
+    output_ref,
+    input_grad_ref,
     gathered_ref,
     value_ref,
     inbox_ref,
-    other_ref,
     total_ref,
     loaded_ref,
     small_value_ref,
     small_inbox_ref,
-    small_other_ref,
     small_all_ref,
+    weights_ref,
+    normed_grad_ref,
+    scale_grad_ref,
     up_send,
     inbox_recv,
     other_recv,
@@ -606,6 +1092,9 @@
     load_sem,
     small_send,
     small_recv,
+    scale_send,
+    scale_recv,
+    weight_sem,
 ):
     rows, own_in, out_steps, gate_steps, steps, root, lag, spacing = sizes
     chunks = steps - out_steps
@@ -616,8 +1105,6 @@
     chips = group // 2
     reach = chips // 2
     core = lax.rem(me, 2)
-    chip = me // 2
-    place = ring_place(chip, chips)
     barrier = pltpu.get_barrier_semaphore()
     greet_seq(barrier, rank, last)
     greet_plane(barrier, me, group)
@@ -625,57 +1112,36 @@
     left = jnp.maximum(rank - 1, 0)
     right = jnp.minimum(rank + 1, last)
 
-    def plane_copy(src, dst, send, recv, to):
-        return pltpu.make_async_remote_copy(
-            src_ref=src,
-            dst_ref=dst,
-            send_sem=send,
-            recv_sem=recv,
-            device_id={"dp": to},
-            device_id_type=MESH,
-        )
+    packed = small_ref.shape[2]
+    model_width = hidden_ref.shape[1]
 
     def small_copy(i, peer, slot):
         return plane_copy(
-            small_ref.at[peer], small_all_ref.at[slot], small_send.at[i], small_recv.at[i], peer
+            small_ref.at[peer],
+            small_all_ref.at[slot, :, pl.ds(0, packed)],
+            small_send.at[i],
+            small_recv.at[i],
+            peer,
+        )
+
+    def scale_copy(i, peer, slot):
+        return plane_copy(
+            scale_grad_ref,
+            small_all_ref.at[slot, :, pl.ds(packed, model_width)],
+            scale_send.at[i],
+            scale_recv.at[i],
+            peer,
         )
 
     for i in range(1, group):
         small_copy(i, lax.rem(me + i, group), me).start()
-    small_all_ref[me] = small_ref[me]
-
-    def ring_chip(ahead):
-        return ring_place(lax.rem(place + ahead + chips, chips), chips)
+    small_all_ref[me, :, 0:packed] = small_ref[me]
 
     def block(chunk, origin, part):
         ref = gathered_ref.at[chunk, core, origin]
         return ref if part is None else ref.at[pl.ds(part * (rows // 2), rows // 2), :]
 
-    def hop(chunk, number, way, source=None):
-        origin = ring_chip(-way * (number - 1))
-        part = None if number < reach else (0 if way == 1 else 1)
-        at = 2 * (number - 1) + (0 if way == 1 else 1)
-        return plane_copy(
-            block(chunk, origin, part) if source is None else source,
-            block(chunk, origin, part),
-            ring_send.at[chunk, at],
-            ring_recv.at[chunk, at],
-            2 * ring_chip(way) + core,
-        )
-
-    def hop_in(chunk, number, way):
-        origin = ring_chip(-way * number)
-        part = None if number < reach else (0 if way == 1 else 1)
-        at = 2 * (number - 1) + (0 if way == 1 else 1)
-        return plane_copy(
-            block(chunk, origin, part),
-            block(chunk, origin, part),
-            ring_send.at[chunk, at],
-            ring_recv.at[chunk, at],
-            2 * ring_chip(way) + core,
-        )
-
-    def own_source(chunk, part, action):
+    def source(chunk, part, action):
         part_rows = pl.ds(0, rows) if part is None else pl.ds(part * (rows // 2), rows // 2)
 
         @pl.when(chunk < gate_steps)
@@ -688,41 +1154,18 @@
             start = pl.multiple_of((chunk - gate_steps) * WIDE, WIDE)
             action(scan_ref.at[part_rows, pl.ds(start, WIDE)])
 
-    def own_copy(chunk, source):
-        return pltpu.make_async_copy(source, block(chunk, chip, None), own_sem.at[chunk])
-
-    def pair_copy(chunk, half):
-        return plane_copy(
-            gathered_ref.at[chunk, half],
-            gathered_ref.at[chunk, half],
-            pair_send.at[chunk],
-            pair_recv.at[chunk],
-            me + 1 - 2 * core,
-        )
+    ring = PlaneRing(
+        block,
+        source,
+        lambda chunk, half: gathered_ref.at[chunk, half],
+        (ring_send, ring_recv, pair_send, pair_recv, own_sem),
+    )
 
     def load_copy(chunk):
         slot = lax.rem(chunk, 2)
         return pltpu.make_async_copy(
             gathered_ref.at[chunk], loaded_ref.at[slot], load_sem.at[slot]
         )
-
-    def ring_stage(chunk, stage):
-        if stage == 0:
-            own_source(chunk, None, lambda source: own_copy(chunk, source).start())
-            for way in (1, -1):
-                part = None if reach > 1 else (0 if way == 1 else 1)
-                own_source(
-                    chunk, part, lambda source, way=way: hop(chunk, 1, way, source).start()
-                )
-        elif stage < reach:
-            for way in (1, -1):
-                hop_in(chunk, stage, way).wait_recv()
-                hop(chunk, stage + 1, way).start()
-        else:
-            for way in (1, -1):
-                hop_in(chunk, stage, way).wait_recv()
-            own_copy(chunk, block(chunk, chip, None)).wait()
-            pair_copy(chunk, core).start()
 
     def compute(step):
         @pl.when(step < out_steps)
@@ -748,10 +1191,110 @@
             arrived = loaded_ref[lax.rem(chunk, 2)].reshape(group * rows, WIDE)
             value_ref[...] = mm(turned_ref[0:own_in, :], arrived, 1, 0)
 
+    def weight_copy(item, action):
+        slot = lax.rem(item, 2)
+        narrow = scan_matrix_ref.shape[1] % WIDE
+
+        def one(matrix_ref, first, width):
+            height = matrix_ref.shape[0]
+            start = pl.multiple_of((item - first) * WIDE, WIDE)
+            action(
+                pltpu.make_async_copy(
+                    matrix_ref.at[:, pl.ds(start, width)],
+                    weights_ref.at[slot, pl.ds(0, height), pl.ds(0, width)],
+                    weight_sem.at[slot],
+                )
+            )
+
+        full = chunks - 1 if narrow else chunks
+
+        @pl.when(item < gate_steps)
+        def _():
+            one(gate_matrix_ref, 0, WIDE)
+
+        @pl.when((item >= gate_steps) & (item < full))
+        def _():
+            one(scan_matrix_ref, gate_steps, WIDE)
+
+        if narrow:
+
+            @pl.when(item == full)
+            def _():
+                one(scan_matrix_ref, gate_steps, narrow)
+
+        @pl.when((item >= chunks) & (item < items))
+        def _():
+            one(out_matrix_ref, chunks, WIDE)
+
+    items = chunks + model_width // WIDE
+
+    def back_product(grad_ref, item, first, width):
+        cols = pl.ds(pl.multiple_of((item - first) * WIDE, WIDE), width)
+        weights = weights_ref[lax.rem(item, 2), 0:model_width, 0:width]
+        normed_grad_ref[...] += mm(grad_ref[:, cols], weights, 1, 1)
+
+    def norm_backward():
+        def block(at, carry):
+            some = pl.ds(pl.multiple_of(at * HEIGHT, HEIGHT), HEIGHT)
+            hidden = hidden_ref[some, :].astype(f32)
+            root_mean = lax.rsqrt(jnp.mean(hidden * hidden, axis=-1, keepdims=True) + norm_eps)
+            plain = hidden * root_mean
+            grad = normed_grad_ref[some, :]
+            scaled = grad * scale_ref[0:1, :]
+            input_grad_ref[some, :] = root_mean * (
+                scaled - plain * jnp.mean(scaled * plain, axis=-1, keepdims=True)
+            ) + own_cot_ref[some, :].astype(f32)
+            return carry + jnp.sum(grad * plain, axis=0, keepdims=True)
+
+        total = lax.fori_loop(0, rows // HEIGHT, block, jnp.zeros((1, model_width), f32))
+        first = iota((8, model_width), 0) == 0
+        scale_grad_ref[...] = jnp.where(first, total, 0.0)
+        for i in range(1, group):
+            scale_copy(i, lax.rem(me + i, group), me).start()
+        small_all_ref[me, :, packed:] = scale_grad_ref[...]
+
+    def local_product(item):
+        narrow = scan_matrix_ref.shape[1] % WIDE
+        full = chunks - 1 if narrow else chunks
+
+        @pl.when(item == 0)
+        def _():
+            normed_grad_ref[...] = jnp.zeros_like(normed_grad_ref)
+
+        weight_copy(item, lambda copy: copy.wait())
+        weight_copy(item + 1, lambda copy: copy.start())
+
+        @pl.when(item < gate_steps)
+        def _():
+            back_product(gate_ref, item, 0, WIDE)
+
+        @pl.when((item >= gate_steps) & (item < full))
+        def _():
+            back_product(scan_ref, item, gate_steps, WIDE)
+
+        if narrow:
+
+            @pl.when(item == full)
+            def _():
+                back_product(scan_ref, item, gate_steps, narrow)
+
+        @pl.when(item == chunks - 1)
+        def _():
+            norm_backward()
+
+        @pl.when(item >= chunks)
+        def _():
+            cols = pl.ds(pl.multiple_of((item - chunks) * WIDE, WIDE), WIDE)
+            output_ref[:, cols] = hidden_ref[:, cols].astype(f32) + mm(
+                post_ref[...], weights_ref[lax.rem(item, 2)], 1, 0
+            )
+
+    weight_copy(0, lambda copy: copy.start())
+
     def up_copy(source, target, step, recv, to):
         return seq_copy(source, target, up_send.at[step], recv.at[step], to)
 
-    def up(value, inbox, other, total, step):
+    def up(value, inbox, total, step):
         edge = ((rank == 0) | (rank == last)) & (rank != root)
         inner = (rank != root) & (rank > 0) & (rank < last)
 
@@ -770,7 +1313,7 @@
 
         @pl.when(rank == root + 1)
         def _():
-            up_copy(inbox, other, step, other_recv, left).start()
+            up_copy(inbox, total, step, other_recv, left).start()
 
         @pl.when(rank > root + 1)
         def _():
@@ -783,8 +1326,8 @@
                 up_copy(inbox, inbox, step, inbox_recv, left).wait_recv()
                 result = result + inbox[...]
             if root < last:
-                up_copy(other, other, step, other_recv, right).wait_recv()
-                result = result + other[...]
+                up_copy(total, total, step, other_recv, right).wait_recv()
+                result = result + total[...]
             total[...] = result
             if root > 0:
                 down_copy(total, step, left_send, left).start()
@@ -835,7 +1378,7 @@
         def _():
             action(store_in(step))
 
-    def drain(inbox, other, total, step):
+    def drain(inbox, total, step):
         @pl.when(rank < root)
         def _():
             up_copy(inbox, inbox, step, inbox_recv, right).wait_send()
@@ -860,19 +1403,19 @@
 
             @pl.when((chunk >= 0) & (chunk < chunks))
             def _(chunk=chunk, stage=stage):
-                ring_stage(chunk, stage)
+                ring.stage(chunk, stage)
 
         ready = step - (out_steps - 1)
 
         @pl.when((ready >= 0) & (ready < chunks))
         def _():
-            pair_copy(ready, 1 - core).wait_recv()
+            ring.wait_pair(ready)
             load_copy(ready).start()
 
         @pl.when(step < steps)
         def _():
             compute(step)
-            up(value_ref, inbox_ref.at[step], other_ref.at[step], total_ref.at[step], step)
+            up(value_ref, inbox_ref.at[step], total_ref.at[step], step)
 
         @pl.when(step == steps)
         def _():
@@ -880,8 +1423,14 @@
                 small_copy(i, lax.rem(me + i, group), me).wait_send()
                 origin = lax.rem(me + group - i, group)
                 small_copy(i, origin, origin).wait_recv()
+                scale_copy(i, origin, me).wait_send()
+                scale_copy(i, origin, origin).wait_recv()
             small_value_ref[...] = jnp.sum(small_all_ref[...], axis=0)
-            up(small_value_ref, small_inbox_ref, small_other_ref, small_out_ref, steps)
+            up(small_value_ref, small_inbox_ref, small_out_ref, steps)
+
+        @pl.when(step < items)
+        def _():
+            local_product(step)
 
         late = step - behind
 
@@ -899,24 +1448,23 @@
     lax.fori_loop(0, steps + 1 + behind, round_, 0)
 
     def finish(step, carry):
-        drain(inbox_ref.at[step], other_ref.at[step], total_ref.at[step], step)
+        drain(inbox_ref.at[step], total_ref.at[step], step)
         stored(step, lambda copy: copy.wait())
         return carry
 
     lax.fori_loop(0, steps, finish, 0)
-    drain(small_inbox_ref, small_other_ref, small_out_ref, steps)
+    drain(small_inbox_ref, small_out_ref, steps)
 
     def finish_ring(chunk, carry):
-        for number in range(1, reach + 1):
-            for way in (1, -1):
-                hop(chunk, number, way).wait_send()
-        pair_copy(chunk, core).wait_send()
+        ring.finish(chunk)
         return carry
 
     lax.fori_loop(0, chunks, finish_ring, 0)
 
 
-def reduce_gradients(turned, cot_all, gate_grad, scan_grad, small, own_in):
+def reduce_gradients(
+    turned, cot_all, gate_grad, scan_grad, small, hidden, cot, post, scale, matrices, own_in
+):
     size = lax.axis_size("seq")
     group = lax.axis_size("dp")
     rows = gate_grad.shape[0]
@@ -928,9 +1476,10 @@
     reach = group // 4
     spacing = min(3, (out_steps - 2) // reach)
     sizes = (rows, own_in, out_steps, gate_steps, steps, size // 2, 3, spacing)
+    assert chunks + model_width // WIDE <= steps
     shape = jax.ShapeDtypeStruct
     dma = pltpu.SemaphoreType.DMA
-    small_shape = small.shape[1:]
+    small_shape = (8, small.shape[2] + model_width)
     anywhere = pl.BlockSpec(memory_space=pl.ANY)
     return pl.pallas_call(
         functools.partial(tail_kernel, sizes),
@@ -938,40 +1487,39 @@
             shape((own_in, chunks * WIDE), f32),
             shape((2 * own_in, model_width), f32),
             shape(small_shape, f32),
+            shape((rows, model_width), f32),
+            shape((rows, model_width), f32),
             shape((chunks, 2, group // 2, rows, WIDE), bf16),
         ),
-        in_specs=vmem(2) + [anywhere] * 2 + vmem(1),
-        out_specs=(anywhere, anywhere, vmem(1)[0], anywhere),
+        in_specs=vmem(9) + [anywhere] * 3,
+        out_specs=(anywhere, anywhere) + tuple(vmem(3)) + (anywhere,),
         scratch_shapes=[
             pltpu.VMEM((own_in, WIDE), f32),
-            pltpu.VMEM((steps, own_in, WIDE), f32),
             pltpu.VMEM((steps, own_in, WIDE), f32),
             pltpu.VMEM((steps, own_in, WIDE), f32),
             pltpu.VMEM((2, 2, group // 2, rows, WIDE), bf16),
             pltpu.VMEM(small_shape, f32),
             pltpu.VMEM(small_shape, f32),
-            pltpu.VMEM(small_shape, f32),
-            pltpu.VMEM(small.shape, f32),
+            pltpu.VMEM((group,) + small_shape, f32),
+            pltpu.VMEM((2, matrices[2].shape[0], WIDE), bf16),
+            pltpu.VMEM((rows, model_width), f32),
+            pltpu.VMEM((8, model_width), f32),
         ]
         + [dma((steps + 1,))] * 6
         + [
             dma((steps, 2)),
-            dma((chunks, 2 * reach)),
-            dma((chunks, 2 * reach)),
-            dma((chunks,)),
-            dma((chunks,)),
-            dma((chunks,)),
+            *PlaneRing.semaphores(chunks),
             dma((2,)),
-            dma((group,)),
-            dma((group,)),
+            *[dma((group,))] * 4,
+            dma((2,)),
         ],
         compiler_params=pltpu.CompilerParams(
-            collective_id=3, has_side_effects=True, vmem_limit_bytes=52 * 2**20
+            collective_id=3, has_side_effects=True, vmem_limit_bytes=56 * 2**20
         ),
         cost_estimate=pl.CostEstimate(
             flops=2 * 10**10, bytes_accessed=2 * 10**8, transcendentals=0
         ),
-    )(turned, cot_all, gate_grad, scan_grad, small)
+    )(turned, cot_all, gate_grad, scan_grad, small, hidden, cot, post, scale, *matrices)
 
 
 def on_device(
@@ -1011,70 +1559,47 @@
     conv_own = convtaps.shape[1]
     conv_width = conv_own * group
 
-    in_low = inproject.astype(bf16)
-    scan_matrix = lax.all_gather(in_low[:, inner:], "dp", axis=0, tiled=True)
-    small = jnp.concatenate([prenorm, postnorm, convtaps.reshape(-1)]).astype(bf16)
-    small = lax.all_gather(small, "dp", axis=0).astype(f32)
-    pre_scale = small[:, :own_in].reshape(-1)
-    post_scale = small[:, own_in : own_in + own_out].reshape(-1)
-    taps = small[:, own_in + own_out :].reshape(group, -1, conv_own)
-    taps = jnp.swapaxes(taps, 0, 1).reshape(-1, conv_width)
-    tap_rows = taps.shape[0]
-    gate_matrix = lax.all_gather(in_low[:, :inner], "dp", axis=0, tiled=True)
-    out_matrix = lax.all_gather(outproject.astype(bf16), "dp", axis=0, tiled=True)
-
-    hidden = hidden_in.reshape(rows, model_width).astype(f32)
+    tap_rows = convtaps.shape[0]
+    small_lanes = -(-max(own_in, own_out, conv_own) // LANES) * LANES
+    small = jnp.concatenate(
+        [
+            jnp.pad(part, ((0, 0), (0, small_lanes - part.shape[1])))
+            for part in (prenorm.reshape(1, -1), convtaps, postnorm.reshape(1, -1))
+        ]
+    )
+    small = jnp.pad(small, ((0, 16 - small.shape[0]), (0, 0))).astype(bf16)
+    hidden_low = hidden_in.reshape(rows, model_width)
     cot_low = out_grad.reshape(rows, model_width)
-    cot_all = lax.all_gather(cot_low, "dp", axis=0, tiled=True)
-    root = lax.rsqrt(jnp.mean(hidden * hidden, axis=-1, keepdims=True) + norm_eps)
-    normed_low = (hidden * root * pre_scale).astype(bf16)
-
-    scan_in = jnp.dot(normed_low, scan_matrix, preferred_element_type=f32).astype(bf16)
-    pad_heads = ((0, 0), (0, LANES - heads))
-    rate = jnp.pad(scan_in[:, conv_width:].astype(f32), pad_heads)
     head_rows = jnp.pad(headcoefs, ((0, 8 - headcoefs.shape[0]), (0, LANES - heads)))
     skip = jnp.repeat(headcoefs[2:3], width, axis=1)
-    taps_pad = jnp.pad(taps, ((0, 8 - tap_rows), (0, 0)))
-    mixer_low, ypre, enter, halo, step, cum, cumt = scan_forward(
-        scan_in, rate, head_rows, skip, taps_pad, sizes
-    )
-
-    gate = jnp.dot(normed_low, gate_matrix, preferred_element_type=f32)
-    mixer = mixer_low.astype(f32)
-    gate_sig = jax.nn.sigmoid(gate)
-    gate_act = gate * gate_sig
-    gated = mixer * gate_act
-    post_root = lax.rsqrt(jnp.mean(gated * gated, axis=-1, keepdims=True) + norm_eps)
-    whitened = gated * post_root
-    post_low = (whitened * post_scale).astype(bf16)
-    output = hidden + jnp.dot(post_low, out_matrix, preferred_element_type=f32)
-
-    post_grad = mm(cot_low, out_matrix, 1, 1)
-    postnorm_grad = jnp.sum(post_grad * whitened, axis=0)
-    dwhite = post_grad * post_scale
-    dgated = post_root * (dwhite - whitened * jnp.mean(dwhite * whitened, axis=-1, keepdims=True))
-    dy = (dgated * gate_act).astype(bf16)
-    gate_grad = (dgated * mixer * gate_sig * (1.0 + gate * (1.0 - gate_sig))).astype(bf16)
-
-    turn = jnp.concatenate(
-        [
-            normed_low.T.reshape(group, own_in, rows),
-            post_low.T.reshape(group, own_out, rows),
-        ],
-        axis=1,
-    )
+    (
+        scan_in,
+        ypre,
+        enter,
+        halo,
+        step,
+        cum,
+        cumt,
+        taps,
+        pre_scale,
+        dy,
+        gate_grad,
+        postnorm_grad,
+        post_low,
+        normed_t,
+        post_t,
+        token,
+        scan_matrix,
+        gate_matrix,
+        out_matrix,
+    ) = front(inproject, outproject, small, hidden_low, cot_low, head_rows, skip, sizes)
+    scan_matrix = scan_matrix.reshape(model_width, -1)
+    gate_matrix = gate_matrix.reshape(model_width, inner)
+    out_matrix = out_matrix.reshape(inner, model_width)
+    cot_all = lax.all_gather(cot_low + token[0, 0].astype(bf16), "dp", axis=0, tiled=True)
     scan_grad, conv_grad, head_grad, turned = scan_backward(
-        scan_in, halo, rate, step, cum, cumt, head_rows, skip, taps_pad, dy, ypre, enter, turn, sizes
-    )
-    normed_grad = mm(gate_grad, gate_matrix, 1, 1) + mm(
-        scan_grad[:, : scan_matrix.shape[1]], scan_matrix, 1, 1
-    )
-    plain = hidden * root
-    prenorm_grad = jnp.sum(normed_grad * plain, axis=0)
-    dplain = normed_grad * pre_scale
-    input_gradient = root * (
-        dplain - plain * jnp.mean(dplain * plain, axis=-1, keepdims=True)
-    ) + cot_low.astype(f32)
+        scan_in, halo, step, cum, cumt, head_rows, skip, taps, dy, ypre, enter, normed_t, post_t, sizes
+    )
 
     head_sums = jnp.concatenate(
         [
@@ -1086,7 +1611,6 @@
     conv_sums = conv_grad[:tap_rows].reshape(tap_rows, group, conv_own)
     packed = jnp.concatenate(
         [
-            prenorm_grad.reshape(group, own_in),
             postnorm_grad.reshape(group, own_out),
             jnp.swapaxes(conv_sums, 0, 1).reshape(group, -1),
             jnp.broadcast_to(head_sums.reshape(1, -1), (group, 3 * heads)),
@@ -1096,14 +1620,24 @@
     packed_size = packed.shape[1]
     packed_lanes = -(-packed_size // (8 * LANES)) * LANES
     packed = jnp.pad(packed, ((0, 0), (0, 8 * packed_lanes - packed_size)))
-    inproj_padded, outproj_owned, packed, _ = reduce_gradients(
-        turned, cot_all, gate_grad, scan_grad, packed.reshape(group, 8, packed_lanes), own_in
+    inproj_padded, outproj_owned, packed, output, input_gradient, _ = reduce_gradients(
+        turned,
+        cot_all,
+        gate_grad,
+        scan_grad,
+        packed.reshape(group, 8, packed_lanes),
+        hidden_low,
+        cot_low,
+        post_low,
+        pre_scale,
+        (gate_matrix, scan_matrix, out_matrix),
+        own_in,
     )
     inproj_owned = inproj_padded[:, :proj_width]
-    packed = packed.reshape(-1)
-    prenorm_owned = packed[:own_in]
-    postnorm_owned = packed[own_in : own_in + own_out]
-    conv_at = own_in + own_out
+    prenorm_owned = lax.dynamic_slice_in_dim(packed[0, packed_lanes:], me * own_in, own_in, 0)
+    packed = packed[:, :packed_lanes].reshape(-1)
+    postnorm_owned = packed[:own_out]
+    conv_at = own_out
     conv_end = conv_at + tap_rows * conv_own
     conv_owned = packed[conv_at:conv_end].reshape(tap_rows, conv_own)
     head_total = packed[conv_end:packed_size].reshape(3, heads)

time: 521 us -> 476 us (0.914)
  Pallas kernels: 285 us -> 411 us
  waiting for transfers between devices: 111 us -> 1.19 us
  matrix products: 47.1 us -> 0 us
  blocking collectives: 10.7 us -> 0 us
  other arithmetic: 35.3 us -> 26.3 us
    all_gather x4 -> x1, waiting for transfers between devices: 110 us -> 1.18 us  [on_device(): lax.all_gather(cot_low + token[0, 0].astype(bf16), 'dp', axis=0, tiled=True)]
    pallas_call x1, Pallas kernels: 38.3 us -> 146 us  [front(): pl.pallas_call(functools.partial(front_kernel, sizes), out_shape=(shape((...]
    dot_general x6 -> x0, matrix products: 47.1 us -> none  [the longest x3 23.7 us: mm(): lax.dot_general(a, b, (((ca,), (cb,)), ((), ())), preferred_element_type=...]
    pallas_call x1, Pallas kernels: 53.9 us -> 65.5 us  [scan_backward(): pl.pallas_call(functools.partial(backward_kernel, sizes), out_shape=(shap...]
    all_gather x1 -> x0, blocking collectives: 10.7 us -> none  [on_device(): small = lax.all_gather(small, 'dp', axis=0).astype(f32)]
    convert_element_type x3 -> x0, other arithmetic: 10.1 us -> none  [the longest x1 4.55 us: on_device(): (dgated * mixer * gate_sig * (1.0 + gate * (1.0 - gate_sig))).astype(bf16)]
    pallas_call x1, Pallas kernels: 193 us -> 200 us  [reduce_gradients(): pl.pallas_call(functools.partial(tail_kernel, sizes), out_shape=(shape((o...]
    unnamed x103 -> x82, local copies, waits for them, and re-layouts: 9.72 us -> 14 us
  transfers between devices with their start and end apart: 4 -> 1, of which waited for: 3 -> 1; matrix products, arithmetic and copies ran while one was open for 11% -> 1% of each run, Pallas kernels for 18% -> 14%
where the time goes in v4:
time: 476 us; the launch traced here: 475 us
  Pallas kernels  411 us (86%)
  other arithmetic  26.3 us (6%)
  local copies, waits for them, and re-layouts  21.5 us (5%)
  between operations  14.5 us (3%)
    pallas_call x1, Pallas kernels, reduce_gradients(): pl.pallas_call(functools.partial(tail_kernel, sizes), out_shape=(shape((o...  200 us
    pallas_call x1, Pallas kernels, front(): pl.pallas_call(functools.partial(front_kernel, sizes), out_shape=(shape((...  146 us
    pallas_call x1, Pallas kernels, scan_backward(): pl.pallas_call(functools.partial(backward_kernel, sizes), out_shape=(shap...  65.5 us
    sub x6, other arithmetic, adam_update(): weight - step_rate * (moment_hat / (jnp.sqrt(square_hat) + adam_eps) + de...  21 us
    unnamed x82, local copies, waits for them, and re-layouts  14 us
  transfers between devices with their start and end apart: 1, of which 1 were waited for; matrix products, arithmetic and copies ran while one was open for 1% of the time, Pallas kernels for 14%

profile of v4, /device:TPU:0, one launch (start us, length us, event | category | flops | bytes accessed | tf_op | source)
XLA Modules:
  0.0 474.6 jit_solution(7586711664176602272)
XLA Ops:
  7.2 0.0 all-gather.2.cloned.1.call-start
  7.2 0.7 slice_bitcast_fusion
  7.9 0.1 broadcast_in_dim.12
  8.0 0.7 broadcast_in_dim.13.skip_ref
  8.7 1.3 pad.32.heads_ref
  10.0 0.7 convert.23
  10.7 0.7 convert.24
  11.4 0.7 convert.22
  12.1 0.6 pad.31.small_ref
  12.7 145.7 %shard_map.395 = (bf16[256,3456]{1,0:T(8,128)(2,1)}, f32[256,3072]{1,0:T(8,128)}, f32[24,128,128]{2,1,0:T(8,128)}, bf16[16,3328]{1,0:T(8,128)(2,1)}, f32[256,128...) custom-call(f32[192,6448]{1,0:T(8,128)} %in_shard_ref.1, ...), custom_call_target="tpu_custom_call" | custom-call | flops 10000000000 | bytes 100000000 | tf_op jit(solution)/shard_map/pallas_call | solution.py:817
  158.4 0.0 copy-start
  158.5 0.0 copy-start.1
  158.5 0.8 convert.25
  159.4 0.5 slice.42
  159.9 1.6 broadcast_add_fusion
  161.5 0.0 all-gather.2.cloned.1.call-update
  161.6 1.4 copy-done.5
  163.0 1.4 copy-done.6
  164.4 1.4 copy-done.7
  165.8 1.1 copy-done.8
  166.9 65.5 %shard_map.396 = (bf16[256,3584]{1,0:T(8,128)(2,1)S(1)}, f32[8,3328]{1,0:T(8,128)S(1)}, f32[8,128]{1,0:T(8,128)S(1)}, bf16[576,2048]{1,0:T(8,128)(2,1)S(1)}) custom-call(bf16[256,3456]{1,0:T(8,128)(2,1)S(1)} %copy-done.4, bf16[16,3328]{1,0:T(8,128)(2,1)S(1)} %copy-done.12, f32[256,128]{1,0:T(8,128)S(1)} %copy-done.9, f32[256,128]{1,0:T(8,128)S(1)} %copy-done.10, ...), custom_call_target="tpu_custom_call" | custom-call | flops 6000000000 | bytes 20000000 | tf_op jit(solution)/shard_map/pallas_call | solution.py:888
  232.4 0.0 copy-start.2
  232.4 1.4 copy-done.2
  233.8 1.2 copy-done.3
  235.1 0.1 reshape.123
  235.1 0.1 reduce_sum.11
  235.3 0.1 broadcast_in_dim.14
  235.4 0.1 reshape.121
  235.5 0.1 copy.51
  235.5 0.1 reshape.122
  235.6 0.5 broadcast.80
  236.1 0.7 reduce.10
  236.8 0.1 concatenate.12
  236.9 0.7 copy.52
  237.6 1.2 all-gather.2.cloned.1.call-done.cot_ref
  238.8 200.0 %shard_map.397 = (f32[192,6656]{1,0:T(8,128)}, f32[384,1536]{1,0:T(8,128)}, f32[8,1920]{1,0:T(8,128)}, f32[256,1536]{1,0:T(8,128)}, f32[256,1536]{1,0:T(8,128)}, /*index=5*/bf16[26,2,4,256,256]{4,3,2,1,0:T(8,128)(2,1)}) custom-call(bf16[576,2048]{1,0:T(8,128)(2,1)} %copy-done.2, bf16[2048,1536]{1,0:T(8,128)(2,1)} %all-gather.2.cloned.1.call-done.cot_ref, ...), custom_call_target="tpu_custom_call" | custom-call | flops 20000000000 | bytes 200000000 | tf_op jit(solution)/shard_map/pallas_call | solution.py:1484
  438.8 0.7 slice.48
  439.5 0.1 slice.54
  439.6 0.8 slice.46
  440.4 0.7 slice_reduce_fusion.1
  441.1 0.1 reshape.131
  441.2 0.1 reshape.132
  441.3 7.5 %multiply_subtract_fusion.1 = (f32[384,1536]{1,0:T(8,128)}, f32[384,1536]{1,0:T(8,128)}, f32[384,1536]{1,0:T(8,128)}) fusion(f32[384,1536]{1,0:T(8,128)S(1)} %copy-done.16, f32[384,1536]{1,0:T(8,128)} %get-tuple-element.134, f32[384,1536]{1,0:T(8,128)} %param.33, f32[384,1536]{1,0:T(8,128)} %param.39), kind=kLoop, calls=%fused_computation.6 | loop fusion | flops 8847360 | bytes 16515072 | tf_op jit(solution)/shard_map/sub | solution.py:35
  448.8 0.1 constant_dynamic-slice_fusion
  448.8 0.5 copy-done.15
  449.3 0.0 copy-start.30
  449.3 0.0 copy-start.31
  449.3 0.0 copy-start.34
  449.3 0.0 copy-start.35
  449.4 0.0 copy-start.36
  449.4 0.0 copy-start.27
  449.4 0.0 copy-start.32
  449.4 0.0 copy-start.33
  449.4 11.0 %multiply_subtract_fusion = (f32[192,6448]{1,0:T(8,128)}, f32[192,6448]{1,0:T(8,128)}, f32[192,6448]{1,0:T(8,128)}, f32[192,6448]{1,0:T(8,128)}) fusion(f32[192,6448]{1,0:T(8,128)S(1)} %bitcast.23, f32[192,6448]{1,0:T(8,128)} %param.29, f32[192,6448]{1,0:T(8,128)} %param.35, f32[192,6656]{1,0:T(8,128)S(1)} %copy-done.15), kind=kLoop, calls=%fused_computation.2 | loop fusion | flops 18570240 | bytes 39616512 | tf_op jit(solution)/shard_map/sub | solution.py:35
  460.5 0.0 copy-done.20
  460.5 0.6 multiply_subtract_fusion.2
  461.1 0.0 copy-done.28
  461.1 0.6 multiply_subtract_fusion.4
  461.8 0.6 multiply_subtract_fusion.5
  462.4 0.6 multiply_subtract_fusion.3
  463.0 1.1 copy.56
  464.1 1.1 copy.57
  465.3 1.1 copy-done.14
  466.4 1.4 copy.58
  (69 shorter events, 0.2 us)
Async XLA Ops:
  7.2 231.6 %all-gather.2.cloned.1.call-start = ((), (), s32[]{:S(2)}) async-start(), calls=%async_computation | async-start | bytes 7077888 | tf_op jit(solution)/shard_map/all_gather | solution.py:1599
  12.7 147.2 %copy-start.19 = (bf16[1,256,1536]{2,1,0:T(8,128)(2,1)S(1)}, bf16[1,256,1536]{2,1,0:T(8,128)(2,1)}, u32[]{:S(2)}) copy-start(bf16[1,256,1536]{2,1,0:T(8,128)(2,1)} %param.21) | copy-start | bytes 2359300
  158.4 3.0 copy-start
  158.5 3.0 copy-start.1
  158.5 3.0 copy-start.4
  158.5 3.0 copy-start.9
  158.5 3.0 copy-start.10
  158.5 3.0 copy-start.11
  158.5 3.0 copy-start.12
  158.5 3.0 copy-start.13
  161.6 1.4 copy-start.5
  163.0 1.4 copy-start.6
  164.4 1.4 copy-start.7
  165.8 1.1 copy-start.8
  166.9 69.2 %copy-start.24 = (f32[1,3072]{1,0:T(1,128)S(1)}, f32[1,3072]{1,0:T(1,128)}, u32[]{:S(2)}) copy-start(f32[1,3072]{1,0:T(1,128)} %get-tuple-element.69) | copy-start | bytes 36868
  232.4 1.4 copy-start.2
  233.8 1.2 copy-start.3
  238.8 202.5 %copy-start.16 = (f32[384,1536]{1,0:T(8,128)S(1)}, f32[384,1536]{1,0:T(8,128)}, u32[]{:S(2)}) copy-start(f32[384,1536]{1,0:T(8,128)} %out_shard_ref.1) | copy-start | bytes 7077892
  441.1 21.3 %copy-start.25 = (f32[384]{0:T(512)}, f32[384]{0:T(512)S(1)}, u32[]{:S(2)}) copy-start(f32[384]{0:T(512)S(1)} %slice_reduce_fusion.1) | copy-start | bytes 4612
  441.2 19.3 %copy-start.20 = (f32[5,416]{1,0:T(8,128)}, f32[5,416]{1,0:T(8,128)S(1)}, u32[]{:S(2)}) copy-start(f32[5,416]{1,0:T(8,128)S(1)} %reshape.131) | copy-start | bytes 24964
  441.2 7.7 %slice-start = ((s8[5013504]{0:T(1024)(128)(4,1)}), s8[819200]{0:T(1024)(128)(4,1)S(1)}, s32[]{:S(2)}) async-start(s8[5013504]{0:T(1024)(128)(4,1)} %bitcast.22), calls=%async_computation.1 | async-start | bytes 1638400
  441.3 19.9 %copy-start.28 = (f32[3,48]{1,0:T(4,128)}, f32[3,48]{1,0:T(4,128)S(1)}, u32[]{:S(2)}) copy-start(f32[3,48]{1,0:T(4,128)S(1)} %reshape.132) | copy-start | bytes 1732
  441.3 7.6 %slice-start.1 = ((s8[5013504]{0:T(1024)(128)(4,1)}), s8[4194304]{0:T(1024)(128)(4,1)S(1)}, s32[]{:S(2)}) async-start(s8[5013504]{0:T(1024)(128)(4,1)} %bitcast.22), calls=%async_computation.2 | async-start | bytes 8388608
  441.3 8.0 %copy-start.15 = (f32[192,6656]{1,0:T(8,128)S(1)}, f32[192,6656]{1,0:T(8,128)}, u32[]{:S(2)}) copy-start(f32[192,6656]{1,0:T(8,128)} %get-tuple-element.80) | copy-start | bytes 15335428
  448.8 12.9 %copy-start.29 = (f32[1,192]{1,0:T(1,128)}, f32[1,192]{1,0:T(1,128)S(1)}, u32[]{:S(2)}) copy-start(f32[1,192]{1,0:T(1,128)S(1)} %constant_dynamic-slice_fusion) | copy-start | bytes 2308
  449.3 11.2 %copy-start.21 = (f32[5,416]{1,0:T(8,128)S(1)}, f32[5,416]{1,0:T(8,128)}, u32[]{:S(2)}) copy-start(f32[5,416]{1,0:T(8,128)} %param.24) | copy-start | bytes 24964
  449.3 11.2 %copy-start.22 = (f32[5,416]{1,0:T(8,128)S(1)}, f32[5,416]{1,0:T(8,128)}, u32[]{:S(2)}) copy-start(f32[5,416]{1,0:T(8,128)} %param.30) | copy-start | bytes 24964
  449.3 11.2 %copy-start.23 = (f32[5,416]{1,0:T(8,128)S(1)}, f32[5,416]{1,0:T(8,128)}, u32[]{:S(2)}) copy-start(f32[5,416]{1,0:T(8,128)} %param.36) | copy-start | bytes 24964
  449.3 11.8 %copy-start.26 = (f32[3,48]{1,0:T(4,128)S(1)}, f32[3,48]{1,0:T(4,128)}, u32[]{:S(2)}) copy-start(f32[3,48]{1,0:T(4,128)} %param.25) | copy-start | bytes 1732
  449.3 11.8 %copy-start.30 = (f32[3,48]{1,0:T(4,128)S(1)}, f32[3,48]{1,0:T(4,128)}, u32[]{:S(2)}) copy-start(f32[3,48]{1,0:T(4,128)} %param.31) | copy-start | bytes 1732
  449.3 11.8 %copy-start.31 = (f32[3,48]{1,0:T(4,128)S(1)}, f32[3,48]{1,0:T(4,128)}, u32[]{:S(2)}) copy-start(f32[3,48]{1,0:T(4,128)} %param.37) | copy-start | bytes 1732
  449.3 12.4 %copy-start.34 = (f32[192]{0:T(256)S(1)}, f32[192]{0:T(256)}, u32[]{:S(2)}) copy-start(f32[192]{0:T(256)} %param.22) | copy-start | bytes 2308
  449.3 12.4 %copy-start.35 = (f32[192]{0:T(256)S(1)}, f32[192]{0:T(256)}, u32[]{:S(2)}) copy-start(f32[192]{0:T(256)} %param.28) | copy-start | bytes 2308
  449.4 12.4 %copy-start.36 = (f32[192]{0:T(256)S(1)}, f32[192]{0:T(256)}, u32[]{:S(2)}) copy-start(f32[192]{0:T(256)} %param.34) | copy-start | bytes 2308
  449.4 13.0 %copy-start.27 = (f32[384]{0:T(512)S(1)}, f32[384]{0:T(512)}, u32[]{:S(2)}) copy-start(f32[384]{0:T(512)} %param.26) | copy-start | bytes 4612
  449.4 13.0 %copy-start.32 = (f32[384]{0:T(512)S(1)}, f32[384]{0:T(512)}, u32[]{:S(2)}) copy-start(f32[384]{0:T(512)} %param.32) | copy-start | bytes 4612
  449.4 13.0 %copy-start.33 = (f32[384]{0:T(512)S(1)}, f32[384]{0:T(512)}, u32[]{:S(2)}) copy-start(f32[384]{0:T(512)} %param.38) | copy-start | bytes 4612
  449.4 13.6 %copy-start.18 = (f32[256,1536]{1,0:T(8,128)S(1)}, f32[256,1536]{1,0:T(8,128)}, u32[]{:S(2)}) copy-start(f32[256,1536]{1,0:T(8,128)} %get-tuple-element.77) | copy-start | bytes 4718596
  460.5 3.7 copy-start.17
  464.1 2.2 copy-start.14
Sparse Core Ops, SparseCore 0:
  161.6 77.1 all-gather.1

commit v5 on v4

--- a/solution.py
+++ b/solution.py
@@ -12,6 +12,10 @@
 HALO = 16
 WIDE = 256
 HEIGHT = 32
+PARTS = 2
+LAG = 4
+COT_AT = 4
+COT_SPACING = 7
 
 norm_eps = 1e-05
 beta_moment = 0.9
@@ -130,6 +134,19 @@
     cot_ref,
     heads_ref,
     skip_ref,
+    pre_scale_ref,
+    gate_grad_ref,
+    post_grad_ref,
+    post_ref,
+    normed_turned_ref,
+    post_turned_ref,
+    dproj_ref,
+    conv_grad_ref,
+    head_grad_ref,
+    scan_all_ref,
+    gate_all_ref,
+    out_all_ref,
+    cot_all_ref,
     u_ref,
     ypre_ref,
     enter_ref,
@@ -138,17 +155,8 @@
     cum_ref,
     cumt_ref,
     taps_ref,
-    pre_scale_ref,
     dy_ref,
-    gate_grad_ref,
-    post_grad_ref,
-    post_ref,
-    normed_t_ref,
     post_t_ref,
-    token_ref,
-    scan_all_ref,
-    gate_all_ref,
-    out_all_ref,
     in_wide_ref,
     out_wide_ref,
     scan_shard_ref,
@@ -166,11 +174,25 @@
     gate_ref,
     gated_ref,
     dpost_ref,
+    normed_t_ref,
+    dscore_ref,
+    dread_ref,
+    dwrite_ref,
+    dcum_ref,
+    dstep_ref,
+    dpre_ref,
+    arrive_ref,
     send_sem,
     recv_sem,
     halo_sem,
+    back_send,
+    back_recv,
+    edge_sem,
     small_send,
     small_recv,
+    turn_send,
+    turn_recv,
+    own_sem,
     wide_sem,
     weight_sem,
     *ring_sems,
@@ -284,7 +306,6 @@
         taps_ref[0:5, device * conv_own : (device + 1) * conv_own] = small[1:6, 0:conv_own]
         post_scale_ref[0:1, device * own_out : (device + 1) * own_out] = small[6:7, 0:own_out]
     pre_scale_ref[1:8, :] = jnp.zeros((7, model_width), f32)
-    token_ref[...] = jnp.zeros_like(token_ref)
 
     def norm(at, carry):
         some = pl.ds(pl.multiple_of(at * HEIGHT, HEIGHT), HEIGHT)
@@ -482,6 +503,22 @@
     turn(post_ref, post_t_ref)
     rounds(at_round, end_round)
     wait_pairs(2)
+    normed_turn = PlaneTurn(
+        normed_t_ref,
+        normed_turned_ref,
+        own_in,
+        rows,
+        (turn_send.at[0], turn_recv.at[0], own_sem.at[0]),
+    )
+    post_turn = PlaneTurn(
+        post_t_ref,
+        post_turned_ref,
+        own_out,
+        rows,
+        (turn_send.at[1], turn_recv.at[1], own_sem.at[1]),
+    )
+    post_turn.start()
+    normed_turn.start()
 
     span = 2 * own_out
 
@@ -539,263 +576,212 @@
 
         lax.fori_loop(0, chunks, finish, 0)
 
-
-def backward_kernel(
-    sizes,
-    u_ref,
-    halo_ref,
-    step_ref,
-    cum_ref,
-    cumt_ref,
-    heads_ref,
-    skip_ref,
-    taps_ref,
-    dy_ref,
-    ypre_ref,
-    enter_ref,
-    normed_t_ref,
-    post_t_ref,
-    dproj_ref,
-    conv_grad_ref,
-    head_grad_ref,
-    turned_ref,
-    conv_ref,
-    score_ref,
-    dscore_ref,
-    dread_ref,
-    dwrite_ref,
-    dcum_ref,
-    dstep_ref,
-    dpre_ref,
-    leave_ref,
-    arrive_ref,
-    send_sem,
-    recv_sem,
-    halo_sem,
-    turn_send,
-    turn_recv,
-    own_sem,
-):
-    rows, inner, tiles, per_tile = sizes
-    conv_width = inner + 2 * N
-    rank = lax.axis_index("seq")
-    last = lax.axis_size("seq") - 1
-    me = lax.axis_index("dp")
-    group = lax.axis_size("dp")
-    barrier = pltpu.get_barrier_semaphore()
-    greet_seq(barrier, rank, last)
-    greet_plane(barrier, me, group)
-    pl.semaphore_wait(barrier, seq_neighbours(rank, last) + group - 1)
-
-    own_in = normed_t_ref.shape[0] // group
-    own_out = post_t_ref.shape[0] // group
-    turns = ((normed_t_ref, 0, own_in), (post_t_ref, own_in, own_out))
-
-    def landing(device, which):
-        _, first, height = turns[which]
-        cols = pl.ds(pl.multiple_of(slot_of(device, group) * rows, rows), rows)
-        return turned_ref.at[pl.ds(first, height), cols]
-
-    def leaving(device, which):
-        source, _, height = turns[which]
-        return source.at[pl.ds(pl.multiple_of(device * height, height), height), :]
-
-    def turn(i, which, peer, source):
-        return plane_copy(
-            leaving(peer, which),
-            landing(source, which),
-            turn_send.at[i, which],
-            turn_recv.at[i, which],
-            peer,
-        )
-
-    own_copies = [
-        pltpu.make_async_copy(leaving(me, which), landing(me, which), own_sem.at[which])
-        for which in range(2)
-    ]
-    for which in range(2):
-        for i in range(1, group):
-            turn(i, which, lax.rem(me + i, group), me).start()
-        own_copies[which].start()
-
-    left = jnp.maximum(rank - 1, 0)
-    cum = cum_ref[...]
-    step = step_ref[...]
-    pre_b, sig_b = conv_tile(conv_ref, halo_ref, u_ref, taps_ref, inner, rows)
-    b_parts = halves(pre_b * sig_b)
-    pre_c, sig_c = conv_tile(conv_ref, halo_ref, u_ref, taps_ref, inner + N, rows)
-    c_parts = halves(pre_c * sig_c)
-    later = iota((rows, rows), 1) >= iota((rows, rows), 0)
-    score_ref[...] = jnp.where(later, mm3(b_parts, c_parts, 1, 1), 0.0)
-    dscore_ref[...] = jnp.zeros_like(dscore_ref)
-    dread_ref[...] = jnp.zeros_like(dread_ref)
-    dwrite_ref[...] = jnp.zeros_like(dwrite_ref)
-    dcum_ref[...] = jnp.zeros_like(dcum_ref)
-    dstep_ref[...] = jnp.zeros_like(dstep_ref)
-    cum_parts = jnp.concatenate(thirds(cum), axis=1)
-    step_parts = jnp.concatenate(thirds(step), axis=1)
-    lane = iota((rows, LANES), 1)
-    final_row = iota((rows, LANES), 0) == rows - 1
-    width = LANES // per_tile
-
-    def chain(tile):
-        return seq_copy(
-            leave_ref.at[tile], arrive_ref.at[tile], send_sem.at[tile], recv_sem.at[tile], left
-        )
-
-    def tap_grads(dpre, extra):
-        sums = [
-            jnp.sum(
-                dpre * conv_ref[HALO - 3 + k : HALO - 3 + k + rows, :], axis=0, keepdims=True
+    def backward():
+        core = lax.rem(me, 2)
+        cot_chunks = cot_ref.shape[1] // WIDE
+
+        def cot_block(chunk, origin, part):
+            ref = cot_all_ref.at[chunk, core, origin]
+            return ref if part is None else ref.at[pl.ds(part * (rows // 2), rows // 2), :]
+
+        def cot_source(chunk, part, action):
+            part_rows = pl.ds(0, rows) if part is None else pl.ds(part * (rows // 2), rows // 2)
+            cols = pl.ds(pl.multiple_of(chunk * WIDE, WIDE), WIDE)
+            action(cot_ref.at[part_rows, cols])
+
+        ring = PlaneRing(
+            cot_block, cot_source, lambda chunk, half: cot_all_ref.at[chunk, half], cot_ring_sems
+        )
+
+        left = jnp.maximum(rank - 1, 0)
+        cum = cum_ref[...]
+        step = step_ref[...]
+        pre_b, sig_b = conv_tile(conv_ref, halo_ref, u_ref, taps_ref, inner, rows)
+        b_parts = halves(pre_b * sig_b)
+        pre_c, sig_c = conv_tile(conv_ref, halo_ref, u_ref, taps_ref, inner + N, rows)
+        c_parts = halves(pre_c * sig_c)
+        later = iota((rows, rows), 1) >= iota((rows, rows), 0)
+        score_ref[...] = jnp.where(later, mm3(b_parts, c_parts, 1, 1), 0.0)
+        dscore_ref[...] = jnp.zeros_like(dscore_ref)
+        dread_ref[...] = jnp.zeros_like(dread_ref)
+        dwrite_ref[...] = jnp.zeros_like(dwrite_ref)
+        dcum_ref[...] = jnp.zeros_like(dcum_ref)
+        dstep_ref[...] = jnp.zeros_like(dstep_ref)
+        cum_parts = jnp.concatenate(thirds(cum), axis=1)
+        step_parts = jnp.concatenate(thirds(step), axis=1)
+        lane = iota((rows, LANES), 1)
+        final_row = iota((rows, LANES), 0) == rows - 1
+        width = LANES // per_tile
+
+        def chain(tile):
+            return seq_copy(
+                leave_ref.at[tile], arrive_ref.at[tile], back_send.at[tile], back_recv.at[tile], left
             )
-            for k in range(4)
-        ]
-        sums.append(jnp.sum(dpre, axis=0, keepdims=True))
-        sums.append(extra)
-        sums.append(jnp.zeros((2, LANES), f32))
-        return jnp.concatenate(sums, axis=0)
-
-    def one(tile, carry):
-        start = pl.multiple_of(tile * LANES, LANES)
-        cols = pl.ds(start, LANES)
-        pick = head_lanes(tile, per_tile, 3)
-        cum_l = mm(cum_parts, pick, 1, 0)
-        step_l = mm(step_parts, pick, 1, 0)
-        total = cum_l[rows - 1 : rows, :]
-        dy = dy_ref[:, cols].astype(f32)
-        reads = halves(dy * jnp.exp(cum_l))
-        denter = mm3(c_parts, reads, 0, 0)
+
+        def tap_grads(dpre, extra):
+            sums = [
+                jnp.sum(
+                    dpre * conv_ref[HALO - 3 + k : HALO - 3 + k + rows, :], axis=0, keepdims=True
+                )
+                for k in range(4)
+            ]
+            sums.append(jnp.sum(dpre, axis=0, keepdims=True))
+            sums.append(extra)
+            sums.append(jnp.zeros((2, LANES), f32))
+            return jnp.concatenate(sums, axis=0)
+
+        def one(tile, carry):
+            start = pl.multiple_of(tile * LANES, LANES)
+            cols = pl.ds(start, LANES)
+            pick = head_lanes(tile, per_tile, 3)
+            cum_l = mm(cum_parts, pick, 1, 0)
+            step_l = mm(step_parts, pick, 1, 0)
+            total = cum_l[rows - 1 : rows, :]
+            dy = dy_ref[:, cols].astype(f32)
+            reads = halves(dy * jnp.exp(cum_l))
+            denter = mm3(c_parts, reads, 0, 0)
+
+            @pl.when(rank < last)
+            def _():
+                chain(tile).wait_recv()
+
+            @pl.when(rank == last)
+            def _():
+                arrive_ref[tile] = jnp.zeros((N, LANES), f32)
+
+            arrive = arrive_ref[tile]
+            leave_ref[tile] = jnp.exp(total) * arrive + denter
+
+            @pl.when(rank > 0)
+            def _():
+                chain(tile).start()
+
+            pre, sig = conv_tile(conv_ref, halo_ref, u_ref, taps_ref, start, rows)
+            values = pre * sig
+            x = values * step_l
+            x_parts = halves(x)
+            tail = jnp.exp(total - cum_l)
+            enter = enter_ref[tile]
+            arrive_parts = halves(arrive)
+            dx_state = mm3(b_parts, arrive_parts, 1, 0) * tail
+            dx = dx_state
+            for h in range(per_tile):
+                row = cumt_ref[pl.ds(tile * per_tile + h, 1), :]
+                col = cum_l[:, h * width : h * width + 1]
+                spread = jnp.exp(jnp.minimum(row - col, 0.0))
+                kernel = halves(spread * score_ref[...])
+                own = jnp.where((lane // width) == h, dy, 0.0).astype(bf16)
+                dx = dx + (mm(kernel[0], own, 1, 0) + mm(kernel[1], own, 1, 0))
+                pairs = mm(x_parts[0], own, 1, 1) + mm(x_parts[1], own, 1, 1)
+                dscore_ref[...] += spread * pairs
+            dread_ref[...] += mm3(reads, halves(enter), 1, 1)
+            dwrite_ref[...] += mm3(halves(x * tail), arrive_parts, 1, 1)
+            ends = jnp.sum(x * dx_state, axis=0, keepdims=True) + jnp.exp(total) * jnp.sum(
+                enter * arrive, axis=0, keepdims=True
+            )
+            dcum = dy * ypre_ref[:, cols] - x * dx + jnp.where(final_row, ends, 0.0)
+            own_head = pick[0:LANES, :]
+            for part in halves(dcum):
+                dcum_ref[...] += mm(part, own_head, 1, 1)
+            for part in halves(dx * values):
+                dstep_ref[...] += mm(part, own_head, 1, 1)
+            dvalues = step_l * dx + skip_ref[0:1, cols] * dy
+            dpre = dvalues * sig * (1.0 + pre * (1.0 - sig))
+            dpre_ref[0:rows, cols] = dpre
+            conv_grad_ref[:, cols] = tap_grads(dpre, jnp.sum(dy * values, axis=0, keepdims=True))
+
+            ring.round(tile - COT_AT, cot_chunks, COT_SPACING)
+
+            return carry
+
+        lax.fori_loop(0, tiles, one, 0)
+        for at in range(tiles - COT_AT, cot_chunks + COT_SPACING * ring.reach):
+            ring.round(at, cot_chunks, COT_SPACING)
+
+        dscore = halves(jnp.where(later, dscore_ref[...], 0.0))
+        dshared = (
+            dwrite_ref[...] + mm3(dscore, c_parts, 1, 0),
+            dread_ref[...] + mm3(dscore, b_parts, 0, 0),
+        )
+        for i in range(2):
+            start = inner + i * N
+            pre, sig = conv_tile(conv_ref, halo_ref, u_ref, taps_ref, start, rows)
+            dpre = dshared[i] * sig * (1.0 + pre * (1.0 - sig))
+            dpre_ref[0:rows, start : start + N] = dpre
+            conv_grad_ref[:, start : start + N] = tap_grads(dpre, jnp.zeros((1, LANES), f32))
+
+        edge = seq_copy(
+            dpre_ref.at[pl.ds(0, 8), :],
+            dpre_ref.at[pl.ds(rows, 8), :],
+            edge_sem.at[0],
+            edge_sem.at[1],
+            left,
+        )
+
+        @pl.when(rank > 0)
+        def _():
+            edge.start()
+
+        upper = (iota((rows, rows), 1) >= iota((rows, rows), 0)).astype(f32).astype(bf16)
+        ddecay = sum(mm(upper, part, 1, 0) for part in thirds(dcum_ref[...]))
+        exp_rate = jnp.exp(heads_ref[1:2, :])
+        drate = (dstep_ref[...] - ddecay * exp_rate) * jax.nn.sigmoid(
+            u_ref[:, conv_width:].astype(f32) + heads_ref[0:1, :]
+        )
+        head_grad_ref[...] = jnp.concatenate(
+            [
+                jnp.sum(drate, axis=0, keepdims=True),
+                jnp.sum(ddecay * (-step * exp_rate), axis=0, keepdims=True),
+                jnp.zeros((6, LANES), f32),
+            ],
+            axis=0,
+        )
+        dproj_ref[:, conv_width : conv_width + LANES] = drate.astype(bf16)
+        dproj_ref[:, conv_width + LANES :] = jnp.zeros(
+            (rows, dproj_ref.shape[1] - conv_width - LANES), bf16
+        )
+
+        @pl.when(rank == last)
+        def _():
+            dpre_ref[rows : rows + 8, :] = jnp.zeros((8, conv_width), f32)
 
         @pl.when(rank < last)
         def _():
-            chain(tile).wait_recv()
-
-        @pl.when(rank == last)
-        def _():
-            arrive_ref[tile] = jnp.zeros((N, LANES), f32)
-
-        arrive = arrive_ref[tile]
-        leave_ref[tile] = jnp.exp(total) * arrive + denter
+            edge.wait_recv()
+
+        def unconv(tile, carry):
+            cols = pl.ds(pl.multiple_of(tile * LANES, LANES), LANES)
+            taps = taps_ref[:, cols]
+            du = taps[3:4, :] * dpre_ref[0:rows, cols]
+            for k in range(3):
+                du = du + taps[k : k + 1, :] * dpre_ref[3 - k : 3 - k + rows, cols]
+            dproj_ref[:, cols] = du.astype(bf16)
+            return carry
+
+        lax.fori_loop(0, conv_width // LANES, unconv, 0)
 
         @pl.when(rank > 0)
         def _():
-            chain(tile).start()
-
-        pre, sig = conv_tile(conv_ref, halo_ref, u_ref, taps_ref, start, rows)
-        values = pre * sig
-        x = values * step_l
-        x_parts = halves(x)
-        tail = jnp.exp(total - cum_l)
-        enter = enter_ref[tile]
-        arrive_parts = halves(arrive)
-        dx_state = mm3(b_parts, arrive_parts, 1, 0) * tail
-        dx = dx_state
-        for h in range(per_tile):
-            row = cumt_ref[pl.ds(tile * per_tile + h, 1), :]
-            col = cum_l[:, h * width : h * width + 1]
-            spread = jnp.exp(jnp.minimum(row - col, 0.0))
-            kernel = halves(spread * score_ref[...])
-            own = jnp.where((lane // width) == h, dy, 0.0).astype(bf16)
-            dx = dx + (mm(kernel[0], own, 1, 0) + mm(kernel[1], own, 1, 0))
-            pairs = mm(x_parts[0], own, 1, 1) + mm(x_parts[1], own, 1, 1)
-            dscore_ref[...] += spread * pairs
-        dread_ref[...] += mm3(reads, halves(enter), 1, 1)
-        dwrite_ref[...] += mm3(halves(x * tail), arrive_parts, 1, 1)
-        ends = jnp.sum(x * dx_state, axis=0, keepdims=True) + jnp.exp(total) * jnp.sum(
-            enter * arrive, axis=0, keepdims=True
-        )
-        dcum = dy * ypre_ref[:, cols] - x * dx + jnp.where(final_row, ends, 0.0)
-        own_head = pick[0:LANES, :]
-        for part in halves(dcum):
-            dcum_ref[...] += mm(part, own_head, 1, 1)
-        for part in halves(dx * values):
-            dstep_ref[...] += mm(part, own_head, 1, 1)
-        dvalues = step_l * dx + skip_ref[0:1, cols] * dy
-        dpre = dvalues * sig * (1.0 + pre * (1.0 - sig))
-        dpre_ref[0:rows, cols] = dpre
-        conv_grad_ref[:, cols] = tap_grads(dpre, jnp.sum(dy * values, axis=0, keepdims=True))
-        return carry
-
-    lax.fori_loop(0, tiles, one, 0)
-
-    dscore = halves(jnp.where(later, dscore_ref[...], 0.0))
-    dshared = (
-        dwrite_ref[...] + mm3(dscore, c_parts, 1, 0),
-        dread_ref[...] + mm3(dscore, b_parts, 0, 0),
-    )
-    for i in range(2):
-        start = inner + i * N
-        pre, sig = conv_tile(conv_ref, halo_ref, u_ref, taps_ref, start, rows)
-        dpre = dshared[i] * sig * (1.0 + pre * (1.0 - sig))
-        dpre_ref[0:rows, start : start + N] = dpre
-        conv_grad_ref[:, start : start + N] = tap_grads(dpre, jnp.zeros((1, LANES), f32))
-
-    edge = seq_copy(
-        dpre_ref.at[pl.ds(0, 8), :],
-        dpre_ref.at[pl.ds(rows, 8), :],
-        halo_sem.at[0],
-        halo_sem.at[1],
-        left,
-    )
-
-    @pl.when(rank > 0)
-    def _():
-        edge.start()
-
-    upper = (iota((rows, rows), 1) >= iota((rows, rows), 0)).astype(f32).astype(bf16)
-    ddecay = sum(mm(upper, part, 1, 0) for part in thirds(dcum_ref[...]))
-    exp_rate = jnp.exp(heads_ref[1:2, :])
-    drate = (dstep_ref[...] - ddecay * exp_rate) * jax.nn.sigmoid(
-        u_ref[:, conv_width:].astype(f32) + heads_ref[0:1, :]
-    )
-    head_grad_ref[...] = jnp.concatenate(
-        [
-            jnp.sum(drate, axis=0, keepdims=True),
-            jnp.sum(ddecay * (-step * exp_rate), axis=0, keepdims=True),
-            jnp.zeros((6, LANES), f32),
-        ],
-        axis=0,
-    )
-    dproj_ref[:, conv_width : conv_width + LANES] = drate.astype(bf16)
-    dproj_ref[:, conv_width + LANES :] = jnp.zeros(
-        (rows, dproj_ref.shape[1] - conv_width - LANES), bf16
-    )
-
-    @pl.when(rank == last)
-    def _():
-        dpre_ref[rows : rows + 8, :] = jnp.zeros((8, conv_width), f32)
-
-    @pl.when(rank < last)
-    def _():
-        edge.wait_recv()
-
-    def unconv(tile, carry):
-        cols = pl.ds(pl.multiple_of(tile * LANES, LANES), LANES)
-        taps = taps_ref[:, cols]
-        du = taps[3:4, :] * dpre_ref[0:rows, cols]
-        for k in range(3):
-            du = du + taps[k : k + 1, :] * dpre_ref[3 - k : 3 - k + rows, cols]
-        dproj_ref[:, cols] = du.astype(bf16)
-        return carry
-
-    lax.fori_loop(0, conv_width // LANES, unconv, 0)
-
-    @pl.when(rank > 0)
-    def _():
-        edge.wait_send()
-
-        def drain(tile, carry):
-            chain(tile).wait_send()
+            edge.wait_send()
+
+            def drain(tile, carry):
+                chain(tile).wait_send()
+                return carry
+
+            lax.fori_loop(0, tiles, drain, 0)
+
+
+        def finish_ring(chunk, carry):
+            ring.wait_pair(chunk)
+            ring.finish(chunk)
             return carry
 
-        lax.fori_loop(0, tiles, drain, 0)
-
-    for which in range(2):
-        own_copies[which].wait()
-        for i in range(1, group):
-            turn(i, which, lax.rem(me + i, group), me).wait_send()
-            origin = lax.rem(me + group - i, group)
-            turn(i, which, origin, origin).wait_recv()
+        lax.fori_loop(0, cot_chunks, finish_ring, 0)
+
+    cot_ring_sems = ring_sems[15:]
+    backward()
+    post_turn.finish()
+    normed_turn.finish()
 
 
 def vmem(count):
@@ -817,29 +803,33 @@
     return pl.pallas_call(
         functools.partial(front_kernel, sizes),
         out_shape=(
-            shape((rows, scan_width), bf16),
-            shape((rows, inner), f32),
-            shape((tiles, N, LANES), f32),
-            shape((HALO, conv_width), bf16),
-            shape((rows, LANES), f32),
-            shape((rows, LANES), f32),
-            shape((LANES, rows), f32),
-            shape((8, conv_width), f32),
             shape((8, model_width), f32),
-            shape((rows, inner), bf16),
             shape((rows, inner), bf16),
             shape((1, inner), f32),
             shape((rows, inner), bf16),
-            shape((model_width, rows), bf16),
-            shape((inner, rows), bf16),
+            shape((own_in, group * rows), bf16),
+            shape((own_out, group * rows), bf16),
+            shape((rows, -(-scan_width // WIDE) * WIDE), bf16),
+            shape((8, conv_width), f32),
             shape((8, LANES), f32),
             shape((group // 2, 2, own_in, scan_width), bf16),
             shape((group // 2, 2, own_in, inner), bf16),
             shape((group // 2, 2, own_out, model_width), bf16),
+            shape((model_width // WIDE, 2, group // 2, rows, WIDE), bf16),
         ),
         in_specs=[anywhere] * 2 + vmem(5),
-        out_specs=tuple(vmem(16) + [anywhere] * 3),
+        out_specs=tuple(vmem(9) + [anywhere] * 4),
         scratch_shapes=[
+            pltpu.VMEM((rows, scan_width), bf16),
+            pltpu.VMEM((rows, inner), f32),
+            pltpu.VMEM((tiles, N, LANES), f32),
+            pltpu.VMEM((HALO, conv_width), bf16),
+            pltpu.VMEM((rows, LANES), f32),
+            pltpu.VMEM((rows, LANES), f32),
+            pltpu.VMEM((LANES, rows), f32),
+            pltpu.VMEM((8, conv_width), f32),
+            pltpu.VMEM((rows, inner), bf16),
+            pltpu.VMEM((inner, rows), bf16),
             pltpu.VMEM(in_shard.shape, f32),
             pltpu.VMEM(out_shard.shape, f32),
             pltpu.VMEM((own_in, scan_width), bf16),
@@ -857,47 +847,7 @@
             pltpu.VMEM((rows, inner), f32),
             pltpu.VMEM((rows, inner), f32),
             pltpu.VMEM((rows, inner), f32),
-            dma((tiles,)),
-            dma((tiles,)),
-            dma((2,)),
-            dma((group,)),
-            dma((group,)),
-            dma((in_chunks + 1,)),
-            dma((2,)),
-        ]
-        + PlaneRing.semaphores(in_chunks)
-        + PlaneRing.semaphores(in_chunks)
-        + PlaneRing.semaphores(out_chunks),
-        compiler_params=pltpu.CompilerParams(
-            collective_id=1, has_side_effects=True, vmem_limit_bytes=58 * 2**20
-        ),
-        cost_estimate=pl.CostEstimate(
-            flops=10**10, bytes_accessed=10**8, transcendentals=4 * 10**6
-        ),
-    )(in_shard, out_shard, small, hidden, cot, heads, skip)
-
-
-def scan_backward(
-    u, halo, step, cum, cumt, heads, skip, taps, dy, ypre, enter, normed_t, post_t, sizes
-):
-    rows, inner, tiles, _ = sizes
-    conv_width = inner + 2 * N
-    shape = jax.ShapeDtypeStruct
-    group = lax.axis_size("dp")
-    turn_rows = (normed_t.shape[0] + post_t.shape[0]) // group
-    return pl.pallas_call(
-        functools.partial(backward_kernel, sizes),
-        out_shape=(
-            shape((rows, -(-u.shape[1] // WIDE) * WIDE), bf16),
-            shape((8, conv_width), f32),
-            shape((8, LANES), f32),
-            shape((turn_rows, group * rows), bf16),
-        ),
-        in_specs=vmem(11) + [pl.BlockSpec(memory_space=pl.ANY)] * 2,
-        out_specs=tuple(vmem(3) + [pl.BlockSpec(memory_space=pl.ANY)]),
-        scratch_shapes=[
-            pltpu.VMEM((HALO + rows, LANES), f32),
-            pltpu.VMEM((rows, rows), f32),
+            pltpu.VMEM((model_width, rows), bf16),
             pltpu.VMEM((rows, rows), f32),
             pltpu.VMEM((rows, N), f32),
             pltpu.VMEM((rows, N), f32),
@@ -905,19 +855,31 @@
             pltpu.VMEM((rows, LANES), f32),
             pltpu.VMEM((rows + 8, conv_width), f32),
             pltpu.VMEM((tiles, N, LANES), f32),
-            pltpu.VMEM((tiles, N, LANES), f32),
-            pltpu.SemaphoreType.DMA((tiles,)),
-            pltpu.SemaphoreType.DMA((tiles,)),
-            pltpu.SemaphoreType.DMA((2,)),
-            pltpu.SemaphoreType.DMA((group, 2)),
-            pltpu.SemaphoreType.DMA((group, 2)),
-            pltpu.SemaphoreType.DMA((2,)),
-        ],
+            dma((tiles,)),
+            dma((tiles,)),
+            dma((2,)),
+            dma((tiles,)),
+            dma((tiles,)),
+            dma((2,)),
+            dma((group,)),
+            dma((group,)),
+            dma((2, group)),
+            dma((2, group)),
+            dma((2,)),
+            dma((in_chunks + 1,)),
+            dma((2,)),
+        ]
+        + PlaneRing.semaphores(in_chunks)
+        + PlaneRing.semaphores(in_chunks)
+        + PlaneRing.semaphores(out_chunks)
+        + PlaneRing.semaphores(model_width // WIDE),
         compiler_params=pltpu.CompilerParams(
-            collective_id=2, has_side_effects=True, vmem_limit_bytes=40 * 2**20
+            collective_id=1, has_side_effects=True, vmem_limit_bytes=60 * 2**20
         ),
-        cost_estimate=pl.CostEstimate(flops=6 * 10**9, bytes_accessed=2 * 10**7, transcendentals=4 * 10**6),
-    )(u, halo, step, cum, cumt, heads, skip, taps, dy, ypre, enter, normed_t, post_t)
+        cost_estimate=pl.CostEstimate(
+            flops=10**10, bytes_accessed=10**8, transcendentals=4 * 10**6
+        ),
+    )(in_shard, out_shard, small, hidden, cot, heads, skip)
 
 
 def plane_copy(src, dst, send, recv, to):
@@ -929,6 +891,52 @@
         device_id={"dp": to},
         device_id_type=MESH,
     )
+
+
+class PlaneTurn:
+    def __init__(self, source, target, height, width, sems):
+        self.source, self.target, self.height, self.width = source, target, height, width
+        self.send, self.recv, self.own_sem = sems
+        self.me = lax.axis_index("dp")
+        self.group = lax.axis_size("dp")
+
+    def rows_for(self, device):
+        return self.source.at[
+            pl.ds(pl.multiple_of(device * self.height, self.height), self.height), :
+        ]
+
+    def columns_of(self, device):
+        start = pl.multiple_of(slot_of(device, self.group) * self.width, self.width)
+        return self.target.at[:, pl.ds(start, self.width)]
+
+    def copy(self, i, peer, origin):
+        return plane_copy(
+            self.rows_for(peer), self.columns_of(origin), self.send.at[i], self.recv.at[i], peer
+        )
+
+    def own(self):
+        return pltpu.make_async_copy(
+            self.rows_for(self.me), self.columns_of(self.me), self.own_sem
+        )
+
+    def start(self):
+        for i in range(1, self.group):
+            self.copy(i, lax.rem(self.me + i, self.group), self.me).start()
+        self.own().start()
+
+    def arrive(self):
+        for i in range(1, self.group):
+            origin = lax.rem(self.me + self.group - i, self.group)
+            self.copy(i, origin, origin).wait_recv()
+        self.own().wait()
+
+    def sent(self):
+        for i in range(1, self.group):
+            self.copy(i, lax.rem(self.me + i, self.group), self.me).wait_send()
+
+    def finish(self):
+        self.arrive()
+        self.sent()
 
 
 class PlaneRing:
@@ -1049,7 +1057,8 @@
 
 def tail_kernel(
     sizes,
-    turned_ref,
+    normed_turned_ref,
+    post_turned_ref,
     cot_ref,
     gate_ref,
     scan_ref,
@@ -1161,35 +1170,45 @@
         (ring_send, ring_recv, pair_send, pair_recv, own_sem),
     )
 
-    def load_copy(chunk):
-        slot = lax.rem(chunk, 2)
-        return pltpu.make_async_copy(
-            gathered_ref.at[chunk], loaded_ref.at[slot], load_sem.at[slot]
-        )
+    def fetch(step, action):
+        order = jnp.where(step < out_steps, step // 2, step - out_steps + out_steps // 2)
+        slot = lax.rem(order, 2)
+
+        @pl.when((step < out_steps) & (lax.rem(step, 2) == 0))
+        def _():
+            action(
+                pltpu.make_async_copy(
+                    cot_ref.at[step // 2], loaded_ref.at[slot], load_sem.at[slot]
+                )
+            )
+
+        @pl.when(step >= out_steps)
+        def _():
+            action(
+                pltpu.make_async_copy(
+                    gathered_ref.at[step - out_steps], loaded_ref.at[slot], load_sem.at[slot]
+                )
+            )
+
+        return slot
 
     def compute(step):
+        arrived = loaded_ref.at[fetch(step, lambda copy: copy.wait())]
+
         @pl.when(step < out_steps)
         def _():
-            cols = pl.ds(pl.multiple_of(step * LANES, LANES), LANES)
-            cot = jnp.concatenate(
-                [
-                    cot_ref[pl.ds((2 * (slot % chips) + slot // chips) * rows, rows), cols]
-                    for slot in range(group)
-                ],
-                axis=0,
+            some = pl.ds(pl.multiple_of(lax.rem(step, 2) * own_in, own_in), own_in)
+            value_ref[...] = mm(
+                post_turned_ref[some, :], arrived[...].reshape(group * rows, WIDE), 1, 0
             )
-            for half in range(2):
-                rows_at = own_in * (1 + half)
-                value_ref[:, half * LANES : (half + 1) * LANES] = mm(
-                    turned_ref[rows_at : rows_at + own_in, :], cot, 1, 0
-                )
 
         @pl.when(step >= out_steps)
         def _():
-            chunk = step - out_steps
-            load_copy(chunk).wait()
-            arrived = loaded_ref[lax.rem(chunk, 2)].reshape(group * rows, WIDE)
-            value_ref[...] = mm(turned_ref[0:own_in, :], arrived, 1, 0)
+            value_ref[...] = mm(
+                normed_turned_ref[...], arrived[...].reshape(group * rows, WIDE), 1, 0
+            )
+
+    fetch(0, lambda copy: copy.start())
 
     def weight_copy(item, action):
         slot = lax.rem(item, 2)
@@ -1291,109 +1310,130 @@
 
     weight_copy(0, lambda copy: copy.start())
 
-    def up_copy(source, target, step, recv, to):
-        return seq_copy(source, target, up_send.at[step], recv.at[step], to)
-
-    def up(value, inbox, total, step):
+    def piece(ref, part, parts):
+        if parts == 1:
+            return ref
+        size = own_in // parts
+        start = part * size if isinstance(part, int) else pl.multiple_of(part * size, size)
+        return ref.at[pl.ds(start, size), :]
+
+    def up_copy(source, target, step, part, parts, recv, to):
+        return seq_copy(
+            piece(source, part, parts),
+            piece(target, part, parts),
+            up_send.at[step, part],
+            recv.at[step, part],
+            to,
+        )
+
+    def down_copy(total, step, part, parts, send, to):
+        return seq_copy(
+            piece(total, part, parts),
+            piece(total, part, parts),
+            send.at[step, part],
+            total_recv.at[step, part],
+            to,
+        )
+
+    def up(value, inbox, total, step, parts, after):
         edge = ((rank == 0) | (rank == last)) & (rank != root)
-        inner = (rank != root) & (rank > 0) & (rank < last)
-
-        @pl.when(edge)
-        def _():
-            inbox[...] = value[...]
-
-        @pl.when(inner)
-        def _():
-            up_copy(inbox, inbox, step, inbox_recv, left).wait_recv()
-            inbox[...] += value[...]
-
+        inner_place = (rank != root) & (rank > 0) & (rank < last)
+        for part in range(parts):
+            here = piece(value, part, parts)
+            inbox_here = piece(inbox, part, parts)
+            total_here = piece(total, part, parts)
+
+            @pl.when(edge)
+            def _(here=here, inbox_here=inbox_here):
+                inbox_here[...] = here[...]
+
+            @pl.when(inner_place)
+            def _(here=here, inbox_here=inbox_here, part=part):
+                up_copy(inbox, inbox, step, part, parts, inbox_recv, left).wait_recv()
+                inbox_here[...] += here[...]
+
+            @pl.when(rank < root)
+            def _(part=part):
+                up_copy(inbox, inbox, step, part, parts, inbox_recv, right).start()
+
+            @pl.when(rank == root + 1)
+            def _(part=part):
+                up_copy(inbox, total, step, part, parts, other_recv, left).start()
+
+            @pl.when(rank > root + 1)
+            def _(part=part):
+                up_copy(inbox, inbox, step, part, parts, inbox_recv, left).start()
+
+            @pl.when(rank == root)
+            def _(here=here, inbox_here=inbox_here, total_here=total_here, part=part):
+                result = here[...]
+                if root > 0:
+                    up_copy(inbox, inbox, step, part, parts, inbox_recv, left).wait_recv()
+                    result = result + inbox_here[...]
+                if root < last:
+                    up_copy(total, total, step, part, parts, other_recv, right).wait_recv()
+                    result = result + total_here[...]
+                total_here[...] = result
+                if root > 0:
+                    down_copy(total, step, part, parts, left_send, left).start()
+                if root < last:
+                    down_copy(total, step, part, parts, right_send, right).start()
+
+            after(part)
+
+    def down(total, step, part, parts):
         @pl.when(rank < root)
         def _():
-            up_copy(inbox, inbox, step, inbox_recv, right).start()
-
-        @pl.when(rank == root + 1)
-        def _():
-            up_copy(inbox, total, step, other_recv, left).start()
-
-        @pl.when(rank > root + 1)
-        def _():
-            up_copy(inbox, inbox, step, inbox_recv, left).start()
-
-        @pl.when(rank == root)
-        def _():
-            result = value[...]
-            if root > 0:
-                up_copy(inbox, inbox, step, inbox_recv, left).wait_recv()
-                result = result + inbox[...]
-            if root < last:
-                up_copy(total, total, step, other_recv, right).wait_recv()
-                result = result + total[...]
-            total[...] = result
-            if root > 0:
-                down_copy(total, step, left_send, left).start()
-            if root < last:
-                down_copy(total, step, right_send, right).start()
-
-    def down_copy(total, step, send, to):
-        return seq_copy(total, total, send.at[step], total_recv.at[step], to)
-
-    def down(total, step):
-        @pl.when(rank < root)
-        def _():
-            down_copy(total, step, left_send, left).wait_recv()
+            down_copy(total, step, part, parts, left_send, left).wait_recv()
 
             @pl.when(rank > 0)
             def _():
-                down_copy(total, step, left_send, left).start()
+                down_copy(total, step, part, parts, left_send, left).start()
 
         @pl.when(rank > root)
         def _():
-            down_copy(total, step, right_send, right).wait_recv()
+            down_copy(total, step, part, parts, right_send, right).wait_recv()
 
             @pl.when(rank < last)
             def _():
-                down_copy(total, step, right_send, right).start()
-
-    def store_out(step, half):
-        cols = pl.ds(pl.multiple_of(step * LANES, LANES), LANES)
-        return pltpu.make_async_copy(
-            total_ref.at[step, :, pl.ds(half * LANES, LANES)],
-            out_ref.at[pl.ds(half * own_in, own_in), cols],
-            store_sem.at[step, half],
-        )
-
-    def store_in(step):
-        cols = pl.ds(pl.multiple_of((step - out_steps) * WIDE, WIDE), WIDE)
-        return pltpu.make_async_copy(
-            total_ref.at[step], in_ref.at[:, cols], store_sem.at[step, 0]
-        )
+                down_copy(total, step, part, parts, right_send, right).start()
+
+    def drain(inbox, total, step, parts):
+        for part in range(parts):
+
+            @pl.when(rank < root)
+            def _(part=part):
+                up_copy(inbox, inbox, step, part, parts, inbox_recv, right).wait_send()
+
+            @pl.when(rank > root)
+            def _(part=part):
+                up_copy(inbox, inbox, step, part, parts, inbox_recv, left).wait_send()
+
+            @pl.when((rank <= root) & (rank > 0))
+            def _(part=part):
+                down_copy(total, step, part, parts, left_send, left).wait_send()
+
+            @pl.when((rank >= root) & (rank < last))
+            def _(part=part):
+                down_copy(total, step, part, parts, right_send, right).wait_send()
 
     def stored(step, action):
         @pl.when(step < out_steps)
         def _():
-            for half in range(2):
-                action(store_out(step, half))
+            some = pl.ds(pl.multiple_of(lax.rem(step, 2) * own_in, own_in), own_in)
+            cols = pl.ds(pl.multiple_of(step // 2 * WIDE, WIDE), WIDE)
+            action(
+                pltpu.make_async_copy(
+                    total_ref.at[step], out_ref.at[some, cols], store_sem.at[step]
+                )
+            )
 
         @pl.when(step >= out_steps)
         def _():
-            action(store_in(step))
-
-    def drain(inbox, total, step):
-        @pl.when(rank < root)
-        def _():
-            up_copy(inbox, inbox, step, inbox_recv, right).wait_send()
-
-        @pl.when(rank > root)
-        def _():
-            up_copy(inbox, inbox, step, inbox_recv, left).wait_send()
-
-        @pl.when((rank <= root) & (rank > 0))
-        def _():
-            down_copy(total, step, left_send, left).wait_send()
-
-        @pl.when((rank >= root) & (rank < last))
-        def _():
-            down_copy(total, step, right_send, right).wait_send()
+            cols = pl.ds(pl.multiple_of((step - out_steps) * WIDE, WIDE), WIDE)
+            action(
+                pltpu.make_async_copy(total_ref.at[step], in_ref.at[:, cols], store_sem.at[step])
+            )
 
     behind = lag * (jnp.maximum(rank - root, 0) + jnp.maximum(root - rank, 0))
 
@@ -1405,17 +1445,35 @@
             def _(chunk=chunk, stage=stage):
                 ring.stage(chunk, stage)
 
-        ready = step - (out_steps - 1)
-
-        @pl.when((ready >= 0) & (ready < chunks))
-        def _():
-            ring.wait_pair(ready)
-            load_copy(ready).start()
+        @pl.when((step + 1 >= out_steps) & (step + 1 < steps))
+        def _():
+            ring.wait_pair(step + 1 - out_steps)
+
+        @pl.when(step + 1 < steps)
+        def _():
+            fetch(step + 1, lambda copy: copy.start())
+
+        def down_late(part):
+            late = PARTS * step + part - behind
+            late_step = late // PARTS
+            late_part = lax.rem(late, PARTS)
+
+            @pl.when((late >= 0) & (late_step < steps))
+            def _():
+                down(total_ref.at[late_step], late_step, late_part, PARTS)
+
+                @pl.when(late_part == PARTS - 1)
+                def _():
+                    stored(late_step, lambda copy: copy.start())
+
+            @pl.when(late == PARTS * steps)
+            def _():
+                down(small_out_ref, steps, 0, 1)
 
         @pl.when(step < steps)
         def _():
             compute(step)
-            up(value_ref, inbox_ref.at[step], total_ref.at[step], step)
+            up(value_ref, inbox_ref.at[step], total_ref.at[step], step, PARTS, down_late)
 
         @pl.when(step == steps)
         def _():
@@ -1426,34 +1484,28 @@
                 scale_copy(i, origin, me).wait_send()
                 scale_copy(i, origin, origin).wait_recv()
             small_value_ref[...] = jnp.sum(small_all_ref[...], axis=0)
-            up(small_value_ref, small_inbox_ref, small_out_ref, steps)
+            up(small_value_ref, small_inbox_ref, small_out_ref, steps, 1, lambda part: None)
+
+        @pl.when(step >= steps)
+        def _():
+            for part in range(PARTS):
+                down_late(part)
 
         @pl.when(step < items)
         def _():
             local_product(step)
 
-        late = step - behind
-
-        @pl.when((late >= 0) & (late < steps))
-        def _():
-            down(total_ref.at[late], late)
-            stored(late, lambda copy: copy.start())
-
-        @pl.when(late == steps)
-        def _():
-            down(small_out_ref, steps)
-
         return carry
 
-    lax.fori_loop(0, steps + 1 + behind, round_, 0)
+    lax.fori_loop(0, steps + 1 + (behind + PARTS - 1) // PARTS, round_, 0)
 
     def finish(step, carry):
-        drain(inbox_ref.at[step], total_ref.at[step], step)
+        drain(inbox_ref.at[step], total_ref.at[step], step, PARTS)
         stored(step, lambda copy: copy.wait())
         return carry
 
     lax.fori_loop(0, steps, finish, 0)
-    drain(small_inbox_ref, small_out_ref, steps)
+    drain(small_inbox_ref, small_out_ref, steps, 1)
 
     def finish_ring(chunk, carry):
         ring.finish(chunk)
@@ -1463,19 +1515,20 @@
 
 
 def reduce_gradients(
-    turned, cot_all, gate_grad, scan_grad, small, hidden, cot, post, scale, matrices, own_in
+    normed_turned, post_turned, cot_all, gate_grad, scan_grad, small, hidden, cot, post, scale, matrices
 ):
     size = lax.axis_size("seq")
     group = lax.axis_size("dp")
     rows = gate_grad.shape[0]
-    model_width = cot_all.shape[1]
-    out_steps = model_width // LANES
+    own_in = normed_turned.shape[0]
+    model_width = hidden.shape[1]
+    out_steps = 2 * (model_width // WIDE)
     gate_steps = gate_grad.shape[1] // WIDE
     chunks = gate_steps + scan_grad.shape[1] // WIDE
     steps = out_steps + chunks
     reach = group // 4
     spacing = min(3, (out_steps - 2) // reach)
-    sizes = (rows, own_in, out_steps, gate_steps, steps, size // 2, 3, spacing)
+    sizes = (rows, own_in, out_steps, gate_steps, steps, size // 2, LAG, spacing)
     assert chunks + model_width // WIDE <= steps
     shape = jax.ShapeDtypeStruct
     dma = pltpu.SemaphoreType.DMA
@@ -1491,7 +1544,7 @@
             shape((rows, model_width), f32),
             shape((chunks, 2, group // 2, rows, WIDE), bf16),
         ),
-        in_specs=vmem(9) + [anywhere] * 3,
+        in_specs=vmem(2) + [anywhere] + vmem(7) + [anywhere] * 3,
         out_specs=(anywhere, anywhere) + tuple(vmem(3)) + (anywhere,),
         scratch_shapes=[
             pltpu.VMEM((own_in, WIDE), f32),
@@ -1505,9 +1558,9 @@
             pltpu.VMEM((rows, model_width), f32),
             pltpu.VMEM((8, model_width), f32),
         ]
-        + [dma((steps + 1,))] * 6
+        + [dma((steps + 1, PARTS))] * 6
         + [
-            dma((steps, 2)),
+            dma((steps,)),
             *PlaneRing.semaphores(chunks),
             dma((2,)),
             *[dma((group,))] * 4,
@@ -1519,7 +1572,19 @@
         cost_estimate=pl.CostEstimate(
             flops=2 * 10**10, bytes_accessed=2 * 10**8, transcendentals=0
         ),
-    )(turned, cot_all, gate_grad, scan_grad, small, hidden, cot, post, scale, *matrices)
+    )(
+        normed_turned,
+        post_turned,
+        cot_all,
+        gate_grad,
+        scan_grad,
+        small,
+        hidden,
+        cot,
+        post,
+        scale,
+        *matrices,
+    )
 
 
 def on_device(
@@ -1573,34 +1638,23 @@
     head_rows = jnp.pad(headcoefs, ((0, 8 - headcoefs.shape[0]), (0, LANES - heads)))
     skip = jnp.repeat(headcoefs[2:3], width, axis=1)
     (
-        scan_in,
-        ypre,
-        enter,
-        halo,
-        step,
-        cum,
-        cumt,
-        taps,
         pre_scale,
-        dy,
         gate_grad,
         postnorm_grad,
         post_low,
-        normed_t,
-        post_t,
-        token,
+        normed_turned,
+        post_turned,
+        scan_grad,
+        conv_grad,
+        head_grad,
         scan_matrix,
         gate_matrix,
         out_matrix,
+        cot_all,
     ) = front(inproject, outproject, small, hidden_low, cot_low, head_rows, skip, sizes)
     scan_matrix = scan_matrix.reshape(model_width, -1)
     gate_matrix = gate_matrix.reshape(model_width, inner)
     out_matrix = out_matrix.reshape(inner, model_width)
-    cot_all = lax.all_gather(cot_low + token[0, 0].astype(bf16), "dp", axis=0, tiled=True)
-    scan_grad, conv_grad, head_grad, turned = scan_backward(
-        scan_in, halo, step, cum, cumt, head_rows, skip, taps, dy, ypre, enter, normed_t, post_t, sizes
-    )
-
     head_sums = jnp.concatenate(
         [
             head_grad[:2, :heads],
@@ -1621,7 +1675,8 @@
     packed_lanes = -(-packed_size // (8 * LANES)) * LANES
     packed = jnp.pad(packed, ((0, 0), (0, 8 * packed_lanes - packed_size)))
     inproj_padded, outproj_owned, packed, output, input_gradient, _ = reduce_gradients(
-        turned,
+        normed_turned,
+        post_turned,
         cot_all,
         gate_grad,
         scan_grad,
@@ -1631,7 +1686,6 @@
         post_low,
         pre_scale,
         (gate_matrix, scan_matrix, out_matrix),
-        own_in,
     )
     inproj_owned = inproj_padded[:, :proj_width]
     prenorm_owned = lax.dynamic_slice_in_dim(packed[0, packed_lanes:], me * own_in, own_in, 0)

time: 476 us -> 454 us (0.954)
  between operations: 14.5 us -> 0.92 us
  local copies, waits for them, and re-layouts: 21.5 us -> 16.4 us
    pallas_call x1, Pallas kernels: 146 us -> 216 us  [front(): pl.pallas_call(functools.partial(front_kernel, sizes), out_shape=(shape((...]
    pallas_call x1 -> x0, Pallas kernels: 65.5 us -> none  [scan_backward(): pl.pallas_call(functools.partial(backward_kernel, sizes), out_shape=(shap...]
    unnamed x82 -> x46, local copies, waits for them, and re-layouts: 14 us -> 6.98 us
    pallas_call x1, Pallas kernels: 200 us -> 194 us  [reduce_gradients(): pl.pallas_call(functools.partial(tail_kernel, sizes), out_shape=(shape((o...]
  transfers between devices with their start and end apart: 1 -> 0, of which waited for: 1 -> 0; matrix products, arithmetic and copies ran while one was open for 1% -> 0% of each run, Pallas kernels for 14% -> 0%
where the time goes in v5:
time: 454 us; the launch traced here: 453 us
  Pallas kernels  410 us (90%)
  other arithmetic  25.8 us (6%)
  local copies, waits for them, and re-layouts  16.4 us (4%)
    pallas_call x1, Pallas kernels, front(): pl.pallas_call(functools.partial(front_kernel, sizes), out_shape=(shape((...  216 us
    pallas_call x1, Pallas kernels, reduce_gradients(): pl.pallas_call(functools.partial(tail_kernel, sizes), out_shape=(shape((o...  194 us
    sub x6, other arithmetic, adam_update(): weight - step_rate * (moment_hat / (jnp.sqrt(square_hat) + adam_eps) + de...  22.2 us

profile of v5, /device:TPU:0, one launch (start us, length us, event | category | flops | bytes accessed | tf_op | source)
XLA Modules:
  0.0 452.9 jit_solution(8574478150375032022)
XLA Ops:
  0.7 0.7 slice_bitcast_fusion
  1.4 0.1 broadcast_in_dim.12
  1.4 0.7 broadcast_in_dim.13.skip_ref
  2.1 0.7 convert.20
  2.8 0.7 convert.21
  3.5 0.7 convert.19
  4.2 0.6 pad.31.small_ref
  4.8 1.3 pad.32.heads_ref
  6.1 215.8 %shard_map.395 = (f32[8,1536]{1,0:T(8,128)}, bf16[256,3072]{1,0:T(8,128)(2,1)}, f32[1,3072]{1,0:T(1,128)}, bf16[256,3072]{1,0:T(8,128)(2,1)}, bf16[192,2048]{1,0...) custom-call(f32[192,6448]{1,0:T(8,128)} %in_shard_ref.1, ...), custom_call_target="tpu_custom_call" | custom-call | flops 10000000000 | bytes 100000000 | tf_op jit(solution)/shard_map/pallas_call | solution.py:803
  221.9 0.9 slice_reduce_fusion
  222.9 0.1 reshape.122
  223.0 0.1 reduce_sum.11
  223.1 0.7 slice.39
  223.8 0.1 broadcast_in_dim.14
  223.9 1.0 reshape.120
  224.9 0.1 copy.51
  224.9 0.1 reshape.121
  225.0 0.5 broadcast.80
  225.5 1.4 reduce.10
  226.9 0.1 concatenate.12
  227.0 0.7 copy.52
  227.7 193.9 %shard_map.396 = (f32[192,6656]{1,0:T(8,128)}, f32[384,1536]{1,0:T(8,128)}, f32[8,1920]{1,0:T(8,128)}, f32[256,1536]{1,0:T(8,128)}, f32[256,1536]{1,0:T(8,128)}, /*index=5*/bf16[26,2,4,256,256]{4,3,2,1,0:T(8,128)(2,1)}) custom-call(bf16[192,2048]{1,0:T(8,128)(2,1)} %get-tuple-element.44.normed_turned_ref, ...), custom_call_target="tpu_custom_call" | custom-call | flops 20000000000 | bytes 200000000 | tf_op jit(solution)/shard_map/pallas_call | solution.py:1537
  421.6 0.0 copy-start
  421.6 0.0 copy-start.1
  421.6 0.0 copy-start.2
  421.7 0.0 copy-start.3
  421.7 15.4 %multiply_subtract_fusion = (f32[192,6448]{1,0:T(8,128)}, f32[192,6448]{1,0:T(8,128)}, f32[192,6448]{1,0:T(8,128)}, f32[192,6448]{1,0:T(8,128)}) fusion(f32[192,6448]{1,0:T(8,128)} %in_shard_ref.1, f32[192,6448]{1,0:T(8,128)} %param.29, f32[192,6448]{1,0:T(8,128)} %param.35, f32[192,6656]{1,0:T(8,128)} %get-tuple-element.60), kind=kLoop, calls=%fused_computation.2 | loop fusion | flops 18570240 | bytes 39616512 | tf_op jit(solution)/shard_map/sub | solution.py:39
  437.1 0.0 copy-done
  437.1 0.0 copy-done.1
  437.1 0.0 copy-done.2
  437.1 1.0 copy-done.3
  438.1 0.0 copy-start.14
  438.2 0.0 copy-start.15
  438.2 0.0 copy-start.18
  438.2 0.0 copy-start.19
  438.2 0.0 copy-start.20
  438.2 0.0 copy-start.11
  438.2 0.0 copy-start.16
  438.2 0.0 copy-start.17
  438.2 4.3 multiply_subtract_fusion.1
  442.5 0.7 slice.43
  443.3 0.1 reshape.130
  443.3 0.0 copy-done.6
  443.4 0.0 copy-done.8
  443.4 0.0 copy-start.5
  443.4 0.6 multiply_subtract_fusion.2
  444.0 0.1 slice.49
  444.1 0.1 reshape.131
  444.2 0.0 copy-done.14
  444.2 0.0 copy-start.12
  444.2 0.6 multiply_subtract_fusion.4
  444.8 0.8 slice.41
  445.6 0.1 constant_dynamic-slice_fusion
  445.7 0.0 copy-done.20
  445.7 0.6 multiply_subtract_fusion.5
  446.3 0.7 slice_reduce_fusion.1
  447.0 0.0 copy-done.11
  447.0 0.0 copy-start.9
  447.0 0.6 multiply_subtract_fusion.3
  447.6 2.7 copy.56
  450.3 0.0 copy-done.4
  450.3 1.1 copy.57
  451.4 0.0 copy-done.12
  451.5 1.4 copy.58
  (25 shorter events, 0.1 us)
Async XLA Ops:
  421.6 15.5 %copy-start = (f32[384,1536]{1,0:T(8,128)S(1)}, f32[384,1536]{1,0:T(8,128)}, u32[]{:S(2)}) copy-start(f32[384,1536]{1,0:T(8,128)} %get-tuple-element.114) | copy-start | bytes 7077892
  421.6 15.5 %copy-start.1 = (f32[384,1536]{1,0:T(8,128)S(1)}, f32[384,1536]{1,0:T(8,128)}, u32[]{:S(2)}) copy-start(f32[384,1536]{1,0:T(8,128)} %out_shard_ref.1) | copy-start | bytes 7077892
  421.6 15.5 %copy-start.2 = (f32[384,1536]{1,0:T(8,128)S(1)}, f32[384,1536]{1,0:T(8,128)}, u32[]{:S(2)}) copy-start(f32[384,1536]{1,0:T(8,128)} %param.33) | copy-start | bytes 7077892
  421.7 16.5 %copy-start.3 = (f32[384,1536]{1,0:T(8,128)S(1)}, f32[384,1536]{1,0:T(8,128)}, u32[]{:S(2)}) copy-start(f32[384,1536]{1,0:T(8,128)} %param.39) | copy-start | bytes 7077892
  438.1 5.2 %copy-start.6 = (f32[5,416]{1,0:T(8,128)S(1)}, f32[5,416]{1,0:T(8,128)}, u32[]{:S(2)}) copy-start(f32[5,416]{1,0:T(8,128)} %param.24) | copy-start | bytes 24964
  438.1 5.2 %copy-start.7 = (f32[5,416]{1,0:T(8,128)S(1)}, f32[5,416]{1,0:T(8,128)}, u32[]{:S(2)}) copy-start(f32[5,416]{1,0:T(8,128)} %param.30) | copy-start | bytes 24964
  438.1 5.2 %copy-start.8 = (f32[5,416]{1,0:T(8,128)S(1)}, f32[5,416]{1,0:T(8,128)}, u32[]{:S(2)}) copy-start(f32[5,416]{1,0:T(8,128)} %param.36) | copy-start | bytes 24964
  438.1 6.0 %copy-start.10 = (f32[3,48]{1,0:T(4,128)S(1)}, f32[3,48]{1,0:T(4,128)}, u32[]{:S(2)}) copy-start(f32[3,48]{1,0:T(4,128)} %param.25) | copy-start | bytes 1732
  438.1 6.0 %copy-start.14 = (f32[3,48]{1,0:T(4,128)S(1)}, f32[3,48]{1,0:T(4,128)}, u32[]{:S(2)}) copy-start(f32[3,48]{1,0:T(4,128)} %param.31) | copy-start | bytes 1732
  438.2 6.0 %copy-start.15 = (f32[3,48]{1,0:T(4,128)S(1)}, f32[3,48]{1,0:T(4,128)}, u32[]{:S(2)}) copy-start(f32[3,48]{1,0:T(4,128)} %param.37) | copy-start | bytes 1732
  438.2 7.5 %copy-start.18 = (f32[192]{0:T(256)S(1)}, f32[192]{0:T(256)}, u32[]{:S(2)}) copy-start(f32[192]{0:T(256)} %param.22) | copy-start | bytes 2308
  438.2 7.5 %copy-start.19 = (f32[192]{0:T(256)S(1)}, f32[192]{0:T(256)}, u32[]{:S(2)}) copy-start(f32[192]{0:T(256)} %param.28) | copy-start | bytes 2308
  438.2 7.5 %copy-start.20 = (f32[192]{0:T(256)S(1)}, f32[192]{0:T(256)}, u32[]{:S(2)}) copy-start(f32[192]{0:T(256)} %param.34) | copy-start | bytes 2308
  438.2 8.8 %copy-start.11 = (f32[384]{0:T(512)S(1)}, f32[384]{0:T(512)}, u32[]{:S(2)}) copy-start(f32[384]{0:T(512)} %param.26) | copy-start | bytes 4612
  438.2 8.8 %copy-start.16 = (f32[384]{0:T(512)S(1)}, f32[384]{0:T(512)}, u32[]{:S(2)}) copy-start(f32[384]{0:T(512)} %param.32) | copy-start | bytes 4612
  438.2 8.8 %copy-start.17 = (f32[384]{0:T(512)S(1)}, f32[384]{0:T(512)}, u32[]{:S(2)}) copy-start(f32[384]{0:T(512)} %param.38) | copy-start | bytes 4612
  443.4 8.1 %copy-start.5 = (f32[5,416]{1,0:T(8,128)}, f32[5,416]{1,0:T(8,128)S(1)}, u32[]{:S(2)}) copy-start(f32[5,416]{1,0:T(8,128)S(1)} %reshape.130) | copy-start | bytes 24964
  444.2 7.3 %copy-start.12 = (f32[3,48]{1,0:T(4,128)}, f32[3,48]{1,0:T(4,128)S(1)}, u32[]{:S(2)}) copy-start(f32[3,48]{1,0:T(4,128)S(1)} %reshape.131) | copy-start | bytes 1732
  445.6 4.7 %copy-start.4 = (f32[256,1536]{1,0:T(8,128)S(1)}, f32[256,1536]{1,0:T(8,128)}, u32[]{:S(2)}) copy-start(f32[256,1536]{1,0:T(8,128)} %get-tuple-element.58) | copy-start | bytes 4718596
  445.7 5.8 %copy-start.13 = (f32[1,192]{1,0:T(1,128)}, f32[1,192]{1,0:T(1,128)S(1)}, u32[]{:S(2)}) copy-start(f32[1,192]{1,0:T(1,128)S(1)} %constant_dynamic-slice_fusion) | copy-start | bytes 2308
  447.0 4.4 copy-start.9

commit v6 on v5

--- a/solution.py
+++ b/solution.py
@@ -14,8 +14,9 @@
 HEIGHT = 32
 PARTS = 2
 LAG = 4
-COT_AT = 4
-COT_SPACING = 7
+COT_AT = 8
+EARLY = 6
+COT_SPACING = 5
 
 norm_eps = 1e-05
 beta_moment = 0.9
@@ -129,20 +130,19 @@
     sizes,
     in_shard_ref,
     out_shard_ref,
-    small_ref,
+    prenorm_ref,
+    convtaps_ref,
+    postnorm_ref,
     hidden_ref,
     cot_ref,
-    heads_ref,
-    skip_ref,
+    headcoefs_ref,
     pre_scale_ref,
-    gate_grad_ref,
-    post_grad_ref,
-    post_ref,
+    gate_grad_out_ref,
+    post_out_ref,
     normed_turned_ref,
     post_turned_ref,
     dproj_ref,
-    conv_grad_ref,
-    head_grad_ref,
+    packed_ref,
     scan_all_ref,
     gate_all_ref,
     out_all_ref,
@@ -182,12 +182,19 @@
     dstep_ref,
     dpre_ref,
     arrive_ref,
+    post_grad_ref,
+    gate_grad_ref,
+    post_ref,
+    small_ref,
+    heads_ref,
+    skip_ref,
     send_sem,
     recv_sem,
     halo_sem,
     back_send,
     back_recv,
     edge_sem,
+    leave_sem,
     small_send,
     small_recv,
     turn_send,
@@ -223,6 +230,20 @@
     for chunk in range(in_chunks):
         in_wide(chunk).start()
     out_wide.start()
+    conv_own = convtaps_ref.shape[1]
+    small_rows = [
+        jnp.concatenate([part, jnp.zeros((part.shape[0], width), f32)], axis=1)
+        if width
+        else part
+        for part, width in (
+            (ref[...], small_ref.shape[1] - ref.shape[1])
+            for ref in (prenorm_ref, convtaps_ref, postnorm_ref)
+        )
+    ]
+    small_rows.append(jnp.zeros((9, small_ref.shape[1]), f32))
+    small_ref[...] = jnp.concatenate(small_rows, axis=0).astype(bf16)
+    heads_ref[...] = jnp.zeros_like(heads_ref)
+    heads_ref[0:3, 0 : headcoefs_ref.shape[1]] = headcoefs_ref[...]
     barrier = pltpu.get_barrier_semaphore()
     greet_seq(barrier, rank, last)
     greet_plane(barrier, me, group)
@@ -262,7 +283,7 @@
     scan_ring = weight_ring(scan_shard_ref, scan_all_ref, HEIGHT, ring_sems[0:5], prepare_scan)
     gate_ring = weight_ring(gate_shard_ref, gate_all_ref, HEIGHT, ring_sems[5:10], prepare_gate)
     out_ring = weight_ring(out_low_ref, out_all_ref, out_height, ring_sems[10:15], prepare_out)
-    spacing = 2
+    spacing = 3
     rings = (
         (scan_ring, 0, in_chunks),
         (gate_ring, in_chunks, in_chunks),
@@ -298,7 +319,6 @@
     for i in range(1, group):
         small_copy(i, lax.rem(me + i, group), me).wait_send()
         small_copy(i, me, lax.rem(me + group - i, group)).wait_recv()
-    conv_own = conv_width // group
     taps_ref[...] = jnp.zeros_like(taps_ref)
     for device in range(group):
         small = small_all_ref[device].astype(f32)
@@ -306,6 +326,17 @@
         taps_ref[0:5, device * conv_own : (device + 1) * conv_own] = small[1:6, 0:conv_own]
         post_scale_ref[0:1, device * own_out : (device + 1) * own_out] = small[6:7, 0:own_out]
     pre_scale_ref[1:8, :] = jnp.zeros((7, model_width), f32)
+
+    skip_parts = jnp.concatenate(
+        thirds(jnp.broadcast_to(heads_ref[2:3, :], (8, LANES))), axis=1
+    )
+
+    def spread_skip(tile, carry):
+        cols = pl.ds(pl.multiple_of(tile * LANES, LANES), LANES)
+        skip_ref[0:1, cols] = mm(skip_parts, head_lanes(tile, per_tile, 3), 1, 0)[0:1, :]
+        return carry
+
+    lax.fori_loop(0, tiles, spread_skip, 0)
 
     def norm(at, carry):
         some = pl.ds(pl.multiple_of(at * HEIGHT, HEIGHT), HEIGHT)
@@ -578,7 +609,7 @@
 
     def backward():
         core = lax.rem(me, 2)
-        cot_chunks = cot_ref.shape[1] // WIDE
+        cot_chunks = EARLY
 
         def cot_block(chunk, origin, part):
             ref = cot_all_ref.at[chunk, core, origin]
@@ -688,7 +719,7 @@
             dvalues = step_l * dx + skip_ref[0:1, cols] * dy
             dpre = dvalues * sig * (1.0 + pre * (1.0 - sig))
             dpre_ref[0:rows, cols] = dpre
-            conv_grad_ref[:, cols] = tap_grads(dpre, jnp.sum(dy * values, axis=0, keepdims=True))
+            packed_ref[:, cols] = tap_grads(dpre, jnp.sum(dy * values, axis=0, keepdims=True))
 
             ring.round(tile - COT_AT, cot_chunks, COT_SPACING)
 
@@ -708,7 +739,7 @@
             pre, sig = conv_tile(conv_ref, halo_ref, u_ref, taps_ref, start, rows)
             dpre = dshared[i] * sig * (1.0 + pre * (1.0 - sig))
             dpre_ref[0:rows, start : start + N] = dpre
-            conv_grad_ref[:, start : start + N] = tap_grads(dpre, jnp.zeros((1, LANES), f32))
+            packed_ref[:, start : start + N] = tap_grads(dpre, jnp.zeros((1, LANES), f32))
 
         edge = seq_copy(
             dpre_ref.at[pl.ds(0, 8), :],
@@ -728,7 +759,7 @@
         drate = (dstep_ref[...] - ddecay * exp_rate) * jax.nn.sigmoid(
             u_ref[:, conv_width:].astype(f32) + heads_ref[0:1, :]
         )
-        head_grad_ref[...] = jnp.concatenate(
+        packed_ref[:, conv_width:] = jnp.concatenate(
             [
                 jnp.sum(drate, axis=0, keepdims=True),
                 jnp.sum(ddecay * (-step * exp_rate), axis=0, keepdims=True),
@@ -736,6 +767,7 @@
             ],
             axis=0,
         )
+        packed_ref[6:7, 0:inner] = post_grad_ref[...]
         dproj_ref[:, conv_width : conv_width + LANES] = drate.astype(bf16)
         dproj_ref[:, conv_width + LANES :] = jnp.zeros(
             (rows, dproj_ref.shape[1] - conv_width - LANES), bf16
@@ -779,7 +811,15 @@
         lax.fori_loop(0, cot_chunks, finish_ring, 0)
 
     cot_ring_sems = ring_sems[15:]
+    leaving = [
+        pltpu.make_async_copy(post_ref, post_out_ref, leave_sem.at[0]),
+        pltpu.make_async_copy(gate_grad_ref, gate_grad_out_ref, leave_sem.at[1]),
+    ]
+    for copy in leaving:
+        copy.start()
     backward()
+    for copy in leaving:
+        copy.wait()
     post_turn.finish()
     normed_turn.finish()
 
@@ -788,7 +828,7 @@
     return [pl.BlockSpec(memory_space=pltpu.VMEM)] * count
 
 
-def front(in_shard, out_shard, small, hidden, cot, heads, skip, sizes):
+def front(in_shard, out_shard, prenorm, convtaps, postnorm, hidden, cot, headcoefs, sizes):
     rows, inner, tiles, _ = sizes
     conv_width = inner + 2 * N
     shape = jax.ShapeDtypeStruct
@@ -798,6 +838,7 @@
     scan_width = -(-(proj_width - inner) // LANES) * LANES
     in_chunks = own_in // HEIGHT
     out_chunks = own_out // (2 * HEIGHT)
+    small_lanes = -(-max(own_in, own_out, convtaps.shape[1]) // LANES) * LANES
     anywhere = pl.BlockSpec(memory_space=pl.ANY)
     dma = pltpu.SemaphoreType.DMA
     return pl.pallas_call(
@@ -805,20 +846,18 @@
         out_shape=(
             shape((8, model_width), f32),
             shape((rows, inner), bf16),
-            shape((1, inner), f32),
             shape((rows, inner), bf16),
             shape((own_in, group * rows), bf16),
             shape((own_out, group * rows), bf16),
             shape((rows, -(-scan_width // WIDE) * WIDE), bf16),
-            shape((8, conv_width), f32),
-            shape((8, LANES), f32),
+            shape((8, conv_width + LANES), f32),
             shape((group // 2, 2, own_in, scan_width), bf16),
             shape((group // 2, 2, own_in, inner), bf16),
             shape((group // 2, 2, own_out, model_width), bf16),
-            shape((model_width // WIDE, 2, group // 2, rows, WIDE), bf16),
+            shape((EARLY, 2, group // 2, rows, WIDE), bf16),
         ),
-        in_specs=[anywhere] * 2 + vmem(5),
-        out_specs=tuple(vmem(9) + [anywhere] * 4),
+        in_specs=[anywhere] * 2 + vmem(6),
+        out_specs=tuple(vmem(1) + [anywhere] * 4 + vmem(2) + [anywhere] * 4),
         scratch_shapes=[
             pltpu.VMEM((rows, scan_width), bf16),
             pltpu.VMEM((rows, inner), f32),
@@ -835,7 +874,7 @@
             pltpu.VMEM((own_in, scan_width), bf16),
             pltpu.VMEM((own_in, inner), bf16),
             pltpu.VMEM((own_out, model_width), bf16),
-            pltpu.VMEM((group,) + small.shape, bf16),
+            pltpu.VMEM((group, 16, small_lanes), bf16),
             pltpu.VMEM((1, inner), f32),
             pltpu.VMEM((rows, model_width), bf16),
             pltpu.VMEM((2, group // 2, 2, own_in, WIDE), bf16),
@@ -855,11 +894,18 @@
             pltpu.VMEM((rows, LANES), f32),
             pltpu.VMEM((rows + 8, conv_width), f32),
             pltpu.VMEM((tiles, N, LANES), f32),
+            pltpu.VMEM((1, inner), f32),
+            pltpu.VMEM((rows, inner), bf16),
+            pltpu.VMEM((rows, inner), bf16),
+            pltpu.VMEM((16, small_lanes), bf16),
+            pltpu.VMEM((8, LANES), f32),
+            pltpu.VMEM((1, inner), f32),
             dma((tiles,)),
             dma((tiles,)),
             dma((2,)),
             dma((tiles,)),
             dma((tiles,)),
+            dma((2,)),
             dma((2,)),
             dma((group,)),
             dma((group,)),
@@ -872,14 +918,14 @@
         + PlaneRing.semaphores(in_chunks)
         + PlaneRing.semaphores(in_chunks)
         + PlaneRing.semaphores(out_chunks)
-        + PlaneRing.semaphores(model_width // WIDE),
+        + PlaneRing.semaphores(EARLY),
         compiler_params=pltpu.CompilerParams(
             collective_id=1, has_side_effects=True, vmem_limit_bytes=60 * 2**20
         ),
         cost_estimate=pl.CostEstimate(
             flops=10**10, bytes_accessed=10**8, transcendentals=4 * 10**6
         ),
-    )(in_shard, out_shard, small, hidden, cot, heads, skip)
+    )(in_shard, out_shard, prenorm, convtaps, postnorm, hidden, cot, headcoefs)
 
 
 def plane_copy(src, dst, send, recv, to):
@@ -1060,12 +1106,12 @@
     normed_turned_ref,
     post_turned_ref,
     cot_ref,
-    gate_ref,
-    scan_ref,
-    small_ref,
-    hidden_ref,
-    own_cot_ref,
-    post_ref,
+    gate_far_ref,
+    scan_far_ref,
+    packed_in_ref,
+    hidden_far_ref,
+    own_cot_far_ref,
+    post_far_ref,
     scale_ref,
     gate_matrix_ref,
     scan_matrix_ref,
@@ -1073,8 +1119,8 @@
     in_ref,
     out_ref,
     small_out_ref,
-    output_ref,
-    input_grad_ref,
+    output_far_ref,
+    input_grad_far_ref,
     gathered_ref,
     value_ref,
     inbox_ref,
@@ -1085,7 +1131,15 @@
     small_all_ref,
     weights_ref,
     normed_grad_ref,
-    scale_grad_ref,
+    packed_ref,
+    gate_ref,
+    scan_ref,
+    hidden_ref,
+    own_cot_ref,
+    post_ref,
+    output_ref,
+    input_grad_ref,
+    far_sem,
     up_send,
     inbox_recv,
     other_recv,
@@ -1101,12 +1155,12 @@
     load_sem,
     small_send,
     small_recv,
-    scale_send,
-    scale_recv,
     weight_sem,
 ):
     rows, own_in, out_steps, gate_steps, steps, root, lag, spacing = sizes
-    chunks = steps - out_steps
+    rest = out_steps // 2 - EARLY
+    back_items = steps - out_steps
+    chunks = back_items + rest
     rank = lax.axis_index("seq")
     last = lax.axis_size("seq") - 1
     me = lax.axis_index("dp")
@@ -1114,6 +1168,22 @@
     chips = group // 2
     reach = chips // 2
     core = lax.rem(me, 2)
+    arriving = [
+        pltpu.make_async_copy(far, near, far_sem.at[at])
+        for at, (far, near) in enumerate(
+            (
+                (gate_far_ref, gate_ref),
+                (scan_far_ref, scan_ref),
+                (hidden_far_ref, hidden_ref),
+                (own_cot_far_ref, own_cot_ref),
+                (post_far_ref, post_ref),
+            )
+        )
+    ]
+    leaving = (
+        pltpu.make_async_copy(input_grad_ref, input_grad_far_ref, far_sem.at[5]),
+        pltpu.make_async_copy(output_ref, output_far_ref, far_sem.at[6]),
+    )
     barrier = pltpu.get_barrier_semaphore()
     greet_seq(barrier, rank, last)
     greet_plane(barrier, me, group)
@@ -1121,30 +1191,12 @@
     left = jnp.maximum(rank - 1, 0)
     right = jnp.minimum(rank + 1, last)
 
-    packed = small_ref.shape[2]
     model_width = hidden_ref.shape[1]
 
     def small_copy(i, peer, slot):
         return plane_copy(
-            small_ref.at[peer],
-            small_all_ref.at[slot, :, pl.ds(0, packed)],
-            small_send.at[i],
-            small_recv.at[i],
-            peer,
-        )
-
-    def scale_copy(i, peer, slot):
-        return plane_copy(
-            scale_grad_ref,
-            small_all_ref.at[slot, :, pl.ds(packed, model_width)],
-            scale_send.at[i],
-            scale_recv.at[i],
-            peer,
-        )
-
-    for i in range(1, group):
-        small_copy(i, lax.rem(me + i, group), me).start()
-    small_all_ref[me, :, 0:packed] = small_ref[me]
+            packed_ref, small_all_ref.at[slot], small_send.at[i], small_recv.at[i], peer
+        )
 
     def block(chunk, origin, part):
         ref = gathered_ref.at[chunk, core, origin]
@@ -1153,15 +1205,21 @@
     def source(chunk, part, action):
         part_rows = pl.ds(0, rows) if part is None else pl.ds(part * (rows // 2), rows // 2)
 
-        @pl.when(chunk < gate_steps)
-        def _():
-            start = pl.multiple_of(chunk * WIDE, WIDE)
-            action(gate_ref.at[part_rows, pl.ds(start, WIDE)])
-
-        @pl.when(chunk >= gate_steps)
-        def _():
-            start = pl.multiple_of((chunk - gate_steps) * WIDE, WIDE)
-            action(scan_ref.at[part_rows, pl.ds(start, WIDE)])
+        def one(ref, first):
+            start = pl.multiple_of((chunk - first) * WIDE, WIDE)
+            action(ref.at[part_rows, pl.ds(start, WIDE)])
+
+        @pl.when(chunk < rest)
+        def _():
+            one(own_cot_far_ref, -EARLY)
+
+        @pl.when((chunk >= rest) & (chunk < rest + gate_steps))
+        def _():
+            one(gate_far_ref, rest)
+
+        @pl.when(chunk >= rest + gate_steps)
+        def _():
+            one(scan_far_ref, rest + gate_steps)
 
     ring = PlaneRing(
         block,
@@ -1170,23 +1228,24 @@
         (ring_send, ring_recv, pair_send, pair_recv, own_sem),
     )
 
+    def order_of(step):
+        return jnp.where(step < out_steps, step // 2, step - out_steps + out_steps // 2)
+
     def fetch(step, action):
-        order = jnp.where(step < out_steps, step // 2, step - out_steps + out_steps // 2)
+        order = order_of(step)
         slot = lax.rem(order, 2)
 
-        @pl.when((step < out_steps) & (lax.rem(step, 2) == 0))
+        @pl.when((order < EARLY) & (lax.rem(step, 2) == 0))
+        def _():
+            action(
+                pltpu.make_async_copy(cot_ref.at[order], loaded_ref.at[slot], load_sem.at[slot])
+            )
+
+        @pl.when((order >= EARLY) & ((step >= out_steps) | (lax.rem(step, 2) == 0)))
         def _():
             action(
                 pltpu.make_async_copy(
-                    cot_ref.at[step // 2], loaded_ref.at[slot], load_sem.at[slot]
-                )
-            )
-
-        @pl.when(step >= out_steps)
-        def _():
-            action(
-                pltpu.make_async_copy(
-                    gathered_ref.at[step - out_steps], loaded_ref.at[slot], load_sem.at[slot]
+                    gathered_ref.at[order - EARLY], loaded_ref.at[slot], load_sem.at[slot]
                 )
             )
 
@@ -1209,6 +1268,8 @@
             )
 
     fetch(0, lambda copy: copy.start())
+    for copy in arriving:
+        copy.start()
 
     def weight_copy(item, action):
         slot = lax.rem(item, 2)
@@ -1225,7 +1286,7 @@
                 )
             )
 
-        full = chunks - 1 if narrow else chunks
+        full = back_items - 1 if narrow else back_items
 
         @pl.when(item < gate_steps)
         def _():
@@ -1241,11 +1302,11 @@
             def _():
                 one(scan_matrix_ref, gate_steps, narrow)
 
-        @pl.when((item >= chunks) & (item < items))
-        def _():
-            one(out_matrix_ref, chunks, WIDE)
-
-    items = chunks + model_width // WIDE
+        @pl.when((item >= back_items) & (item < items))
+        def _():
+            one(out_matrix_ref, back_items, WIDE)
+
+    items = back_items + model_width // WIDE
 
     def back_product(grad_ref, item, first, width):
         cols = pl.ds(pl.multiple_of((item - first) * WIDE, WIDE), width)
@@ -1266,19 +1327,21 @@
             return carry + jnp.sum(grad * plain, axis=0, keepdims=True)
 
         total = lax.fori_loop(0, rows // HEIGHT, block, jnp.zeros((1, model_width), f32))
-        first = iota((8, model_width), 0) == 0
-        scale_grad_ref[...] = jnp.where(first, total, 0.0)
+        packed_ref[...] = packed_in_ref[...]
+        packed_ref[7:8, 0:model_width] = total
         for i in range(1, group):
-            scale_copy(i, lax.rem(me + i, group), me).start()
-        small_all_ref[me, :, packed:] = scale_grad_ref[...]
+            small_copy(i, lax.rem(me + i, group), me).start()
+        small_all_ref[me] = packed_ref[...]
 
     def local_product(item):
         narrow = scan_matrix_ref.shape[1] % WIDE
-        full = chunks - 1 if narrow else chunks
+        full = back_items - 1 if narrow else back_items
 
         @pl.when(item == 0)
         def _():
             normed_grad_ref[...] = jnp.zeros_like(normed_grad_ref)
+            for copy in arriving:
+                copy.wait()
 
         weight_copy(item, lambda copy: copy.wait())
         weight_copy(item + 1, lambda copy: copy.start())
@@ -1297,16 +1360,21 @@
             def _():
                 back_product(scan_ref, item, gate_steps, narrow)
 
-        @pl.when(item == chunks - 1)
+        @pl.when(item == back_items - 1)
         def _():
             norm_backward()
-
-        @pl.when(item >= chunks)
-        def _():
-            cols = pl.ds(pl.multiple_of((item - chunks) * WIDE, WIDE), WIDE)
+            leaving[0].start()
+
+        @pl.when(item >= back_items)
+        def _():
+            cols = pl.ds(pl.multiple_of((item - back_items) * WIDE, WIDE), WIDE)
             output_ref[:, cols] = hidden_ref[:, cols].astype(f32) + mm(
                 post_ref[...], weights_ref[lax.rem(item, 2)], 1, 0
             )
+
+        @pl.when(item == items - 1)
+        def _():
+            leaving[1].start()
 
     weight_copy(0, lambda copy: copy.start())
 
@@ -1445,9 +1513,12 @@
             def _(chunk=chunk, stage=stage):
                 ring.stage(chunk, stage)
 
-        @pl.when((step + 1 >= out_steps) & (step + 1 < steps))
-        def _():
-            ring.wait_pair(step + 1 - out_steps)
+        follow = step + 1
+        arrives = (follow >= out_steps) | ((order_of(follow) >= EARLY) & (lax.rem(follow, 2) == 0))
+
+        @pl.when(arrives & (follow < steps))
+        def _():
+            ring.wait_pair(order_of(follow) - EARLY)
 
         @pl.when(step + 1 < steps)
         def _():
@@ -1481,8 +1552,6 @@
                 small_copy(i, lax.rem(me + i, group), me).wait_send()
                 origin = lax.rem(me + group - i, group)
                 small_copy(i, origin, origin).wait_recv()
-                scale_copy(i, origin, me).wait_send()
-                scale_copy(i, origin, origin).wait_recv()
             small_value_ref[...] = jnp.sum(small_all_ref[...], axis=0)
             up(small_value_ref, small_inbox_ref, small_out_ref, steps, 1, lambda part: None)
 
@@ -1491,9 +1560,9 @@
             for part in range(PARTS):
                 down_late(part)
 
-        @pl.when(step < items)
-        def _():
-            local_product(step)
+        @pl.when((step >= 1) & (step < 1 + items))
+        def _():
+            local_product(step - 1)
 
         return carry
 
@@ -1512,10 +1581,12 @@
         return carry
 
     lax.fori_loop(0, chunks, finish_ring, 0)
+    for copy in leaving:
+        copy.wait()
 
 
 def reduce_gradients(
-    normed_turned, post_turned, cot_all, gate_grad, scan_grad, small, hidden, cot, post, scale, matrices
+    normed_turned, post_turned, cot_early, gate_grad, scan_grad, packed, hidden, cot, post, scale, matrices
 ):
     size = lax.axis_size("seq")
     group = lax.axis_size("dp")
@@ -1524,28 +1595,30 @@
     model_width = hidden.shape[1]
     out_steps = 2 * (model_width // WIDE)
     gate_steps = gate_grad.shape[1] // WIDE
-    chunks = gate_steps + scan_grad.shape[1] // WIDE
-    steps = out_steps + chunks
+    back_items = gate_steps + scan_grad.shape[1] // WIDE
+    steps = out_steps + back_items
+    chunks = back_items + out_steps // 2 - EARLY
     reach = group // 4
     spacing = min(3, (out_steps - 2) // reach)
+    assert out_steps == 2 * EARLY
     sizes = (rows, own_in, out_steps, gate_steps, steps, size // 2, LAG, spacing)
-    assert chunks + model_width // WIDE <= steps
+    assert back_items + model_width // WIDE < steps
     shape = jax.ShapeDtypeStruct
     dma = pltpu.SemaphoreType.DMA
-    small_shape = (8, small.shape[2] + model_width)
+    small_shape = packed.shape
     anywhere = pl.BlockSpec(memory_space=pl.ANY)
     return pl.pallas_call(
         functools.partial(tail_kernel, sizes),
         out_shape=(
-            shape((own_in, chunks * WIDE), f32),
+            shape((own_in, back_items * WIDE), f32),
             shape((2 * own_in, model_width), f32),
             shape(small_shape, f32),
             shape((rows, model_width), f32),
             shape((rows, model_width), f32),
             shape((chunks, 2, group // 2, rows, WIDE), bf16),
         ),
-        in_specs=vmem(2) + [anywhere] + vmem(7) + [anywhere] * 3,
-        out_specs=(anywhere, anywhere) + tuple(vmem(3)) + (anywhere,),
+        in_specs=vmem(2) + [anywhere] * 3 + vmem(1) + [anywhere] * 3 + vmem(1) + [anywhere] * 3,
+        out_specs=(anywhere, anywhere) + tuple(vmem(1)) + (anywhere,) * 3,
         scratch_shapes=[
             pltpu.VMEM((own_in, WIDE), f32),
             pltpu.VMEM((steps, own_in, WIDE), f32),
@@ -1556,14 +1629,22 @@
             pltpu.VMEM((group,) + small_shape, f32),
             pltpu.VMEM((2, matrices[2].shape[0], WIDE), bf16),
             pltpu.VMEM((rows, model_width), f32),
-            pltpu.VMEM((8, model_width), f32),
+            pltpu.VMEM(small_shape, f32),
+            pltpu.VMEM(gate_grad.shape, bf16),
+            pltpu.VMEM(scan_grad.shape, bf16),
+            pltpu.VMEM(hidden.shape, bf16),
+            pltpu.VMEM(cot.shape, bf16),
+            pltpu.VMEM(post.shape, bf16),
+            pltpu.VMEM((rows, model_width), f32),
+            pltpu.VMEM((rows, model_width), f32),
+            dma((7,)),
         ]
         + [dma((steps + 1, PARTS))] * 6
         + [
             dma((steps,)),
             *PlaneRing.semaphores(chunks),
             dma((2,)),
-            *[dma((group,))] * 4,
+            *[dma((group,))] * 2,
             dma((2,)),
         ],
         compiler_params=pltpu.CompilerParams(
@@ -1575,16 +1656,45 @@
     )(
         normed_turned,
         post_turned,
-        cot_all,
+        cot_early,
         gate_grad,
         scan_grad,
-        small,
+        packed,
         hidden,
         cot,
         post,
         scale,
         *matrices,
     )
+
+
+def adam_kernel(*refs):
+    ins, outs = refs[:8], refs[8:]
+    for matrix in range(2):
+        gradient, weight, moment, square = (ref[...] for ref in ins[4 * matrix : 4 * matrix + 4])
+        gradient = gradient[:, : weight.shape[1]]
+        updated = adam_update(weight, moment, square, gradient, rate_matrix, weight_decay)
+        for ref, value in zip(outs[4 * matrix : 4 * matrix + 4], (gradient,) + updated):
+            ref[...] = value
+
+
+def adam_matrices(matrices):
+    blocks = 12
+    flat = [array for four in matrices for array in four]
+    out = [four[1] for four in matrices for _ in range(4)]
+
+    def spec(array):
+        return pl.BlockSpec((array.shape[0] // blocks, array.shape[1]), lambda at: (at, 0))
+
+    results = pl.pallas_call(
+        adam_kernel,
+        grid=(blocks,),
+        out_shape=[jax.ShapeDtypeStruct(array.shape, f32) for array in out],
+        in_specs=[spec(array) for array in flat],
+        out_specs=[spec(array) for array in out],
+        compiler_params=pltpu.CompilerParams(vmem_limit_bytes=58 * 2**20),
+    )(*flat)
+    return results[:4], results[4:]
 
 
 def on_device(
@@ -1625,82 +1735,68 @@
     conv_width = conv_own * group
 
     tap_rows = convtaps.shape[0]
-    small_lanes = -(-max(own_in, own_out, conv_own) // LANES) * LANES
-    small = jnp.concatenate(
-        [
-            jnp.pad(part, ((0, 0), (0, small_lanes - part.shape[1])))
-            for part in (prenorm.reshape(1, -1), convtaps, postnorm.reshape(1, -1))
-        ]
-    )
-    small = jnp.pad(small, ((0, 16 - small.shape[0]), (0, 0))).astype(bf16)
     hidden_low = hidden_in.reshape(rows, model_width)
     cot_low = out_grad.reshape(rows, model_width)
-    head_rows = jnp.pad(headcoefs, ((0, 8 - headcoefs.shape[0]), (0, LANES - heads)))
-    skip = jnp.repeat(headcoefs[2:3], width, axis=1)
     (
         pre_scale,
         gate_grad,
-        postnorm_grad,
         post_low,
         normed_turned,
         post_turned,
         scan_grad,
-        conv_grad,
-        head_grad,
+        packed,
         scan_matrix,
         gate_matrix,
         out_matrix,
-        cot_all,
-    ) = front(inproject, outproject, small, hidden_low, cot_low, head_rows, skip, sizes)
+        cot_early,
+    ) = front(
+        inproject,
+        outproject,
+        prenorm.reshape(1, -1),
+        convtaps,
+        postnorm.reshape(1, -1),
+        hidden_low,
+        cot_low,
+        headcoefs,
+        sizes,
+    )
     scan_matrix = scan_matrix.reshape(model_width, -1)
     gate_matrix = gate_matrix.reshape(model_width, inner)
     out_matrix = out_matrix.reshape(inner, model_width)
-    head_sums = jnp.concatenate(
-        [
-            head_grad[:2, :heads],
-            jnp.sum(conv_grad[tap_rows : tap_rows + 1, :inner].reshape(1, heads, width), axis=-1),
-        ],
-        axis=0,
-    )
-    conv_sums = conv_grad[:tap_rows].reshape(tap_rows, group, conv_own)
-    packed = jnp.concatenate(
-        [
-            postnorm_grad.reshape(group, own_out),
-            jnp.swapaxes(conv_sums, 0, 1).reshape(group, -1),
-            jnp.broadcast_to(head_sums.reshape(1, -1), (group, 3 * heads)),
-        ],
-        axis=1,
-    )
-    packed_size = packed.shape[1]
-    packed_lanes = -(-packed_size // (8 * LANES)) * LANES
-    packed = jnp.pad(packed, ((0, 0), (0, 8 * packed_lanes - packed_size)))
     inproj_padded, outproj_owned, packed, output, input_gradient, _ = reduce_gradients(
         normed_turned,
         post_turned,
-        cot_all,
+        cot_early,
         gate_grad,
         scan_grad,
-        packed.reshape(group, 8, packed_lanes),
+        packed,
         hidden_low,
         cot_low,
         post_low,
         pre_scale,
         (gate_matrix, scan_matrix, out_matrix),
     )
-    inproj_owned = inproj_padded[:, :proj_width]
-    prenorm_owned = lax.dynamic_slice_in_dim(packed[0, packed_lanes:], me * own_in, own_in, 0)
-    packed = packed[:, :packed_lanes].reshape(-1)
-    postnorm_owned = packed[:own_out]
-    conv_at = own_out
-    conv_end = conv_at + tap_rows * conv_own
-    conv_owned = packed[conv_at:conv_end].reshape(tap_rows, conv_own)
-    head_total = packed[conv_end:packed_size].reshape(3, heads)
+    prenorm_owned = lax.dynamic_slice_in_dim(packed[7], me * own_in, own_in, 0)
+    postnorm_owned = lax.dynamic_slice_in_dim(packed[6], me * own_out, own_out, 0)
+    conv_owned = lax.dynamic_slice_in_dim(packed[:tap_rows], me * conv_own, conv_own, 1)
+    head_total = jnp.concatenate(
+        [
+            packed[:2, conv_width : conv_width + heads],
+            jnp.sum(packed[5:6, :inner].reshape(1, heads, width), axis=-1),
+        ]
+    )
 
     prenorm_new, prenorm_mom, prenorm_sq = adam_update(
         prenorm, prenorm_first, prenorm_second, prenorm_owned, rate_vector, 0.0
     )
-    inproj_new, inproj_mom, inproj_sq = adam_update(
-        inproject, inproject_first, inproject_second, inproj_owned, rate_matrix, weight_decay
+    (
+        (inproj_owned, inproj_new, inproj_mom, inproj_sq),
+        (outproj_owned, outproj_new, outproj_mom, outproj_sq),
+    ) = adam_matrices(
+        (
+            (inproj_padded, inproject, inproject_first, inproject_second),
+            (outproj_owned, outproject, outproject_first, outproject_second),
+        )
     )
     conv_new, conv_mom, conv_sq = adam_update(
         convtaps, convtaps_first, convtaps_second, conv_owned, rate_vector, 0.0
@@ -1710,9 +1806,6 @@
     )
     postnorm_new, postnorm_mom, postnorm_sq = adam_update(
         postnorm, postnorm_first, postnorm_second, postnorm_owned, rate_vector, 0.0
-    )
-    outproj_new, outproj_mom, outproj_sq = adam_update(
-        outproject, outproject_first, outproject_second, outproj_owned, rate_matrix, weight_decay
     )
     return (
         output.reshape(seq_here, rows, model_width),

time: 454 us -> 442 us (0.974)
  other arithmetic: 25.8 us -> 3.47 us
  Pallas kernels: 410 us -> 430 us
  local copies, waits for them, and re-layouts: 16.4 us -> 6.4 us
    pallas_call x0 -> x1, Pallas kernels: none -> 24.5 us  [adam_matrices(): pl.pallas_call(adam_kernel, grid=(blocks,), out_shape=[jax.ShapeDtypeStru...]
    sub x6 -> x4, other arithmetic: 22.2 us -> 3.36 us  [adam_update(): weight - step_rate * (moment_hat / (jnp.sqrt(square_hat) + adam_eps) + de...]
    pallas_call x1, Pallas kernels: 216 us -> 211 us  [front(): pl.pallas_call(functools.partial(front_kernel, sizes), out_shape=(shape((...]
    unnamed x46 -> x34, local copies, waits for them, and re-layouts: 6.98 us -> 2.37 us
where the time goes in v6:
time: 442 us; the launch traced here: 441 us
  Pallas kernels  430 us (97%)
  local copies, waits for them, and re-layouts  6.4 us (1%)
    pallas_call x1, Pallas kernels, front(): pl.pallas_call(functools.partial(front_kernel, sizes), out_shape=(shape((...  211 us
    pallas_call x1, Pallas kernels, reduce_gradients(): pl.pallas_call(functools.partial(tail_kernel, sizes), out_shape=(shape((o...  195 us
    pallas_call x1, Pallas kernels, adam_matrices(): pl.pallas_call(adam_kernel, grid=(blocks,), out_shape=[jax.ShapeDtypeStru...  24.5 us

profile of v6, /device:TPU:0, one launch (start us, length us, event | category | flops | bytes accessed | tf_op | source)
XLA Modules:
  0.0 440.9 jit_solution(9349072902123566173)
XLA Ops:
  0.7 1.2 reshape.86.postnorm_ref
  1.9 210.9 %shard_map.395 = (f32[8,1536]{1,0:T(8,128)}, bf16[256,3072]{1,0:T(8,128)(2,1)}, bf16[256,3072]{1,0:T(8,128)(2,1)}, bf16[192,2048]{1,0:T(8,128)(2,1)}, bf16[384,2...) custom-call(f32[192,6448]{1,0:T(8,128)} %refs_1_.1, ...), custom_call_target="tpu_custom_call" | custom-call | flops 10000000000 | bytes 100000000 | tf_op jit(solution)/shard_map/pallas_call | solution.py:844
  212.9 0.0 copy-start.10
  212.9 0.0 copy-start.11
  212.9 0.0 copy-start.12
  212.9 194.7 %shard_map.396 = (f32[192,6656]{1,0:T(8,128)}, f32[384,1536]{1,0:T(8,128)}, f32[8,3456]{1,0:T(8,128)}, f32[256,1536]{1,0:T(8,128)}, f32[256,1536]{1,0:T(8,128)}, /*index=5*/bf16[26,2,4,256,256]{4,3,2,1,0:T(8,128)(2,1)}) custom-call(bf16[192,2048]{1,0:T(8,128)(2,1)} %get-tuple-element.50.normed_turned_ref, ...), custom_call_target="tpu_custom_call" | custom-call | flops 20000000000 | bytes 200000000 | tf_op jit(solution)/shard_map/pallas_call | solution.py:1610
  407.6 0.9 slice_reduce_fusion
  408.6 0.1 reshape.94
  408.6 0.1 reduce_sum.11
  408.7 0.7 slice.17
  409.4 0.0 copy-done.10
  409.4 0.0 copy-done.11
  409.4 0.0 copy-done.12
  409.4 0.6 multiply_subtract_fusion.2
  410.1 0.0 copy-start.2
  410.1 0.0 copy-start.3
  410.1 0.0 copy-start.4
  410.1 0.0 copy-start.5
  410.1 0.0 copy-start.8
  410.1 0.0 copy-start.9
  410.1 0.0 copy-start.13
  410.1 0.0 copy-start.14
  410.1 0.0 copy-start.15
  410.1 0.0 copy-start.1
  410.1 24.5 %shard_map.397 = (f32[192,6448]{1,0:T(8,128)}, f32[192,6448]{1,0:T(8,128)}, f32[192,6448]{1,0:T(8,128)}, f32[192,6448]{1,0:T(8,128)}, f32[384,1536]{1,0:T(8,128)...) custom-call(f32[192,6656]{1,0:T(8,128)} %get-tuple-element.64.refs_0_, f32[192,6448]{1,0:T(8,128)} %refs_1_.1, ...), custom_call_target="tpu_custom_call" | custom-call | tf_op jit(solution)/shard_map/pallas_call | solution.py:1689
  434.7 0.0 copy-start
  434.7 0.0 copy-done.2
  434.7 0.0 copy-done.3
  434.7 0.0 copy-done.4
  434.7 1.5 multiply_subtract_fusion
  436.2 1.0 fusion.8
  437.3 0.0 copy-done.5
  437.3 0.0 copy-done.8
  437.3 0.0 copy-done.9
  437.3 0.0 copy-start.6
  437.3 0.6 multiply_subtract_fusion.1
  437.9 0.1 constant_dynamic-slice_fusion.1
  438.0 0.0 copy-start.7
  438.0 0.0 copy-done.13
  438.0 0.0 copy-done.14
  438.0 0.0 copy-done.15
  438.0 0.6 multiply_subtract_fusion.3
  438.6 0.0 copy-done.1
  438.6 1.1 copy.48
  439.7 0.0 copy-done
  439.7 1.1 copy.49
  440.9 0.0 copy-done.6
  440.9 0.0 copy-done.7
  (1 shorter events, 0.0 us)
Async XLA Ops:
  212.9 196.6 %copy-start.10 = (f32[3,48]{1,0:T(4,128)S(1)}, f32[3,48]{1,0:T(4,128)}, u32[]{:S(2)}) copy-start(f32[3,48]{1,0:T(4,128)} %headcoefs_ref.1) | copy-start | bytes 1732
  212.9 196.6 %copy-start.11 = (f32[3,48]{1,0:T(4,128)S(1)}, f32[3,48]{1,0:T(4,128)}, u32[]{:S(2)}) copy-start(f32[3,48]{1,0:T(4,128)} %param.31) | copy-start | bytes 1732
  212.9 196.6 %copy-start.12 = (f32[3,48]{1,0:T(4,128)S(1)}, f32[3,48]{1,0:T(4,128)}, u32[]{:S(2)}) copy-start(f32[3,48]{1,0:T(4,128)} %param.37) | copy-start | bytes 1732
  410.1 24.6 %copy-start.2 = (f32[5,416]{1,0:T(8,128)S(1)}, f32[5,416]{1,0:T(8,128)}, u32[]{:S(2)}) copy-start(f32[5,416]{1,0:T(8,128)} %convtaps_ref.1) | copy-start | bytes 24964
  410.1 24.6 %copy-start.3 = (f32[5,416]{1,0:T(8,128)S(1)}, f32[5,416]{1,0:T(8,128)}, u32[]{:S(2)}) copy-start(f32[5,416]{1,0:T(8,128)} %param.30) | copy-start | bytes 24964
  410.1 24.6 %copy-start.4 = (f32[5,416]{1,0:T(8,128)S(1)}, f32[5,416]{1,0:T(8,128)}, u32[]{:S(2)}) copy-start(f32[5,416]{1,0:T(8,128)} %param.36) | copy-start | bytes 24964
  410.1 27.2 %copy-start.5 = (f32[384]{0:T(512)S(1)}, f32[384]{0:T(512)}, u32[]{:S(2)}) copy-start(f32[384]{0:T(512)} %param.26) | copy-start | bytes 4612
  410.1 27.2 %copy-start.8 = (f32[384]{0:T(512)S(1)}, f32[384]{0:T(512)}, u32[]{:S(2)}) copy-start(f32[384]{0:T(512)} %param.32) | copy-start | bytes 4612
  410.1 27.2 %copy-start.9 = (f32[384]{0:T(512)S(1)}, f32[384]{0:T(512)}, u32[]{:S(2)}) copy-start(f32[384]{0:T(512)} %param.38) | copy-start | bytes 4612
  410.1 27.9 %copy-start.13 = (f32[192]{0:T(256)S(1)}, f32[192]{0:T(256)}, u32[]{:S(2)}) copy-start(f32[192]{0:T(256)} %param.22) | copy-start | bytes 2308
  410.1 27.9 %copy-start.14 = (f32[192]{0:T(256)S(1)}, f32[192]{0:T(256)}, u32[]{:S(2)}) copy-start(f32[192]{0:T(256)} %param.28) | copy-start | bytes 2308
  410.1 27.9 %copy-start.15 = (f32[192]{0:T(256)S(1)}, f32[192]{0:T(256)}, u32[]{:S(2)}) copy-start(f32[192]{0:T(256)} %param.34) | copy-start | bytes 2308
  410.1 28.5 %copy-start.1 = (f32[256,1536]{1,0:T(8,128)S(1)}, f32[256,1536]{1,0:T(8,128)}, u32[]{:S(2)}) copy-start(f32[256,1536]{1,0:T(8,128)} %get-tuple-element.61) | copy-start | bytes 4718596
  434.7 5.1 %copy-start = (f32[256,1536]{1,0:T(8,128)S(1)}, f32[256,1536]{1,0:T(8,128)}, u32[]{:S(2)}) copy-start(f32[256,1536]{1,0:T(8,128)} %get-tuple-element.62) | copy-start | bytes 4718596
  437.3 3.6 copy-start.6
  438.0 2.9 copy-start.7

commit v7 on v6

--- a/solution.py
+++ b/solution.py
@@ -1679,7 +1679,7 @@
 
 
 def adam_matrices(matrices):
-    blocks = 12
+    blocks = 4
     flat = [array for four in matrices for array in four]
     out = [four[1] for four in matrices for _ in range(4)]
 

time: 442 us -> 437 us (0.989)
  Pallas kernels: 430 us -> 425 us
    pallas_call x1, Pallas kernels: 24.5 us -> 19.7 us  [adam_matrices(): pl.pallas_call(adam_kernel, grid=(blocks,), out_shape=[jax.ShapeDtypeStru...]
where the time goes in v7:
time: 437 us; the launch traced here: 436 us
  Pallas kernels  425 us (97%)
  local copies, waits for them, and re-layouts  6.4 us (1%)
    pallas_call x1, Pallas kernels, front(): pl.pallas_call(functools.partial(front_kernel, sizes), out_shape=(shape((...  211 us
    pallas_call x1, Pallas kernels, reduce_gradients(): pl.pallas_call(functools.partial(tail_kernel, sizes), out_shape=(shape((o...  195 us
    pallas_call x1, Pallas kernels, adam_matrices(): pl.pallas_call(adam_kernel, grid=(blocks,), out_shape=[jax.ShapeDtypeStru...  19.7 us

profile of v7, /device:TPU:0, one launch (start us, length us, event | category | flops | bytes accessed | tf_op | source)
XLA Modules:
  0.0 436.1 jit_solution(1206916379458657064)
XLA Ops:
  0.7 1.2 reshape.86.postnorm_ref
  1.9 210.9 %shard_map.395 = (f32[8,1536]{1,0:T(8,128)}, bf16[256,3072]{1,0:T(8,128)(2,1)}, bf16[256,3072]{1,0:T(8,128)(2,1)}, bf16[192,2048]{1,0:T(8,128)(2,1)}, bf16[384,2...) custom-call(f32[192,6448]{1,0:T(8,128)} %refs_1_.1, ...), custom_call_target="tpu_custom_call" | custom-call | flops 10000000000 | bytes 100000000 | tf_op jit(solution)/shard_map/pallas_call | solution.py:844
  212.9 0.0 copy-start.10
  212.9 0.0 copy-start.11
  212.9 0.0 copy-start.12
  212.9 194.7 %shard_map.396 = (f32[192,6656]{1,0:T(8,128)}, f32[384,1536]{1,0:T(8,128)}, f32[8,3456]{1,0:T(8,128)}, f32[256,1536]{1,0:T(8,128)}, f32[256,1536]{1,0:T(8,128)}, /*index=5*/bf16[26,2,4,256,256]{4,3,2,1,0:T(8,128)(2,1)}) custom-call(bf16[192,2048]{1,0:T(8,128)(2,1)} %get-tuple-element.50.normed_turned_ref, ...), custom_call_target="tpu_custom_call" | custom-call | flops 20000000000 | bytes 200000000 | tf_op jit(solution)/shard_map/pallas_call | solution.py:1610
  407.6 0.9 slice_reduce_fusion
  408.6 0.1 reshape.94
  408.6 0.1 reduce_sum.11
  408.7 0.7 slice.17
  409.4 0.0 copy-done.10
  409.4 0.0 copy-done.11
  409.4 0.0 copy-done.12
  409.4 0.6 multiply_subtract_fusion.2
  410.1 0.0 copy-start.2
  410.1 0.0 copy-start.3
  410.1 0.0 copy-start.4
  410.1 0.0 copy-start.5
  410.1 0.0 copy-start.8
  410.1 0.0 copy-start.9
  410.1 0.0 copy-start.13
  410.1 0.0 copy-start.14
  410.1 0.0 copy-start.15
  410.1 0.0 copy-start.1
  410.1 19.7 %shard_map.397 = (f32[192,6448]{1,0:T(8,128)}, f32[192,6448]{1,0:T(8,128)}, f32[192,6448]{1,0:T(8,128)}, f32[192,6448]{1,0:T(8,128)}, f32[384,1536]{1,0:T(8,128)...) custom-call(f32[192,6656]{1,0:T(8,128)} %get-tuple-element.64.refs_0_, f32[192,6448]{1,0:T(8,128)} %refs_1_.1, ...), custom_call_target="tpu_custom_call" | custom-call | tf_op jit(solution)/shard_map/pallas_call | solution.py:1689
  429.9 0.0 copy-start
  429.9 0.0 copy-done.2
  429.9 0.0 copy-done.3
  429.9 0.0 copy-done.4
  429.9 1.5 multiply_subtract_fusion
  431.5 1.0 fusion.8
  432.5 0.0 copy-done.5
  432.5 0.0 copy-done.8
  432.5 0.0 copy-done.9
  432.5 0.0 copy-start.6
  432.6 0.6 multiply_subtract_fusion.1
  433.2 0.1 constant_dynamic-slice_fusion.1
  433.2 0.0 copy-start.7
  433.2 0.0 copy-done.13
  433.2 0.0 copy-done.14
  433.2 0.0 copy-done.15
  433.2 0.6 multiply_subtract_fusion.3
  433.8 0.0 copy-done.1
  433.8 1.1 copy.48
  435.0 0.0 copy-done
  435.0 1.1 copy.49
  436.1 0.0 copy-done.6
  436.1 0.0 copy-done.7
  (1 shorter events, 0.0 us)
Async XLA Ops:
  212.9 196.6 %copy-start.10 = (f32[3,48]{1,0:T(4,128)S(1)}, f32[3,48]{1,0:T(4,128)}, u32[]{:S(2)}) copy-start(f32[3,48]{1,0:T(4,128)} %headcoefs_ref.1) | copy-start | bytes 1732
  212.9 196.6 %copy-start.11 = (f32[3,48]{1,0:T(4,128)S(1)}, f32[3,48]{1,0:T(4,128)}, u32[]{:S(2)}) copy-start(f32[3,48]{1,0:T(4,128)} %param.31) | copy-start | bytes 1732
  212.9 196.6 %copy-start.12 = (f32[3,48]{1,0:T(4,128)S(1)}, f32[3,48]{1,0:T(4,128)}, u32[]{:S(2)}) copy-start(f32[3,48]{1,0:T(4,128)} %param.37) | copy-start | bytes 1732
  410.1 19.9 %copy-start.2 = (f32[5,416]{1,0:T(8,128)S(1)}, f32[5,416]{1,0:T(8,128)}, u32[]{:S(2)}) copy-start(f32[5,416]{1,0:T(8,128)} %convtaps_ref.1) | copy-start | bytes 24964
  410.1 19.9 %copy-start.3 = (f32[5,416]{1,0:T(8,128)S(1)}, f32[5,416]{1,0:T(8,128)}, u32[]{:S(2)}) copy-start(f32[5,416]{1,0:T(8,128)} %param.30) | copy-start | bytes 24964
  410.1 19.9 %copy-start.4 = (f32[5,416]{1,0:T(8,128)S(1)}, f32[5,416]{1,0:T(8,128)}, u32[]{:S(2)}) copy-start(f32[5,416]{1,0:T(8,128)} %param.36) | copy-start | bytes 24964
  410.1 22.5 %copy-start.5 = (f32[384]{0:T(512)S(1)}, f32[384]{0:T(512)}, u32[]{:S(2)}) copy-start(f32[384]{0:T(512)} %param.26) | copy-start | bytes 4612
  410.1 22.5 %copy-start.8 = (f32[384]{0:T(512)S(1)}, f32[384]{0:T(512)}, u32[]{:S(2)}) copy-start(f32[384]{0:T(512)} %param.32) | copy-start | bytes 4612
  410.1 22.5 %copy-start.9 = (f32[384]{0:T(512)S(1)}, f32[384]{0:T(512)}, u32[]{:S(2)}) copy-start(f32[384]{0:T(512)} %param.38) | copy-start | bytes 4612
  410.1 23.1 %copy-start.13 = (f32[192]{0:T(256)S(1)}, f32[192]{0:T(256)}, u32[]{:S(2)}) copy-start(f32[192]{0:T(256)} %param.22) | copy-start | bytes 2308
  410.1 23.1 %copy-start.14 = (f32[192]{0:T(256)S(1)}, f32[192]{0:T(256)}, u32[]{:S(2)}) copy-start(f32[192]{0:T(256)} %param.28) | copy-start | bytes 2308
  410.1 23.1 %copy-start.15 = (f32[192]{0:T(256)S(1)}, f32[192]{0:T(256)}, u32[]{:S(2)}) copy-start(f32[192]{0:T(256)} %param.34) | copy-start | bytes 2308
  410.1 23.7 %copy-start.1 = (f32[256,1536]{1,0:T(8,128)S(1)}, f32[256,1536]{1,0:T(8,128)}, u32[]{:S(2)}) copy-start(f32[256,1536]{1,0:T(8,128)} %get-tuple-element.61) | copy-start | bytes 4718596
  429.9 5.1 %copy-start = (f32[256,1536]{1,0:T(8,128)S(1)}, f32[256,1536]{1,0:T(8,128)}, u32[]{:S(2)}) copy-start(f32[256,1536]{1,0:T(8,128)} %get-tuple-element.62) | copy-start | bytes 4718596
  432.5 3.6 copy-start.6
  433.2 2.9 copy-start.7

commit v8 on v7

--- a/solution.py
+++ b/solution.py
@@ -14,7 +14,7 @@
 HEIGHT = 32
 PARTS = 2
 LAG = 4
-COT_AT = 8
+COT_AT = 10
 EARLY = 6
 COT_SPACING = 5
 
@@ -1601,7 +1601,7 @@
     reach = group // 4
     spacing = min(3, (out_steps - 2) // reach)
     assert out_steps == 2 * EARLY
-    sizes = (rows, own_in, out_steps, gate_steps, steps, size // 2, LAG, spacing)
+    sizes = (rows, own_in, out_steps, gate_steps, steps, size // 2 - 1, LAG, spacing)
     assert back_items + model_width // WIDE < steps
     shape = jax.ShapeDtypeStruct
     dma = pltpu.SemaphoreType.DMA

time: 437 us -> 427 us (0.977)
  Pallas kernels: 425 us -> 414 us
    pallas_call x1, Pallas kernels: 195 us -> 185 us  [reduce_gradients(): pl.pallas_call(functools.partial(tail_kernel, sizes), out_shape=(shape((o...]
where the time goes in v8:
time: 427 us; the launch traced here: 425 us
  Pallas kernels  414 us (97%)
  local copies, waits for them, and re-layouts  6.4 us (1%)
    pallas_call x1, Pallas kernels, front(): pl.pallas_call(functools.partial(front_kernel, sizes), out_shape=(shape((...  210 us
    pallas_call x1, Pallas kernels, reduce_gradients(): pl.pallas_call(functools.partial(tail_kernel, sizes), out_shape=(shape((o...  185 us
    pallas_call x1, Pallas kernels, adam_matrices(): pl.pallas_call(adam_kernel, grid=(blocks,), out_shape=[jax.ShapeDtypeStru...  19.7 us

profile of v8, /device:TPU:0, one launch (start us, length us, event | category | flops | bytes accessed | tf_op | source)
XLA Modules:
  0.0 425.1 jit_solution(7572626365743031443)
XLA Ops:
  0.7 1.2 reshape.86.postnorm_ref
  1.9 209.7 %shard_map.395 = (f32[8,1536]{1,0:T(8,128)}, bf16[256,3072]{1,0:T(8,128)(2,1)}, bf16[256,3072]{1,0:T(8,128)(2,1)}, bf16[192,2048]{1,0:T(8,128)(2,1)}, bf16[384,2...) custom-call(f32[192,6448]{1,0:T(8,128)} %refs_1_.1, ...), custom_call_target="tpu_custom_call" | custom-call | flops 10000000000 | bytes 100000000 | tf_op jit(solution)/shard_map/pallas_call | solution.py:844
  211.6 0.0 copy-start.10
  211.6 0.0 copy-start.11
  211.6 0.0 copy-start.12
  211.6 184.9 %shard_map.396 = (f32[192,6656]{1,0:T(8,128)}, f32[384,1536]{1,0:T(8,128)}, f32[8,3456]{1,0:T(8,128)}, f32[256,1536]{1,0:T(8,128)}, f32[256,1536]{1,0:T(8,128)}, /*index=5*/bf16[26,2,4,256,256]{4,3,2,1,0:T(8,128)(2,1)}) custom-call(bf16[192,2048]{1,0:T(8,128)(2,1)} %get-tuple-element.50.normed_turned_ref, ...), custom_call_target="tpu_custom_call" | custom-call | flops 20000000000 | bytes 200000000 | tf_op jit(solution)/shard_map/pallas_call | solution.py:1610
  396.6 0.9 slice_reduce_fusion
  397.5 0.1 reshape.94
  397.6 0.1 reduce_sum.11
  397.7 0.7 slice.17
  398.4 0.0 copy-done.10
  398.4 0.0 copy-done.11
  398.4 0.0 copy-done.12
  398.4 0.6 multiply_subtract_fusion.2
  399.0 0.0 copy-start.2
  399.0 0.0 copy-start.3
  399.0 0.0 copy-start.4
  399.0 0.0 copy-start.5
  399.0 0.0 copy-start.8
  399.0 0.0 copy-start.9
  399.0 0.0 copy-start.13
  399.0 0.0 copy-start.14
  399.1 0.0 copy-start.15
  399.1 0.0 copy-start.1
  399.1 19.7 %shard_map.397 = (f32[192,6448]{1,0:T(8,128)}, f32[192,6448]{1,0:T(8,128)}, f32[192,6448]{1,0:T(8,128)}, f32[192,6448]{1,0:T(8,128)}, f32[384,1536]{1,0:T(8,128)...) custom-call(f32[192,6656]{1,0:T(8,128)} %get-tuple-element.64.refs_0_, f32[192,6448]{1,0:T(8,128)} %refs_1_.1, ...), custom_call_target="tpu_custom_call" | custom-call | tf_op jit(solution)/shard_map/pallas_call | solution.py:1689
  418.8 0.0 copy-start
  418.8 0.0 copy-done.2
  418.9 0.0 copy-done.3
  418.9 0.0 copy-done.4
  418.9 1.5 multiply_subtract_fusion
  420.4 1.0 fusion.8
  421.5 0.0 copy-done.5
  421.5 0.0 copy-done.8
  421.5 0.0 copy-done.9
  421.5 0.0 copy-start.6
  421.5 0.6 multiply_subtract_fusion.1
  422.1 0.1 constant_dynamic-slice_fusion.1
  422.2 0.0 copy-start.7
  422.2 0.0 copy-done.13
  422.2 0.0 copy-done.14
  422.2 0.0 copy-done.15
  422.2 0.6 multiply_subtract_fusion.3
  422.8 0.0 copy-done.1
  422.8 1.1 copy.48
  423.9 0.0 copy-done
  423.9 1.1 copy.49
  425.1 0.0 copy-done.6
  425.1 0.0 copy-done.7
  (1 shorter events, 0.0 us)
Async XLA Ops:
  211.6 186.8 %copy-start.10 = (f32[3,48]{1,0:T(4,128)S(1)}, f32[3,48]{1,0:T(4,128)}, u32[]{:S(2)}) copy-start(f32[3,48]{1,0:T(4,128)} %headcoefs_ref.1) | copy-start | bytes 1732
  211.6 186.8 %copy-start.11 = (f32[3,48]{1,0:T(4,128)S(1)}, f32[3,48]{1,0:T(4,128)}, u32[]{:S(2)}) copy-start(f32[3,48]{1,0:T(4,128)} %param.31) | copy-start | bytes 1732
  211.6 186.8 %copy-start.12 = (f32[3,48]{1,0:T(4,128)S(1)}, f32[3,48]{1,0:T(4,128)}, u32[]{:S(2)}) copy-start(f32[3,48]{1,0:T(4,128)} %param.37) | copy-start | bytes 1732
  399.0 19.9 %copy-start.2 = (f32[5,416]{1,0:T(8,128)S(1)}, f32[5,416]{1,0:T(8,128)}, u32[]{:S(2)}) copy-start(f32[5,416]{1,0:T(8,128)} %convtaps_ref.1) | copy-start | bytes 24964
  399.0 19.9 %copy-start.3 = (f32[5,416]{1,0:T(8,128)S(1)}, f32[5,416]{1,0:T(8,128)}, u32[]{:S(2)}) copy-start(f32[5,416]{1,0:T(8,128)} %param.30) | copy-start | bytes 24964
  399.0 19.9 %copy-start.4 = (f32[5,416]{1,0:T(8,128)S(1)}, f32[5,416]{1,0:T(8,128)}, u32[]{:S(2)}) copy-start(f32[5,416]{1,0:T(8,128)} %param.36) | copy-start | bytes 24964
  399.0 22.5 %copy-start.5 = (f32[384]{0:T(512)S(1)}, f32[384]{0:T(512)}, u32[]{:S(2)}) copy-start(f32[384]{0:T(512)} %param.26) | copy-start | bytes 4612
  399.0 22.5 %copy-start.8 = (f32[384]{0:T(512)S(1)}, f32[384]{0:T(512)}, u32[]{:S(2)}) copy-start(f32[384]{0:T(512)} %param.32) | copy-start | bytes 4612
  399.0 22.5 %copy-start.9 = (f32[384]{0:T(512)S(1)}, f32[384]{0:T(512)}, u32[]{:S(2)}) copy-start(f32[384]{0:T(512)} %param.38) | copy-start | bytes 4612
  399.0 23.1 %copy-start.13 = (f32[192]{0:T(256)S(1)}, f32[192]{0:T(256)}, u32[]{:S(2)}) copy-start(f32[192]{0:T(256)} %param.22) | copy-start | bytes 2308
  399.0 23.1 %copy-start.14 = (f32[192]{0:T(256)S(1)}, f32[192]{0:T(256)}, u32[]{:S(2)}) copy-start(f32[192]{0:T(256)} %param.28) | copy-start | bytes 2308
  399.1 23.1 %copy-start.15 = (f32[192]{0:T(256)S(1)}, f32[192]{0:T(256)}, u32[]{:S(2)}) copy-start(f32[192]{0:T(256)} %param.34) | copy-start | bytes 2308
  399.1 23.7 %copy-start.1 = (f32[256,1536]{1,0:T(8,128)S(1)}, f32[256,1536]{1,0:T(8,128)}, u32[]{:S(2)}) copy-start(f32[256,1536]{1,0:T(8,128)} %get-tuple-element.61) | copy-start | bytes 4718596
  418.8 5.1 %copy-start = (f32[256,1536]{1,0:T(8,128)S(1)}, f32[256,1536]{1,0:T(8,128)}, u32[]{:S(2)}) copy-start(f32[256,1536]{1,0:T(8,128)} %get-tuple-element.62) | copy-start | bytes 4718596
  421.5 3.6 copy-start.6
  422.2 2.9 copy-start.7
